TPU v7x, 32 devices: a whole 2x2x4 slice. The times are simulated.
32 devices in a mesh: dp: 8 (over y, x, core), tensor: 4 (over z).
Axes of the slice: x: 2, y: 2, z: 4, core: 2. Of those that a mesh axis runs over, the one named last changes fastest.
Arguments:
- normed: bfloat16 [1024, 5376], P(('dp', 'tensor')), may hold values from -6 to 6
- grad_kv: bfloat16 [1024, 2048], P('dp', 'tensor'), may hold values from -6 to 6
- weight: bfloat16 [5376, 2048], P(None, 'tensor'), may hold values from -0.125 to 0.125
Outputs:
- grad_input: bfloat16 [1024, 5376], P(('dp', 'tensor'))
- grad_weight: float32 [5376, 2048], P('dp', 'tensor')
All inputs are finite; a program needn't handle non-finite values.
Results may differ from a plain program's by a relative error of at most 0.009.
Values may be sent and summed in bfloat16 or wider, within the bound.
No kernel may reach another device: no remote copies, remote signals or barrier semaphores. Data moves between devices by JAX's collectives and lax.ppermute only.
A program may use at most 64 MiB of HBM per device.

v0:
```python
import jax
import jax.numpy as jnp
from jax import lax
from jax.sharding import PartitionSpec as P


def body(normed, grad_kv, weight):
    summed = lax.psum_scatter(
        lax.dot_general(
            grad_kv, weight, (((1,), (1,)), ((), ())), preferred_element_type=jnp.float32
        ).astype(jnp.bfloat16),
        "tensor",
        scatter_dimension=0,
        tiled=True,
    )
    gathered = lax.all_gather(normed, "tensor", axis=0, tiled=True)
    grad_weight = lax.psum_scatter(
        lax.dot_general(
            gathered, grad_kv, (((0,), (0,)), ((), ())), preferred_element_type=jnp.float32
        ),
        "dp",
        scatter_dimension=0,
        tiled=True,
    )
    return (summed, grad_weight)


def solution(mesh):
    in_specs = (P(("dp", "tensor"), None), P("dp", "tensor"), P(None, "tensor"))
    out_specs = (P(("dp", "tensor"), None), P("dp", "tensor"))
    return jax.shard_map(body, mesh=mesh, in_specs=in_specs, out_specs=out_specs, check_vma=False)
```

profile of v0, /device:TPU:0, one launch (start us, length us, event | category | flops | bytes accessed | tf_op | source)
XLA Modules:
  0.0 174.2 jit_solution(18265246781900420572)
XLA Ops:
  7.2 0.0 copy-start
  7.2 0.0 all-gather.2.cloned.1.call-start
  7.2 0.7 all-gather.2.cloned.1.call-update
  7.9 0.0 reduce-scatter.3.cloned.1.call-start
  8.0 0.1 copy-done
  8.1 5.6 %convolution_convert_fusion = bf16[128,5376]{1,0:T(8,128)(2,1)} fusion(bf16[128,512]{1,0:T(8,128)(2,1)S(1)} %copy-done, bf16[5376,512]{1,0:T(8,128)(2,1)} %param.5), kind=kOutput, calls=%fused_computation | convolution fusion | flops 705331200 | bytes 7012352 | tf_op jit(solution)/shard_map/dot_general | solution.py:9
  13.7 0.0 reduce-scatter.3.cloned.1.call-update
  13.7 0.0 reduce-scatter.5.cloned.1.call-start
  13.7 32.4 %all-gather.2.cloned.1.call-done = bf16[128,5376]{1,0:T(8,128)(2,1)} async-done(((bf16[32,5376]{1,0:T(8,128)(2,1)}), bf16[128,5376]{1,0:T(8,128)(2,1)}) %all-gather.2.cloned.1.call-update) | async-done | bytes 1376272 | tf_op jit(solution)/shard_map/all_gather | solution.py:16
  46.1 7.1 %fusion = f32[5376,512]{1,0:T(8,128)} fusion(bf16[128,5376]{1,0:T(8,128)(2,1)} %all-gather.2.cloned.1.call-done, bf16[128,512]{1,0:T(8,128)(2,1)S(1)} %copy-done), kind=kOutput, calls=%fused_computation.1 | convolution fusion | flops 704643072 | bytes 12517376 | tf_op jit(solution)/shard_map/dot_general | solution.py:18
  53.3 0.0 reduce-scatter.5.cloned.1.call-update
  53.3 26.9 %reduce-scatter.3.cloned.1.call-done = bf16[32,5376]{1,0:T(8,128)(2,1)} async-done(((bf16[128,5376]{1,0:T(8,128)(2,1)}), bf16[32,5376]{1,0:T(8,128)(2,1)}) %reduce-scatter.3.cloned.1.call-update) | async-done | bytes 344080 | tf_op jit(solution)/shard_map/reduce_scatter | solution.py:8
  80.2 87.5 %reduce-scatter.5.cloned.1.call-done = f32[672,512]{1,0:T(8,128)} async-done(((f32[5376,512]{1,0:T(8,128)}), f32[672,512]{1,0:T(8,128)}) %reduce-scatter.5.cloned.1.call-update) | async-done | bytes 1376272 | tf_op jit(solution)/shard_map/reduce_scatter | solution.py:17
Async XLA Ops:
  7.2 0.9 copy-start
  7.2 39.0 %all-gather.2.cloned.1.call-start = ((), (), s32[]{:S(2)}) async-start(), calls=%async_computation.3 | async-start | bytes 1720320 | tf_op jit(solution)/shard_map/all_gather | solution.py:16
  7.9 72.3 %reduce-scatter.3.cloned.1.call-start = ((), (), s32[]{:S(2)}) async-start(), calls=%async_computation.2 | async-start | bytes 1720320 | tf_op jit(solution)/shard_map/reduce_scatter | solution.py:8
  13.7 154.0 %reduce-scatter.5.cloned.1.call-start = ((), (), s32[]{:S(2)}) async-start(), calls=%async_computation.4 | async-start | bytes 12386304 | tf_op jit(solution)/shard_map/reduce_scatter | solution.py:17
Sparse Core Ops, SparseCore 0:
  9.6 36.5 all-gather.1
  49.0 31.1 reduce-scatter.2
  84.8 82.8 reduce-scatter.4
where the time goes:
time: 174 us
  waiting for transfers between devices  148 us (85%)
  between operations  13.7 us (8%)
  matrix products  12.7 us (7%)
    reduce_scatter x1, waiting for transfers between devices, body(): lax.psum_scatter(lax.dot_general(gathered, grad_kv, (((0,), (0,)), ((), (...  87.5 us
    all_gather x1, waiting for transfers between devices, body(): gathered = lax.all_gather(normed, 'tensor', axis=0, tiled=True)  32.4 us
    reduce_scatter x1, waiting for transfers between devices, body(): lax.psum_scatter(lax.dot_general(grad_kv, weight, (((1,), (1,)), ((), ())...  26.9 us
    dot_general x1, matrix products, body(): lax.dot_general(gathered, grad_kv, (((0,), (0,)), ((), ())), preferred_el...  7.13 us
    dot_general x1, matrix products, body(): lax.dot_general(grad_kv, weight, (((1,), (1,)), ((), ())), preferred_elem...  5.6 us
  transfers between devices with their start and end apart: 3, of which 3 were waited for; matrix products, arithmetic and copies ran while one was open for 7% of the time, Pallas kernels for 0%

commit v1 on v0

v1 whole, which is shorter than its diff:
```python
import functools
import math

import jax
import jax.numpy as jnp
from jax import lax
from jax.experimental import pallas as pl
from jax.experimental.pallas import tpu as pltpu
from jax.sharding import PartitionSpec as P

BF16 = jnp.bfloat16
F32 = jnp.float32
LANES = 128
VMEM = pl.BlockSpec(memory_space=pltpu.VMEM)
PARAMS = pltpu.CompilerParams(vmem_limit_bytes=48 * 1024 * 1024)


class Plan:
    def __init__(self, mesh, normed, grad_kv):
        self.n_dp, self.n_t = mesh.shape["dp"], mesh.shape["tensor"]
        self.chips = self.n_dp // 2
        self.rows, self.feats = normed.shape
        self.kv = grad_kv.shape[1]
        self.width = self.feats // self.n_dp
        self.tokens = self.rows * self.n_dp
        self.tiles = self.feats // LANES
        starts = [self.width * d // LANES * LANES for d in range(self.n_dp)]
        ends = [self.width * d - s + self.width for d, s in enumerate(starts)]
        self.window = -(-max(ends) // LANES) * LANES
        self.step = math.gcd(self.width, LANES)
        self.power = self.chips & (self.chips - 1) == 0

    def chip_to(self, chip, q):
        return chip ^ q if self.power else lax.rem(chip + q, self.chips) if not isinstance(chip, int) else (chip + q) % self.chips

    def chip_from(self, chip, q):
        return chip ^ q if self.power else lax.rem(chip + self.chips - q, self.chips)

    def start_of(self, d):
        exact = d * self.width
        return jnp.minimum(exact // LANES * LANES, self.feats - self.window)

    def swap_cores(self, x):
        return lax.ppermute(x, "dp", [(d, d ^ 1) for d in range(self.n_dp)])

    def to_chip(self, x, q):
        return lax.ppermute(x, "dp", [(d, 2 * self.chip_to(d // 2, q) + d % 2) for d in range(self.n_dp)])

    def along(self, x):
        pairs = []
        for d in range(self.n_dp):
            for t in range(self.n_t):
                to = t - 1 if d % 2 else t + 1
                pairs.append((d * self.n_t + t, d * self.n_t + to if 0 <= to < self.n_t else (d ^ 1) * self.n_t + t))
        return lax.ppermute(x, ("dp", "tensor"), pairs)


def split_kernel(plan, normed_ref, keep_ref, send_ref):
    d = lax.axis_index("dp")
    chip, core = d // 2, d % 2
    for q in range(plan.chips):
        to = plan.chip_to(chip, q)
        for ref, c in ((keep_ref, core), (send_ref, 1 - core)):
            start = pl.multiple_of(plan.start_of(2 * to + c), LANES)
            ref[q] = normed_ref[:, pl.ds(start, plan.window)]


def turn_kernel(plan, *refs):
    *pieces, out_ref, scratch = refs
    d = lax.axis_index("dp")
    offset = pl.multiple_of(d * plan.width - plan.start_of(d), plan.step)
    per_tile = LANES // pieces[0].shape[0]
    for j in range(plan.tokens // LANES):
        tile = jnp.concatenate([ref[...] for ref in pieces[j * per_tile : (j + 1) * per_tile]], axis=0)
        scratch[...] = tile.T
        out_ref[j] = scratch[pl.ds(offset, plan.width), :]


def partial_kernel(plan, own_ref, other_ref, weight_ref, out_ref):
    both = jnp.concatenate([own_ref[...], other_ref[...]], axis=0)
    product = lax.dot_general(both, weight_ref[...], (((1,), (1,)), ((), ())), preferred_element_type=F32).astype(BF16)
    for r in range(out_ref.shape[0]):
        for j in range(out_ref.shape[1]):
            out_ref[r, j] = product[r * plan.rows : (r + 1) * plan.rows, j * LANES : (j + 1) * LANES]


def weight_kernel(plan, *refs):
    n = plan.n_t
    kv_ref, own_ref, *blocks, out_ref = refs
    mine, theirs = blocks[: n - 1], blocks[n - 1 :]
    d, t = lax.axis_index("dp"), lax.axis_index("tensor")
    chip, core = d // 2, d % 2
    place = jnp.where(core == 0, t, n - 1 - t)
    for k in range(n):
        source = jnp.where(core == 0, lax.rem(t + n - k, n), lax.rem(t + k, n))
        rows = []
        for q in range(plan.chips):
            at = 2 * plan.chip_from(chip, q)
            rows += [kv_ref[at + core, source], kv_ref[at + 1 - core, source]]
        rows = jnp.concatenate(rows, axis=0)
        if k:
            block = jnp.where(place >= k, mine[k - 1][...], theirs[n - k - 1][...])
        else:
            block = own_ref[...]
        block = block.reshape(plan.tokens // LANES, plan.width, LANES)
        block = jnp.concatenate([block[j] for j in range(plan.tokens // LANES)], axis=1)
        term = jnp.dot(block, rows, preferred_element_type=F32)
        if k:
            out_ref[...] += term
        else:
            out_ref[...] = term


def input_kernel(plan, partial_ref, mine_ref, theirs_ref, out_ref):
    n = plan.n_t
    core, t = lax.axis_index("dp") % 2, lax.axis_index("tensor")
    place = jnp.where(core == 0, t, n - 1 - t)
    for j in range(plan.tiles):
        total = partial_ref[t, j].astype(F32)
        total += jnp.where(place >= 1, mine_ref[j].astype(F32), 0.0)
        total += jnp.where(place < n - 1, theirs_ref[j].astype(F32), 0.0)
        out_ref[:, j * LANES : (j + 1) * LANES] = total.astype(BF16)


def body(mesh, normed, grad_kv, weight):
    plan = Plan(mesh, normed, grad_kv)
    n = plan.n_t
    flat = (plan.tiles, plan.rows, LANES)
    d, t = lax.axis_index("dp"), lax.axis_index("tensor")
    core = d % 2
    place = jnp.where(core == 0, t, n - 1 - t)

    all_kv = lax.all_gather(grad_kv, "dp", axis=0, tiled=False)
    other_kv = plan.swap_cores(grad_kv)

    pieces = jax.ShapeDtypeStruct((plan.chips, plan.rows, plan.window), BF16)
    keep, send = pl.pallas_call(
        functools.partial(split_kernel, plan), out_shape=(pieces, pieces), in_specs=[VMEM], out_specs=(VMEM, VMEM),
        compiler_params=PARAMS, name="split",
    )(normed)
    got = plan.swap_cores(send)
    pairs = [jnp.concatenate([keep[q], got[q]], axis=0) for q in range(plan.chips)]
    pairs = [plan.to_chip(pairs[q], q) if q else pairs[q] for q in range(plan.chips)]

    targets = 2 * n
    group = 6
    part = pl.pallas_call(
        functools.partial(partial_kernel, plan),
        out_shape=jax.ShapeDtypeStruct((targets,) + flat, BF16),
        grid=(plan.tiles // group,),
        in_specs=[
            pl.BlockSpec(grad_kv.shape, lambda i: (0, 0)),
            pl.BlockSpec(grad_kv.shape, lambda i: (0, 0)),
            pl.BlockSpec((group * LANES, plan.kv), lambda i: (i, 0)),
        ],
        out_specs=pl.BlockSpec((targets, group, plan.rows, LANES), lambda i: (0, i, 0, 0)),
        compiler_params=PARAMS, name="partials",
        cost_estimate=pl.CostEstimate(flops=4 * grad_kv.size * plan.feats, bytes_accessed=weight.size * 2 + targets * normed.size * 2, transcendentals=0),
    )(grad_kv, other_kv, weight)
    part_own, part_other = part[:n], part[n:]

    own = pl.pallas_call(
        functools.partial(turn_kernel, plan),
        out_shape=jax.ShapeDtypeStruct((plan.tokens // LANES, plan.width, LANES), BF16),
        in_specs=[VMEM] * plan.chips, out_specs=VMEM,
        scratch_shapes=[pltpu.VMEM((plan.window, LANES), BF16)],
        compiler_params=PARAMS, name="turn",
    )(*pairs).reshape(flat)
    other = plan.swap_cores(own)

    def passed(received, partial, slot):
        target = jnp.clip(jnp.where(core == 0, t + n - slot + 1, t - (n - slot + 1)), 0, n - 1)
        mine = lax.dynamic_index_in_dim(partial, target, 0, keepdims=False).astype(F32)
        arrived = jnp.where(place >= 1, received.astype(F32), 0.0)
        return (arrived + jnp.where(place < slot - 1, mine, 0.0)).astype(BF16)

    mine, theirs = [], []
    first, second = plan.along(own), plan.along(other)
    for slot in range(2, n + 1):
        mine.append(first)
        theirs.append(plan.swap_cores(second))
        first, second = plan.along(passed(first, part_other, slot)), plan.along(passed(second, part_own, slot))
    rest = plan.swap_cores(first)

    grad_weight = pl.pallas_call(
        functools.partial(weight_kernel, plan),
        out_shape=jax.ShapeDtypeStruct((plan.width, plan.kv), F32),
        in_specs=[VMEM] * (2 * n), out_specs=VMEM,
        compiler_params=PARAMS, name="weights",
        cost_estimate=pl.CostEstimate(flops=2 * n * normed.size * plan.kv, bytes_accessed=4 * plan.width * plan.kv, transcendentals=0),
    )(all_kv.reshape(plan.n_dp, n, plan.rows, plan.kv), own, *mine, *theirs)

    grad_input = pl.pallas_call(
        functools.partial(input_kernel, plan),
        out_shape=jax.ShapeDtypeStruct(normed.shape, BF16),
        in_specs=[VMEM] * 3, out_specs=VMEM,
        compiler_params=PARAMS, name="inputs",
    )(part_own, second, rest)
    return grad_input, grad_weight


def solution(mesh):
    in_specs = (P(("dp", "tensor"), None), P("dp", "tensor"), P(None, "tensor"))
    out_specs = (P(("dp", "tensor"), None), P("dp", "tensor"))
    return jax.shard_map(functools.partial(body, mesh), mesh=mesh, in_specs=in_specs, out_specs=out_specs, check_vma=False)
```

time: 174 us -> 73.9 us (0.42)
  waiting for transfers between devices: 148 us -> 15.2 us
  starting transfers between devices: 0.12 us -> 23.4 us
  matrix products: 12.7 us -> 0 us
  Pallas kernels: 0 us -> 10.4 us
  other arithmetic: 0 us -> 6.49 us
  local copies, waits for them, and re-layouts: 0.12 us -> 3.84 us
    reduce_scatter x2 -> x0, waiting for transfers between devices: 114 us -> none  [the longest x1 87.5 us: body(): lax.psum_scatter(lax.dot_general(gathered, grad_kv, (((0,), (0,)), ((), (...]
    all_gather x1, waiting for transfers between devices: 32.4 us -> 0.01 us  [body(): all_kv = lax.all_gather(grad_kv, 'dp', axis=0, tiled=False)]
    ppermute x0 -> x18, starting transfers between devices: none -> 23.4 us  [the longest x8 17.3 us: along(): return lax.ppermute(x, ('dp', 'tensor'), pairs)]
    ppermute x0 -> x18, waiting for transfers between devices: none -> 15.1 us  [the longest x8 8.27 us: along(): return lax.ppermute(x, ('dp', 'tensor'), pairs)]
    dot_general x2 -> x0, matrix products: 12.7 us -> none  [the longest x1 7.13 us: body(): lax.dot_general(gathered, grad_kv, (((0,), (0,)), ((), ())), preferred_el...]
    pallas_call x0 -> x5, Pallas kernels: none -> 10.4 us  [the longest x1 6.29 us: body(): pl.pallas_call(functools.partial(partial_kernel, plan), out_shape=jax.Sha...]
    convert_element_type x0 -> x6, other arithmetic: none -> 6.45 us  [passed(): return (arrived + jnp.where(place < slot - 1, mine, 0.0)).astype(BF16)]
    unnamed x2 -> x8, local copies, waits for them, and re-layouts: 0.12 us -> 2.2 us
  transfers between devices with their start and end apart: 3 -> 19, of which waited for: 3 -> 10; matrix products, arithmetic and copies ran while one was open for 7% -> 11% of each run, Pallas kernels for 0% -> 10%
where the time goes in v1:
time: 73.9 us; the launch traced here: 73.4 us
  starting transfers between devices  23.4 us (32%)
  waiting for transfers between devices  15.2 us (21%)
  between operations  14.2 us (19%)
  Pallas kernels  10.4 us (14%)
  other arithmetic  6.49 us (9%)
  local copies, waits for them, and re-layouts  3.84 us (5%)
    ppermute x8, starting transfers between devices, along(): return lax.ppermute(x, ('dp', 'tensor'), pairs)  17.3 us
    ppermute x8, waiting for transfers between devices, along(): return lax.ppermute(x, ('dp', 'tensor'), pairs)  8.27 us
    convert_element_type x6, other arithmetic, passed(): return (arrived + jnp.where(place < slot - 1, mine, 0.0)).astype(BF16)  6.45 us
    pallas_call x1, Pallas kernels, body(): pl.pallas_call(functools.partial(partial_kernel, plan), out_shape=jax.Sha...  6.29 us
    ppermute x3, waiting for transfers between devices, to_chip(): lax.ppermute(x, 'dp', [(d, 2 * self.chip_to(d // 2, q) + d % 2) for d in...  5.48 us
    ppermute x3, starting transfers between devices, to_chip(): lax.ppermute(x, 'dp', [(d, 2 * self.chip_to(d // 2, q) + d % 2) for d in...  4.35 us
    pallas_call x1, Pallas kernels, body(): pl.pallas_call(functools.partial(weight_kernel, plan), out_shape=jax.Shap...  2.93 us
    unnamed x8, local copies, waits for them, and re-layouts  2.2 us
  transfers between devices with their start and end apart: 19, of which 10 were waited for; matrix products, arithmetic and copies ran while one was open for 11% of the time, Pallas kernels for 10%

profile of v1, /device:TPU:0, one launch (start us, length us, event | category | flops | bytes accessed | tf_op | source)
XLA Modules:
  0.0 73.4 jit_solution(11974032020120030530)
XLA Ops:
  7.2 0.0 all-gather.3.cloned.1.call-start
  7.2 0.5 collective-permute-start
  7.7 1.0 %copy-done.2 = bf16[32,5376]{1,0:T(8,128)(2,1)S(1)} copy-done((bf16[32,5376]{1,0:T(8,128)(2,1)S(1)}, bf16[32,5376]{1,0:T(8,128)(2,1)}, u32[]{:S(2)}) %copy-start.2) | copy-done | bytes 344088
  8.8 0.1 collective-permute-start.1
  8.9 1.4 %collective-permute-done.1 = bf16[4,32,768]{2,1,0:T(8,128)(2,1)S(1)} collective-permute-done((bf16[4,32,768]{2,1,0:T(8,128)(2,1)S(1)}, bf16[4,32,768]{2,1,0:T(8,128)(2,1)S(1)}, u32[]{:S(2)}, u32[]{:S(2)}) %collective-permute-start.1) | collective-permute-done | bytes 196640 | tf_op jit(solution)/shard_map/ppermute | solution.py:44
  10.3 2.7 %collective-permute-start.2 = (bf16[64,768]{1,0:T(8,128)(2,1)S(1)}, bf16[64,768]{1,0:T(8,128)(2,1)S(1)}, u32[]{:S(2)}, u32[]{:S(2)}) collective-permute-start(bf16[64,768]{1,0:T(8,128)(2,1)S(1)} %pad_maximum_fusion.1), channel_id=1, source_target_pairs={{0,8},{4,12},{8,0},{12,4},{16,24},{20,28},{24,16},{28,20},{1,9},{5... | collective-permute-start | bytes 294920 | tf_op jit(solution)/shard_map/ppermute | solution.py:47
  13.0 1.6 %collective-permute-start.3 = (bf16[64,768]{1,0:T(8,128)(2,1)S(1)}, bf16[64,768]{1,0:T(8,128)(2,1)S(1)}, u32[]{:S(2)}, u32[]{:S(2)}) collective-permute-start(bf16[64,768]{1,0:T(8,128)(2,1)S(1)} %pad_maximum_fusion.2), channel_id=1, source_target_pairs={{0,16},{4,20},{8,24},{12,28},{16,0},{20,4},{24,8},{28,12},{1,17},{... | collective-permute-start | bytes 294920 | tf_op jit(solution)/shard_map/ppermute | solution.py:47
  14.6 0.1 collective-permute-start.4
  14.7 1.6 %collective-permute-done.2.refs_1_ = bf16[64,768]{1,0:T(8,128)(2,1)S(1)} collective-permute-done((bf16[64,768]{1,0:T(8,128)(2,1)S(1)}, bf16[64,768]{1,0:T(8,128)(2,1)S(1)}, u32[]{:S(2)}, u32[]{:S(2)}) %collective-permute-start.2) | collective-permute-done | bytes 98336 | tf_op jit(solution)/shard_map/ppermute | solution.py:47
  16.3 2.7 %collective-permute-done.3.refs_2_ = bf16[64,768]{1,0:T(8,128)(2,1)S(1)} collective-permute-done((bf16[64,768]{1,0:T(8,128)(2,1)S(1)}, bf16[64,768]{1,0:T(8,128)(2,1)S(1)}, u32[]{:S(2)}, u32[]{:S(2)}) %collective-permute-start.3) | collective-permute-done | bytes 98336 | tf_op jit(solution)/shard_map/ppermute | solution.py:47
  19.0 1.2 %collective-permute-done.4.refs_3_ = bf16[64,768]{1,0:T(8,128)(2,1)S(1)} collective-permute-done((bf16[64,768]{1,0:T(8,128)(2,1)S(1)}, bf16[64,768]{1,0:T(8,128)(2,1)S(1)}, u32[]{:S(2)}, u32[]{:S(2)}) %collective-permute-start.4) | collective-permute-done | bytes 98336 | tf_op jit(solution)/shard_map/ppermute | solution.py:47
  20.2 0.2 turn.1
  20.4 0.1 collective-permute-start.5
  20.4 1.6 %collective-permute-start.10 = (bf16[42,32,128]{2,1,0:T(8,128)(2,1)S(1)}, bf16[42,32,128]{2,1,0:T(8,128)(2,1)S(1)}, u32[]{:S(2)}, u32[]{:S(2)}) collective-permute-start(bf16[42,32,128]{2,1,0:T(8,128)(2,1)S(1)} %bitcast.43), channel_id=1, source_target_pairs={{0,1},{1,2},{2,3},{3,7},{4,0},{5,4},{6,5},{7,6},{8,9},{9,10},{10,1... | collective-permute-start | bytes 1032200 | tf_op jit(solution)/shard_map/ppermute | solution.py:55
  22.0 0.0 collective-permute-done.other_ref
  22.0 6.3 %partials.1 = bf16[8,42,32,128]{3,2,1,0:T(8,128)(2,1)S(1)} custom-call(bf16[128,512]{1,0:T(8,128)(2,1)S(1)} %copy-done.1, bf16[128,512]{1,0:T(8,128)(2,1)S(1)} %collective-permute-done.other_ref, bf16[5376,512]{1,0:T(8,128)(2,1)} %weight_ref.1), custom_call_target="tpu_custom_call" | custom-call | flops 1409286144 | bytes 8257536 | tf_op jit(solution)/shard_map/partials/pallas_call | solution.py:147
  28.3 1.6 %fusion.6 = (bf16[4,42,32,128]{3,2,1,0:T(8,128)(2,1)}, bf16[4,42,32,128]{3,2,1,0:T(8,128)(2,1)S(1)}) fusion(bf16[8,42,32,128]{3,2,1,0:T(8,128)(2,1)S(1)} %partials.1), kind=kLoop, calls=%fused_computation.24 | loop fusion | bytes 5505024 | tf_op jit(solution)/shard_map/slice | solution.py:160
  29.9 0.0 collective-permute-done.5
  30.0 1.6 %collective-permute-start.6 = (bf16[42,32,128]{2,1,0:T(8,128)(2,1)S(1)}, bf16[42,32,128]{2,1,0:T(8,128)(2,1)}, u32[]{:S(2)}, u32[]{:S(2)}) collective-permute-start(bf16[42,32,128]{2,1,0:T(8,128)(2,1)S(1)} %collective-permute-done.5), channel_id=1, source_target_pairs={{0,1},{1,2},{2,3},{3,7},{4,0},{5,4},{6,5},{7,6},{8,9},{9,10},{10,1... | collective-permute-start | bytes 1032200 | tf_op jit(solution)/shard_map/ppermute | solution.py:55
  31.5 0.0 collective-permute-done.10.refs_2_
  31.5 1.1 %fusion.2 = bf16[42,32,128]{2,1,0:T(8,128)(2,1)S(1)} fusion(bf16[42,32,128]{2,1,0:T(8,128)(2,1)S(1)} %collective-permute-done.10.refs_2_, bf16[4,42,32,128]{3,2,1,0:T(8,128)(2,1)} %get-tuple-element.6, s32[]{:T(128)S(6)} %min.13, pred[]{:T(512)S(6)} %lt.26, pred[]{:T(512)S(6)} %ge.2), kind=kLoop, calls=%fused_computation.5 | loop fusion | flops 1032192 | bytes 1032198 | tf_op jit(solution)/shard_map/convert_element_type | solution.py:175
  32.6 1.6 %collective-permute-start.11 = (bf16[42,32,128]{2,1,0:T(8,128)(2,1)S(1)}, bf16[42,32,128]{2,1,0:T(8,128)(2,1)S(1)}, u32[]{:S(2)}, u32[]{:S(2)}) collective-permute-start(bf16[42,32,128]{2,1,0:T(8,128)(2,1)S(1)} %fusion.2), channel_id=1, source_target_pairs={{0,1},{1,2},{2,3},{3,7},{4,0},{5,4},{6,5},{7,6},{8,9},{9,10},{10,1... | collective-permute-start | bytes 1032200 | tf_op jit(solution)/shard_map/ppermute | solution.py:55
  34.2 0.0 all-gather.3.cloned.1.call-update
  34.3 2.0 %collective-permute-done.6 = bf16[42,32,128]{2,1,0:T(8,128)(2,1)} collective-permute-done((bf16[42,32,128]{2,1,0:T(8,128)(2,1)S(1)}, bf16[42,32,128]{2,1,0:T(8,128)(2,1)}, u32[]{:S(2)}, u32[]{:S(2)}) %collective-permute-start.6) | collective-permute-done | bytes 344096 | tf_op jit(solution)/shard_map/ppermute | solution.py:55
  36.3 1.1 %fusion.5 = bf16[42,32,128]{2,1,0:T(8,128)(2,1)S(1)} fusion(bf16[42,32,128]{2,1,0:T(8,128)(2,1)} %collective-permute-done.6, bf16[4,42,32,128]{3,2,1,0:T(8,128)(2,1)S(1)} %get-tuple-element.7.partial_ref, s32[]{:T(128)S(6)} %min.13, pred[]{:T(512)S(6)} %lt.26, pred[]{:T(512)S(6)} %ge.2), kind=kLoop, calls=%fused_computation.11 | loop fusion | flops 1032192 | bytes 1032198 | tf_op jit(solution)/shard_map/convert_element_type | solution.py:175
  37.4 2.6 %collective-permute-start.7 = (bf16[42,32,128]{2,1,0:T(8,128)(2,1)S(1)}, bf16[42,32,128]{2,1,0:T(8,128)(2,1)S(1)}, u32[]{:S(2)}, u32[]{:S(2)}) collective-permute-start(bf16[42,32,128]{2,1,0:T(8,128)(2,1)S(1)} %fusion.5), channel_id=1, source_target_pairs={{0,1},{1,2},{2,3},{3,7},{4,0},{5,4},{6,5},{7,6},{8,9},{9,10},{10,1... | collective-permute-start | bytes 1032200 | tf_op jit(solution)/shard_map/ppermute | solution.py:55
  40.0 0.0 collective-permute-done.11.refs_3_
  40.0 1.8 %fusion.1 = bf16[42,32,128]{2,1,0:T(8,128)(2,1)} fusion(bf16[42,32,128]{2,1,0:T(8,128)(2,1)S(1)} %collective-permute-done.11.refs_3_, bf16[4,42,32,128]{3,2,1,0:T(8,128)(2,1)} %get-tuple-element.6, s32[]{:T(128)S(6)} %min.14, pred[]{:T(512)S(6)} %lt.27, pred[]{:T(512)S(6)} %ge.2), kind=kLoop, calls=%fused_computation.3 | loop fusion | flops 1032192 | bytes 1032198 | tf_op jit(solution)/shard_map/convert_element_type | solution.py:175
  41.9 2.4 %collective-permute-start.12 = (bf16[42,32,128]{2,1,0:T(8,128)(2,1)}, bf16[42,32,128]{2,1,0:T(8,128)(2,1)S(1)}, u32[]{:S(2)}, u32[]{:S(2)}) collective-permute-start(bf16[42,32,128]{2,1,0:T(8,128)(2,1)} %fusion.1), channel_id=1, source_target_pairs={{0,1},{1,2},{2,3},{3,7},{4,0},{5,4},{6,5},{7,6},{8,9},{9,10},{10,1... | collective-permute-start | bytes 1032200 | tf_op jit(solution)/shard_map/ppermute | solution.py:55
  44.3 0.5 collective-permute-done.7
  44.8 0.1 fusion.4
  44.9 2.5 %collective-permute-start.8 = (bf16[42,32,128]{2,1,0:T(8,128)(2,1)S(1)}, bf16[42,32,128]{2,1,0:T(8,128)(2,1)}, u32[]{:S(2)}, u32[]{:S(2)}) collective-permute-start(bf16[42,32,128]{2,1,0:T(8,128)(2,1)S(1)} %fusion.4), channel_id=1, source_target_pairs={{0,1},{1,2},{2,3},{3,7},{4,0},{5,4},{6,5},{7,6},{8,9},{9,10},{10,1... | collective-permute-start | bytes 1032200 | tf_op jit(solution)/shard_map/ppermute | solution.py:55
  47.4 2.0 %collective-permute-done.12.refs_4_ = bf16[42,32,128]{2,1,0:T(8,128)(2,1)S(1)} collective-permute-done((bf16[42,32,128]{2,1,0:T(8,128)(2,1)}, bf16[42,32,128]{2,1,0:T(8,128)(2,1)S(1)}, u32[]{:S(2)}, u32[]{:S(2)}) %collective-permute-start.12) | collective-permute-done | bytes 344096 | tf_op jit(solution)/shard_map/ppermute | solution.py:55
  49.4 1.1 %fusion = bf16[42,32,128]{2,1,0:T(8,128)(2,1)S(1)} fusion(bf16[42,32,128]{2,1,0:T(8,128)(2,1)S(1)} %collective-permute-done.12.refs_4_, bf16[4,42,32,128]{3,2,1,0:T(8,128)(2,1)} %get-tuple-element.6, s32[]{:T(128)S(6)} %min.15, pred[]{:T(512)S(6)} %lt.28, pred[]{:T(512)S(6)} %ge.2), kind=kLoop, calls=%fused_computation.1 | loop fusion | flops 1032192 | bytes 1032198 | tf_op jit(solution)/shard_map/convert_element_type | solution.py:175
  50.5 2.4 %collective-permute-start.13 = (bf16[42,32,128]{2,1,0:T(8,128)(2,1)S(1)}, bf16[42,32,128]{2,1,0:T(8,128)(2,1)S(1)}, u32[]{:S(2)}, u32[]{:S(2)}) collective-permute-start(bf16[42,32,128]{2,1,0:T(8,128)(2,1)S(1)} %fusion), channel_id=1, source_target_pairs={{0,1},{1,2},{2,3},{3,7},{4,0},{5,4},{6,5},{7,6},{8,9},{9,10},{10,1... | collective-permute-start | bytes 1032200 | tf_op jit(solution)/shard_map/ppermute | solution.py:55
  52.9 0.1 collective-permute-done.8
  53.0 1.1 %fusion.3 = bf16[42,32,128]{2,1,0:T(8,128)(2,1)S(1)} fusion(bf16[42,32,128]{2,1,0:T(8,128)(2,1)} %collective-permute-done.8, bf16[4,42,32,128]{3,2,1,0:T(8,128)(2,1)S(1)} %get-tuple-element.7.partial_ref, s32[]{:T(128)S(6)} %min.15, pred[]{:T(512)S(6)} %lt.28, pred[]{:T(512)S(6)} %ge.2), kind=kLoop, calls=%fused_computation.7 | loop fusion | flops 1032192 | bytes 1032198 | tf_op jit(solution)/shard_map/convert_element_type | solution.py:175
  54.1 2.6 %collective-permute-start.9 = (bf16[42,32,128]{2,1,0:T(8,128)(2,1)S(1)}, bf16[42,32,128]{2,1,0:T(8,128)(2,1)S(1)}, u32[]{:S(2)}, u32[]{:S(2)}) collective-permute-start(bf16[42,32,128]{2,1,0:T(8,128)(2,1)S(1)} %fusion.3), channel_id=1, source_target_pairs={{0,1},{1,2},{2,3},{3,7},{4,0},{5,4},{6,5},{7,6},{8,9},{9,10},{10,1... | collective-permute-start | bytes 1032200 | tf_op jit(solution)/shard_map/ppermute | solution.py:55
  56.7 1.0 %collective-permute-done.13 = bf16[42,32,128]{2,1,0:T(8,128)(2,1)S(1)} collective-permute-done((bf16[42,32,128]{2,1,0:T(8,128)(2,1)S(1)}, bf16[42,32,128]{2,1,0:T(8,128)(2,1)S(1)}, u32[]{:S(2)}, u32[]{:S(2)}) %collective-permute-start.13) | collective-permute-done | bytes 344096 | tf_op jit(solution)/shard_map/ppermute | solution.py:55
  57.7 0.0 collective-permute-start.14
  57.7 0.5 collective-permute-start.15
  58.2 0.0 collective-permute-start.16
  58.2 0.5 collective-permute-start.17
  58.7 2.8 %collective-permute-done.9.mine_ref = bf16[42,32,128]{2,1,0:T(8,128)(2,1)S(1)} collective-permute-done((bf16[42,32,128]{2,1,0:T(8,128)(2,1)S(1)}, bf16[42,32,128]{2,1,0:T(8,128)(2,1)S(1)}, u32[]{:S(2)}, u32[]{:S(2)}) %collective-permute-start.9) | collective-permute-done | bytes 344096 | tf_op jit(solution)/shard_map/ppermute | solution.py:55
  61.5 0.9 %inputs.1 = bf16[32,5376]{1,0:T(8,128)(2,1)} custom-call(bf16[4,42,32,128]{3,2,1,0:T(8,128)(2,1)S(1)} %get-tuple-element.7.partial_ref, bf16[42,32,128]{2,1,0:T(8,128)(2,1)S(1)} %collective-permute-done.9.mine_ref, bf16[42,32,128]{2,1,0:T(8,128)(2,1)S(1)} %collective-permute-done.14.theirs_ref), custom_call_target="tpu_custom_call" | custom-call | tf_op jit(solution)/shard_map/inputs/pallas_call | solution.py:193
  62.4 0.0 collective-permute-done.17.refs_7_
  62.4 1.2 %copy-done = bf16[1024,512]{1,0:T(8,128)(2,1)S(1)} copy-done((bf16[1024,512]{1,0:T(8,128)(2,1)S(1)}, bf16[1024,512]{1,0:T(8,128)(2,1)}, u32[]{:S(2)}) %copy-start) | copy-done | bytes 1048600
  63.6 2.9 %weights.1 = f32[672,512]{1,0:T(8,128)} custom-call(bf16[8,4,32,512]{3,2,1,0:T(8,128)(2,1)S(1)} %bitcast.45, bf16[42,32,128]{2,1,0:T(8,128)(2,1)S(1)} %bitcast.44, bf16[42,32,128]{2,1,0:T(8,128)(2,1)S(1)} %collective-permute-done.10.refs_2_, bf16[42,32,128]{2,1,0:T(8,128)(2,1)S(1)} %collective-permute-done.11.refs_3_, ...), custom_call_target="tpu_custom_call" | custom-call | flops 704643072 | bytes 1376256 | tf_op jit(solution)/shard_map/weights/pallas_call | solution.py:185
  (17 shorter events, 0.1 us)
Async XLA Ops:
  7.2 14.9 %copy-start.1 = (bf16[128,512]{1,0:T(8,128)(2,1)S(1)}, bf16[128,512]{1,0:T(8,128)(2,1)}, u32[]{:S(2)}) copy-start(bf16[128,512]{1,0:T(8,128)(2,1)} %own_ref.1) | copy-start | bytes 393220
  7.2 55.2 %all-gather.3.cloned.1.call-start = ((), (), s32[]{:S(2)}) async-start(), calls=%async_computation | async-start | bytes 1179648 | tf_op jit(solution)/shard_map/all_gather | solution.py:133
  7.2 14.8 %collective-permute-start = (bf16[128,512]{1,0:T(8,128)(2,1)}, bf16[128,512]{1,0:T(8,128)(2,1)S(1)}, u32[]{:S(2)}, u32[]{:S(2)}) collective-permute-start(bf16[128,512]{1,0:T(8,128)(2,1)} %own_ref.1), channel_id=1, source_target_pairs={{0,4},{4,0},{8,12},{12,8},{16,20},{20,16},{24,28},{28,24},{1,5},{5... | collective-permute-start | bytes 393224 | tf_op jit(solution)/shard_map/ppermute | solution.py:44
  7.7 1.0 %copy-start.2 = (bf16[32,5376]{1,0:T(8,128)(2,1)S(1)}, bf16[32,5376]{1,0:T(8,128)(2,1)}, u32[]{:S(2)}) copy-start(bf16[32,5376]{1,0:T(8,128)(2,1)} %normed_ref.1) | copy-start | bytes 1032196
  8.8 1.5 %collective-permute-start.1 = (bf16[4,32,768]{2,1,0:T(8,128)(2,1)S(1)}, bf16[4,32,768]{2,1,0:T(8,128)(2,1)S(1)}, u32[]{:S(2)}, u32[]{:S(2)}) collective-permute-start(bf16[4,32,768]{2,1,0:T(8,128)(2,1)S(1)} %get-tuple-element.5), channel_id=1, source_target_pairs={{0,4},{4,0},{8,12},{12,8},{16,20},{20,16},{24,28},{28,24},{1,5},{5... | collective-permute-start | bytes 589832 | tf_op jit(solution)/shard_map/ppermute | solution.py:44
  10.3 6.0 %collective-permute-start.2 = (bf16[64,768]{1,0:T(8,128)(2,1)S(1)}, bf16[64,768]{1,0:T(8,128)(2,1)S(1)}, u32[]{:S(2)}, u32[]{:S(2)}) collective-permute-start(bf16[64,768]{1,0:T(8,128)(2,1)S(1)} %pad_maximum_fusion.1), channel_id=1, source_target_pairs={{0,8},{4,12},{8,0},{12,4},{16,24},{20,28},{24,16},{28,20},{1,9},{5... | collective-permute-start | bytes 294920 | tf_op jit(solution)/shard_map/ppermute | solution.py:47
  13.0 6.0 %collective-permute-start.3 = (bf16[64,768]{1,0:T(8,128)(2,1)S(1)}, bf16[64,768]{1,0:T(8,128)(2,1)S(1)}, u32[]{:S(2)}, u32[]{:S(2)}) collective-permute-start(bf16[64,768]{1,0:T(8,128)(2,1)S(1)} %pad_maximum_fusion.2), channel_id=1, source_target_pairs={{0,16},{4,20},{8,24},{12,28},{16,0},{20,4},{24,8},{28,12},{1,17},{... | collective-permute-start | bytes 294920 | tf_op jit(solution)/shard_map/ppermute | solution.py:47
  14.6 5.6 %collective-permute-start.4 = (bf16[64,768]{1,0:T(8,128)(2,1)S(1)}, bf16[64,768]{1,0:T(8,128)(2,1)S(1)}, u32[]{:S(2)}, u32[]{:S(2)}) collective-permute-start(bf16[64,768]{1,0:T(8,128)(2,1)S(1)} %pad_maximum_fusion.3), channel_id=1, source_target_pairs={{0,24},{4,28},{8,16},{12,20},{16,8},{20,12},{24,0},{28,4},{1,25},{... | collective-permute-start | bytes 294920 | tf_op jit(solution)/shard_map/ppermute | solution.py:47
  20.4 9.6 %collective-permute-start.5 = (bf16[42,32,128]{2,1,0:T(8,128)(2,1)S(1)}, bf16[42,32,128]{2,1,0:T(8,128)(2,1)S(1)}, u32[]{:S(2)}, u32[]{:S(2)}) collective-permute-start(bf16[42,32,128]{2,1,0:T(8,128)(2,1)S(1)} %bitcast.42), channel_id=1, source_target_pairs={{0,4},{4,0},{8,12},{12,8},{16,20},{20,16},{24,28},{28,24},{1,5},{5... | collective-permute-start | bytes 1032200 | tf_op jit(solution)/shard_map/ppermute | solution.py:44
  20.4 11.1 %collective-permute-start.10 = (bf16[42,32,128]{2,1,0:T(8,128)(2,1)S(1)}, bf16[42,32,128]{2,1,0:T(8,128)(2,1)S(1)}, u32[]{:S(2)}, u32[]{:S(2)}) collective-permute-start(bf16[42,32,128]{2,1,0:T(8,128)(2,1)S(1)} %bitcast.43), channel_id=1, source_target_pairs={{0,1},{1,2},{2,3},{3,7},{4,0},{5,4},{6,5},{7,6},{8,9},{9,10},{10,1... | collective-permute-start | bytes 1032200 | tf_op jit(solution)/shard_map/ppermute | solution.py:55
  30.0 6.3 %collective-permute-start.6 = (bf16[42,32,128]{2,1,0:T(8,128)(2,1)S(1)}, bf16[42,32,128]{2,1,0:T(8,128)(2,1)}, u32[]{:S(2)}, u32[]{:S(2)}) collective-permute-start(bf16[42,32,128]{2,1,0:T(8,128)(2,1)S(1)} %collective-permute-done.5), channel_id=1, source_target_pairs={{0,1},{1,2},{2,3},{3,7},{4,0},{5,4},{6,5},{7,6},{8,9},{9,10},{10,1... | collective-permute-start | bytes 1032200 | tf_op jit(solution)/shard_map/ppermute | solution.py:55
  32.6 7.4 %collective-permute-start.11 = (bf16[42,32,128]{2,1,0:T(8,128)(2,1)S(1)}, bf16[42,32,128]{2,1,0:T(8,128)(2,1)S(1)}, u32[]{:S(2)}, u32[]{:S(2)}) collective-permute-start(bf16[42,32,128]{2,1,0:T(8,128)(2,1)S(1)} %fusion.2), channel_id=1, source_target_pairs={{0,1},{1,2},{2,3},{3,7},{4,0},{5,4},{6,5},{7,6},{8,9},{9,10},{10,1... | collective-permute-start | bytes 1032200 | tf_op jit(solution)/shard_map/ppermute | solution.py:55
  37.4 7.4 %collective-permute-start.7 = (bf16[42,32,128]{2,1,0:T(8,128)(2,1)S(1)}, bf16[42,32,128]{2,1,0:T(8,128)(2,1)S(1)}, u32[]{:S(2)}, u32[]{:S(2)}) collective-permute-start(bf16[42,32,128]{2,1,0:T(8,128)(2,1)S(1)} %fusion.5), channel_id=1, source_target_pairs={{0,1},{1,2},{2,3},{3,7},{4,0},{5,4},{6,5},{7,6},{8,9},{9,10},{10,1... | collective-permute-start | bytes 1032200 | tf_op jit(solution)/shard_map/ppermute | solution.py:55
  41.9 7.5 %collective-permute-start.12 = (bf16[42,32,128]{2,1,0:T(8,128)(2,1)}, bf16[42,32,128]{2,1,0:T(8,128)(2,1)S(1)}, u32[]{:S(2)}, u32[]{:S(2)}) collective-permute-start(bf16[42,32,128]{2,1,0:T(8,128)(2,1)} %fusion.1), channel_id=1, source_target_pairs={{0,1},{1,2},{2,3},{3,7},{4,0},{5,4},{6,5},{7,6},{8,9},{9,10},{10,1... | collective-permute-start | bytes 1032200 | tf_op jit(solution)/shard_map/ppermute | solution.py:55
  44.8 12.9 %copy-start.3 = (bf16[42,32,128]{2,1,0:T(8,128)(2,1)}, bf16[42,32,128]{2,1,0:T(8,128)(2,1)S(1)}, u32[]{:S(2)}) copy-start(bf16[42,32,128]{2,1,0:T(8,128)(2,1)S(1)} %collective-permute-done.7) | copy-start | bytes 1032196
  44.9 8.0 %collective-permute-start.8 = (bf16[42,32,128]{2,1,0:T(8,128)(2,1)S(1)}, bf16[42,32,128]{2,1,0:T(8,128)(2,1)}, u32[]{:S(2)}, u32[]{:S(2)}) collective-permute-start(bf16[42,32,128]{2,1,0:T(8,128)(2,1)S(1)} %fusion.4), channel_id=1, source_target_pairs={{0,1},{1,2},{2,3},{3,7},{4,0},{5,4},{6,5},{7,6},{8,9},{9,10},{10,1... | collective-permute-start | bytes 1032200 | tf_op jit(solution)/shard_map/ppermute | solution.py:55
  50.5 7.2 %collective-permute-start.13 = (bf16[42,32,128]{2,1,0:T(8,128)(2,1)S(1)}, bf16[42,32,128]{2,1,0:T(8,128)(2,1)S(1)}, u32[]{:S(2)}, u32[]{:S(2)}) collective-permute-start(bf16[42,32,128]{2,1,0:T(8,128)(2,1)S(1)} %fusion), channel_id=1, source_target_pairs={{0,1},{1,2},{2,3},{3,7},{4,0},{5,4},{6,5},{7,6},{8,9},{9,10},{10,1... | collective-permute-start | bytes 1032200 | tf_op jit(solution)/shard_map/ppermute | solution.py:55
  54.1 7.4 %collective-permute-start.9 = (bf16[42,32,128]{2,1,0:T(8,128)(2,1)S(1)}, bf16[42,32,128]{2,1,0:T(8,128)(2,1)S(1)}, u32[]{:S(2)}, u32[]{:S(2)}) collective-permute-start(bf16[42,32,128]{2,1,0:T(8,128)(2,1)S(1)} %fusion.3), channel_id=1, source_target_pairs={{0,1},{1,2},{2,3},{3,7},{4,0},{5,4},{6,5},{7,6},{8,9},{9,10},{10,1... | collective-permute-start | bytes 1032200 | tf_op jit(solution)/shard_map/ppermute | solution.py:55
  57.7 3.8 %collective-permute-start.14 = (bf16[42,32,128]{2,1,0:T(8,128)(2,1)S(1)}, bf16[42,32,128]{2,1,0:T(8,128)(2,1)S(1)}, u32[]{:S(2)}, u32[]{:S(2)}) collective-permute-start(bf16[42,32,128]{2,1,0:T(8,128)(2,1)S(1)} %collective-permute-done.13), channel_id=1, source_target_pairs={{0,4},{4,0},{8,12},{12,8},{16,20},{20,16},{24,28},{28,24},{1,5},{5... | collective-permute-start | bytes 1032200 | tf_op jit(solution)/shard_map/ppermute | solution.py:44
  57.7 4.7 %collective-permute-start.15 = (bf16[42,32,128]{2,1,0:T(8,128)(2,1)}, bf16[42,32,128]{2,1,0:T(8,128)(2,1)S(1)}, u32[]{:S(2)}, u32[]{:S(2)}) collective-permute-start(bf16[42,32,128]{2,1,0:T(8,128)(2,1)} %collective-permute-done.6), channel_id=1, source_target_pairs={{0,4},{4,0},{8,12},{12,8},{16,20},{20,16},{24,28},{28,24},{1,5},{5... | collective-permute-start | bytes 1032200 | tf_op jit(solution)/shard_map/ppermute | solution.py:44
  58.2 4.2 %collective-permute-start.16 = (bf16[42,32,128]{2,1,0:T(8,128)(2,1)}, bf16[42,32,128]{2,1,0:T(8,128)(2,1)S(1)}, u32[]{:S(2)}, u32[]{:S(2)}) collective-permute-start(bf16[42,32,128]{2,1,0:T(8,128)(2,1)} %copy-done.3), channel_id=1, source_target_pairs={{0,4},{4,0},{8,12},{12,8},{16,20},{20,16},{24,28},{28,24},{1,5},{5... | collective-permute-start | bytes 1032200 | tf_op jit(solution)/shard_map/ppermute | solution.py:44
  58.2 4.2 %collective-permute-start.17 = (bf16[42,32,128]{2,1,0:T(8,128)(2,1)}, bf16[42,32,128]{2,1,0:T(8,128)(2,1)}, u32[]{:S(2)}, u32[]{:S(2)}) collective-permute-start(bf16[42,32,128]{2,1,0:T(8,128)(2,1)} %collective-permute-done.8), channel_id=1, source_target_pairs={{0,4},{4,0},{8,12},{12,8},{16,20},{20,16},{24,28},{28,24},{1,5},{5... | collective-permute-start | bytes 1032200 | tf_op jit(solution)/shard_map/ppermute | solution.py:44
  62.4 1.2 %copy-start = (bf16[1024,512]{1,0:T(8,128)(2,1)S(1)}, bf16[1024,512]{1,0:T(8,128)(2,1)}, u32[]{:S(2)}) copy-start(bf16[1024,512]{1,0:T(8,128)(2,1)} %all-gather.3.cloned.1.call-done) | copy-start | bytes 3145732
Sparse Core Ops, SparseCore 0:
  34.4 20.5 all-gather.2

commit v2 on v1

v2 whole, which is shorter than its diff:
```python
import functools
import math

import jax
import jax.numpy as jnp
from jax import lax
from jax.experimental import pallas as pl
from jax.experimental.pallas import tpu as pltpu
from jax.sharding import PartitionSpec as P

LIMIT = 8
TWICE = 0
SPLIT = 1
COST = 1 * 10**8
BF16 = jnp.bfloat16
F32 = jnp.float32
LANES = 128
VMEM = pl.BlockSpec(memory_space=pltpu.VMEM)
ANY = pl.BlockSpec(memory_space=pl.ANY)
PARAMS = pltpu.CompilerParams(vmem_limit_bytes=LIMIT * 1024 * 1024)


class Plan:
    def __init__(self, mesh, normed, grad_kv):
        self.n_dp, self.n_t = mesh.shape["dp"], mesh.shape["tensor"]
        self.chips = self.n_dp // 2
        self.rows, self.feats = normed.shape
        self.kv = grad_kv.shape[1]
        self.width = self.feats // self.n_dp
        self.tokens = self.rows * self.n_dp
        self.tiles = self.feats // LANES
        self.half_tiles = self.tokens // 2 // LANES
        starts = [self.width * d // LANES * LANES for d in range(self.n_dp)]
        ends = [self.width * d - s + self.width for d, s in enumerate(starts)]
        self.window = -(-max(ends) // LANES) * LANES
        self.step = math.gcd(self.width, LANES)
        self.power = self.chips & (self.chips - 1) == 0

    def chip_to(self, chip, q):
        return chip ^ q if self.power else lax.rem(chip + q, self.chips) if not isinstance(chip, int) else (chip + q) % self.chips

    def chip_from(self, chip, q):
        return chip ^ q if self.power else lax.rem(chip + self.chips - q, self.chips)

    def start_of(self, d):
        exact = d * self.width
        return jnp.minimum(exact // LANES * LANES, self.feats - self.window)

    def swap_cores(self, x):
        return lax.ppermute(x, "dp", [(d, d ^ 1) for d in range(self.n_dp)])

    def to_chip(self, x, q):
        return lax.ppermute(x, "dp", [(d, 2 * self.chip_to(d // 2, q) + d % 2) for d in range(self.n_dp)])

    def along(self, x):
        pairs = []
        for d in range(self.n_dp):
            for t in range(self.n_t):
                to = t - 1 if d % 2 else t + 1
                pairs.append((d * self.n_t + t, d * self.n_t + to if 0 <= to < self.n_t else (d ^ 1) * self.n_t + t))
        return lax.ppermute(x, ("dp", "tensor"), pairs)


def split_kernel(plan, normed_ref, *out_refs):
    chip = lax.axis_index("dp") // 2
    for q, out_ref in enumerate(out_refs):
        for group in range(2):
            start = pl.multiple_of(plan.start_of(2 * plan.chip_to(chip, q) + group), LANES)
            out_ref[group] = normed_ref[:, pl.ds(start, plan.window)]


def turn_kernel(plan, *refs):
    pieces, out_ref, scratch = refs[: plan.chips], refs[-2], refs[-1]
    chip = lax.axis_index("dp") // 2
    per_tile = LANES // plan.rows
    for group in range(2):
        d = 2 * chip + group
        offset = pl.multiple_of(d * plan.width - plan.start_of(d), plan.step)
        for j in range(plan.half_tiles):
            tile = jnp.concatenate([ref[group] for ref in pieces[j * per_tile : (j + 1) * per_tile]], axis=0)
            scratch[...] = tile.T
            out_ref[group, j] = scratch[pl.ds(offset, plan.width), :]


def partial_kernel(plan, own_ref, other_ref, *refs):
    weights, out_refs = refs[:-2], refs[-2:]
    both = jnp.concatenate([own_ref[...], other_ref[...]], axis=0)
    product = lax.dot_general(both, jnp.concatenate([ref[...] for ref in weights], axis=0), (((1,), (1,)), ((), ())), preferred_element_type=F32).astype(BF16)
    for half, out_ref in enumerate(out_refs):
        for r in range(plan.n_t):
            at = (half * plan.n_t + r) * plan.rows
            for j in range(out_ref.shape[1]):
                out_ref[r, j] = product[at : at + plan.rows, j * LANES : (j + 1) * LANES]


def pass_kernel(plan, slot, received_ref, partial_ref, *refs):
    n, out_ref = plan.n_t, refs[-1]
    core, t = lax.axis_index("dp") % 2, lax.axis_index("tensor")
    place = jnp.where(core == 0, t, n - 1 - t)
    target = jnp.clip(jnp.where(core == 0, t + n - slot + 1, t - (n - slot + 1)), 0, n - 1)

    @pl.when(place >= slot - 1)
    def _():
        out_ref[...] = received_ref[...]

    @pl.when(place == 0)
    def _():
        out_ref[...] = partial_ref[target]

    @pl.when((place > 0) & (place < slot - 1))
    def _():
        for j in range(plan.tiles):
            out_ref[j] = (received_ref[j].astype(F32) + partial_ref[target, j].astype(F32)).astype(BF16)


def weight_kernel(plan, *refs):
    n, half = plan.n_t, plan.tokens // 2 // plan.n_t
    kv_refs, own, theirs = refs[:2], refs[2 : 2 + 2 * n], refs[2 + 2 * n : -4]
    out_ref, token_ref, block, rows = refs[-4:]
    core, t = lax.axis_index("dp") % 2, lax.axis_index("tensor")
    place = jnp.where(core == 0, t, n - 1 - t)
    shape = (plan.half_tiles, plan.width, LANES)
    for k in range(n):
        source = jnp.where(core == 0, lax.rem(t + n - k, n), lax.rem(t + k, n))
        at = pl.ds(pl.multiple_of(source * plan.rows, plan.rows), plan.rows)
        for parity in range(2):
            begin = (2 * k + parity) * plan.half_tiles * LANES
            for q in range(plan.chips):
                rows[begin + q * plan.rows : begin + (q + 1) * plan.rows, :] = kv_refs[parity][q, at, :]

            def fill(ref, group):
                piece = ref[group].reshape(shape)
                for j in range(plan.half_tiles):
                    block[:, begin + j * LANES : begin + (j + 1) * LANES] = piece[j]

            if k:
                pl.when(place >= k)(lambda: fill(own[2 * k + parity], core))
                pl.when(place < k)(lambda: fill(theirs[n - k - 1], 1 - parity))
            else:
                fill(own[parity], core)
    token_ref[...] = jnp.zeros_like(token_ref)
    out_ref[...] = jnp.dot(block[...], rows[...], preferred_element_type=F32)


def pick_kernel(first_ref, second_ref, out_ref):
    core = lax.axis_index("dp") % 2
    out_ref[0] = first_ref[1 - core]
    out_ref[1] = second_ref[1 - core]


def stack_kernel(*refs):
    for i, ref in enumerate(refs[:-1]):
        refs[-1][i] = ref[...]


def hold_kernel(x_ref, after_ref, out_ref):
    out_ref[...] = x_ref[...]


def half_kernel(plan, partial_ref, mine_ref, after_ref, out_ref):
    n = plan.n_t
    core, t = lax.axis_index("dp") % 2, lax.axis_index("tensor")
    place = jnp.where(core == 0, t, n - 1 - t)
    for j in range(plan.tiles):
        out_ref[j] = partial_ref[t, j].astype(F32) + jnp.where(place >= 1, mine_ref[j].astype(F32), 0.0)


def input_kernel(plan, half_ref, theirs_ref, out_ref):
    n = plan.n_t
    core, t = lax.axis_index("dp") % 2, lax.axis_index("tensor")
    place = jnp.where(core == 0, t, n - 1 - t)
    for j in range(plan.tiles):
        total = half_ref[j] + jnp.where(place < n - 1, theirs_ref[j].astype(F32), 0.0)
        out_ref[:, j * LANES : (j + 1) * LANES] = total.astype(BF16)


def body(mesh, normed, grad_kv, weight):
    plan = Plan(mesh, normed, grad_kv)
    n = plan.n_t
    flat = (plan.tiles, plan.rows, LANES)
    halves = (2, plan.tiles // 2, plan.rows, LANES)
    core = lax.axis_index("dp") % 2

    other_kv = plan.swap_cores(grad_kv)
    near_kv = plan.swap_cores(other_kv) if TWICE else grad_kv
    pieces = pl.pallas_call(
        functools.partial(split_kernel, plan),
        out_shape=[jax.ShapeDtypeStruct((2, plan.rows, plan.window), BF16)] * plan.chips,
        in_specs=[VMEM], out_specs=[VMEM] * plan.chips, compiler_params=PARAMS, name="split",
    )(normed)
    order = range(plan.chips - 1, 0, -1)
    moved = {q: plan.to_chip(pieces[q], q) for q in order}
    pieces = [pieces[0]] + [moved[q] for q in range(1, plan.chips)]

    group = 6
    part_own, part_other = pl.pallas_call(
        functools.partial(partial_kernel, plan),
        out_shape=[jax.ShapeDtypeStruct((n,) + flat, BF16)] * 2,
        grid=(plan.tiles // group,),
        in_specs=[
            pl.BlockSpec(grad_kv.shape, lambda i: (0, 0)),
            pl.BlockSpec(grad_kv.shape, lambda i: (0, 0)),
        ]
        + [pl.BlockSpec((group * LANES // SPLIT, plan.kv), functools.partial(lambda j, i: (SPLIT * i + j, 0), j)) for j in range(SPLIT)],
        out_specs=[pl.BlockSpec((n, group, plan.rows, LANES), lambda i: (0, i, 0, 0))] * 2,
        compiler_params=PARAMS, name="partials",
        cost_estimate=pl.CostEstimate(flops=4 * grad_kv.size * plan.feats, bytes_accessed=weight.size * 2 + 2 * n * normed.size * 2, transcendentals=0),
    )(near_kv, other_kv, *[weight] * SPLIT)

    first = pl.pallas_call(
        functools.partial(turn_kernel, plan),
        out_shape=jax.ShapeDtypeStruct((2, plan.half_tiles, plan.width, LANES), BF16),
        in_specs=[VMEM] * plan.chips + [ANY], out_specs=VMEM,
        scratch_shapes=[pltpu.VMEM((plan.window, LANES), BF16)],
        compiler_params=PARAMS, name="turn",
    )(*pieces, part_own).reshape(flat)
    second = plan.swap_cores(first)

    def passed(received, partial, slot, after):
        return pl.pallas_call(
            functools.partial(pass_kernel, plan, slot),
            out_shape=jax.ShapeDtypeStruct(flat, BF16),
            in_specs=[VMEM] * 2 + [ANY] * len(after), out_specs=VMEM, compiler_params=PARAMS, name="passed",
            cost_estimate=pl.CostEstimate(flops=COST, bytes_accessed=0, transcendentals=0),
        )(received, partial, *after)

    own, theirs = [first.reshape(halves), second.reshape(halves)], []
    first, second = plan.along(first), plan.along(second)

    held_kv = pl.pallas_call(
        hold_kernel, out_shape=jax.ShapeDtypeStruct(grad_kv.shape, BF16),
        in_specs=[VMEM, ANY], out_specs=VMEM, compiler_params=PARAMS, name="hold",
    )(near_kv, first)
    kv = pl.pallas_call(
        stack_kernel, out_shape=jax.ShapeDtypeStruct((plan.chips,) + grad_kv.shape, BF16),
        in_specs=[VMEM] * plan.chips, out_specs=VMEM, compiler_params=PARAMS, name="stack",
    )(*[plan.to_chip(held_kv, q) if q else held_kv for q in range(plan.chips)])
    kvs = [kv, plan.swap_cores(kv)]
    trail = [own[1], second]
    for slot in range(2, n + 1):
        got = [first.reshape(halves), second.reshape(halves)]
        own += got
        sent = [passed(first, part_other, slot, [trail[slot - 2]]), passed(second, part_own, slot, theirs[-1:])]
        first, second = plan.along(sent[0]), plan.along(sent[1])
        trail.append(second)
        theirs.append(plan.swap_cores(pl.pallas_call(
            pick_kernel, out_shape=jax.ShapeDtypeStruct(halves, BF16), in_specs=[VMEM] * 2, out_specs=VMEM,
            compiler_params=PARAMS, name="pick",
        )(*got)))
    rest = plan.swap_cores(first)

    grad_weight, token = pl.pallas_call(
        functools.partial(weight_kernel, plan),
        out_shape=(jax.ShapeDtypeStruct((plan.width, plan.kv), F32), jax.ShapeDtypeStruct((8, LANES), F32)),
        in_specs=[VMEM] * (3 * n + 1), out_specs=(VMEM, VMEM),
        scratch_shapes=[pltpu.VMEM((plan.width, n * plan.tokens), BF16), pltpu.VMEM((n * plan.tokens, plan.kv), BF16)],
        compiler_params=pltpu.CompilerParams(vmem_limit_bytes=8 * 1024 * 1024 + 4 * n * plan.tokens * (plan.width + plan.kv)), name="weights",
        cost_estimate=pl.CostEstimate(flops=2 * n * normed.size * plan.kv, bytes_accessed=4 * plan.width * plan.kv, transcendentals=0),
    )(*kvs, *own, *theirs)

    half = pl.pallas_call(
        functools.partial(half_kernel, plan),
        out_shape=jax.ShapeDtypeStruct(flat, F32),
        in_specs=[VMEM] * 2 + [ANY], out_specs=VMEM,
        compiler_params=PARAMS, name="half",
        cost_estimate=pl.CostEstimate(flops=COST, bytes_accessed=0, transcendentals=0),
    )(part_own, second, token)
    grad_input = pl.pallas_call(
        functools.partial(input_kernel, plan),
        out_shape=jax.ShapeDtypeStruct(normed.shape, BF16),
        in_specs=[VMEM] * 2, out_specs=VMEM,
        compiler_params=PARAMS, name="inputs",
    )(half, rest)
    return grad_input, grad_weight


def solution(mesh):
    in_specs = (P(("dp", "tensor"), None), P("dp", "tensor"), P(None, "tensor"))
    out_specs = (P(("dp", "tensor"), None), P("dp", "tensor"))
    return jax.shard_map(functools.partial(body, mesh), mesh=mesh, in_specs=in_specs, out_specs=out_specs, check_vma=False)
```

time: 73.9 us -> 49.2 us (0.67)
  between operations: 14.2 us -> 0.83 us
  other arithmetic: 6.49 us -> 0 us
  waiting for transfers between devices: 15.2 us -> 10.3 us
  Pallas kernels: 10.4 us -> 6.91 us
  starting transfers between devices: 23.4 us -> 26.5 us
    convert_element_type x6 -> x0, other arithmetic: 6.45 us -> none  [passed(): return (arrived + jnp.where(place < slot - 1, mine, 0.0)).astype(BF16)]
    ppermute x3 -> x6, starting transfers between devices: 4.35 us -> 8.66 us  [to_chip(): lax.ppermute(x, 'dp', [(d, 2 * self.chip_to(d // 2, q) + d % 2) for d in...]
    pallas_call x3 -> x15, Pallas kernels: 9.26 us -> 5.9 us  [the longest x1 3.02 us: body(): pl.pallas_call(functools.partial(partial_kernel, plan), out_shape=[jax.Sh...]
    ppermute x3 -> x6, waiting for transfers between devices: 5.48 us -> 2.65 us  [to_chip(): lax.ppermute(x, 'dp', [(d, 2 * self.chip_to(d // 2, q) + d % 2) for d in...]
    unnamed x8 -> x6, local copies, waits for them, and re-layouts: 2.2 us -> 4.44 us
    slice x1 -> x0, local copies, waits for them, and re-layouts: 1.61 us -> none  [body(): part_own, part_other = (part[:n], part[n:])]
    ppermute x7, waiting for transfers between devices: 1.38 us -> 0.15 us  [swap_cores(): return lax.ppermute(x, 'dp', [(d, d ^ 1) for d in range(self.n_dp)])]
    ppermute x8, starting transfers between devices: 17.3 us -> 16.5 us  [along(): return lax.ppermute(x, ('dp', 'tensor'), pairs)]
  transfers between devices with their start and end apart: 19 -> 21, of which waited for: 10 -> 7; matrix products, arithmetic and copies ran while one was open for 11% -> 0% of each run, Pallas kernels for 10% -> 12%
where the time goes in v2:
time: 49.2 us; the launch traced here: 49 us
  starting transfers between devices  26.5 us (54%)
  waiting for transfers between devices  10.3 us (21%)
  Pallas kernels  6.91 us (14%)
  local copies, waits for them, and re-layouts  4.44 us (9%)
  between operations  0.83 us (2%)
    ppermute x8, starting transfers between devices, along(): return lax.ppermute(x, ('dp', 'tensor'), pairs)  16.5 us
    ppermute x6, starting transfers between devices, to_chip(): lax.ppermute(x, 'dp', [(d, 2 * self.chip_to(d // 2, q) + d % 2) for d in...  8.66 us
    ppermute x8, waiting for transfers between devices, along(): return lax.ppermute(x, ('dp', 'tensor'), pairs)  7.55 us
    unnamed x6, local copies, waits for them, and re-layouts  4.44 us
    pallas_call x1, Pallas kernels, body(): pl.pallas_call(functools.partial(partial_kernel, plan), out_shape=[jax.Sh...  3.02 us
    ppermute x6, waiting for transfers between devices, to_chip(): lax.ppermute(x, 'dp', [(d, 2 * self.chip_to(d // 2, q) + d % 2) for d in...  2.65 us
    pallas_call x1, Pallas kernels, body(): pl.pallas_call(functools.partial(weight_kernel, plan), out_shape=(jax.Sha...  2.42 us
    ppermute x7, starting transfers between devices, swap_cores(): return lax.ppermute(x, 'dp', [(d, d ^ 1) for d in range(self.n_dp)])  1.35 us
  transfers between devices with their start and end apart: 21, of which 7 were waited for; matrix products, arithmetic and copies ran while one was open for 0% of the time, Pallas kernels for 12%

profile of v2, /device:TPU:0, one launch (start us, length us, event | category | flops | bytes accessed | tf_op | source)
XLA Modules:
  0.0 49.0 jit_solution(4703307164475083899)
XLA Ops:
  0.6 0.5 %collective-permute-start = (bf16[128,512]{1,0:T(8,128)(2,1)}, bf16[128,512]{1,0:T(8,128)(2,1)S(1)}, u32[]{:S(2)}, u32[]{:S(2)}) collective-permute-start(bf16[128,512]{1,0:T(8,128)(2,1)} %x_ref.1), channel_id=1, source_target_pairs={{0,4},{4,0},{8,12},{12,8},{16,20},{20,16},{24,28},{28,24},{1,5},{5... | collective-permute-start | bytes 393224 | tf_op jit(solution)/shard_map/ppermute | solution.py:50
  1.1 1.0 %copy-done.2 = bf16[32,5376]{1,0:T(8,128)(2,1)S(1)} copy-done((bf16[32,5376]{1,0:T(8,128)(2,1)S(1)}, bf16[32,5376]{1,0:T(8,128)(2,1)}, u32[]{:S(2)}) %copy-start.2) | copy-done | bytes 344088
  2.2 2.6 %collective-permute-start.1 = (bf16[2,32,768]{2,1,0:T(8,128)(2,1)S(1)}, bf16[2,32,768]{2,1,0:T(8,128)(2,1)S(1)}, u32[]{:S(2)}, u32[]{:S(2)}) collective-permute-start(bf16[2,32,768]{2,1,0:T(8,128)(2,1)S(1)} %get-tuple-element.12), channel_id=1, source_target_pairs={{0,8},{4,12},{8,0},{12,4},{16,24},{20,28},{24,16},{28,20},{1,9},{5... | collective-permute-start | bytes 294920 | tf_op jit(solution)/shard_map/ppermute | solution.py:53
  4.7 1.5 %collective-permute-start.2 = (bf16[2,32,768]{2,1,0:T(8,128)(2,1)S(1)}, bf16[2,32,768]{2,1,0:T(8,128)(2,1)S(1)}, u32[]{:S(2)}, u32[]{:S(2)}) collective-permute-start(bf16[2,32,768]{2,1,0:T(8,128)(2,1)S(1)} %get-tuple-element.13), channel_id=1, source_target_pairs={{0,16},{4,20},{8,24},{12,28},{16,0},{20,4},{24,8},{28,12},{1,17},{... | collective-permute-start | bytes 294920 | tf_op jit(solution)/shard_map/ppermute | solution.py:53
  6.3 0.0 collective-permute-start.3
  6.3 0.0 collective-permute-done.other_ref
  6.3 2.6 %copy-done = bf16[5376,512]{1,0:T(8,128)(2,1)S(1)} copy-done((bf16[5376,512]{1,0:T(8,128)(2,1)S(1)}, bf16[5376,512]{1,0:T(8,128)(2,1)}, u32[]{:S(2)}) %copy-start) | copy-done | bytes 5505048
  8.9 0.9 %copy-done.1 = bf16[128,512]{1,0:T(8,128)(2,1)S(1)} copy-done((bf16[128,512]{1,0:T(8,128)(2,1)S(1)}, bf16[128,512]{1,0:T(8,128)(2,1)}, u32[]{:S(2)}) %copy-start.1) | copy-done | bytes 131096
  9.8 3.0 %partials.1 = (bf16[4,42,32,128]{3,2,1,0:T(8,128)(2,1)S(1)}, bf16[4,42,32,128]{3,2,1,0:T(8,128)(2,1)S(1)}) custom-call(bf16[128,512]{1,0:T(8,128)(2,1)S(1)} %copy-done.1, bf16[128,512]{1,0:T(8,128)(2,1)S(1)} %collective-permute-done.other_ref, bf16[5376,512]{1,0:T(8,128)(2,1)S(1)} %copy-done), custom_call_target="tpu_custom_call" | custom-call | flops 1409286144 | bytes 8257536 | tf_op jit(solution)/shard_map/partials/pallas_call | solution.py:196
  12.8 0.0 collective-permute-done.1.refs_1_
  12.8 0.0 collective-permute-done.2.refs_2_
  12.8 0.0 collective-permute-done.3.refs_3_
  12.8 0.2 turn.1
  13.0 0.1 collective-permute-start.4
  13.1 2.0 %collective-permute-start.7 = (bf16[42,32,128]{2,1,0:T(8,128)(2,1)S(1)}, bf16[42,32,128]{2,1,0:T(8,128)(2,1)S(1)}, u32[]{:S(2)}, u32[]{:S(2)}) collective-permute-start(bf16[42,32,128]{2,1,0:T(8,128)(2,1)S(1)} %bitcast.24), channel_id=1, source_target_pairs={{0,1},{1,2},{2,3},{3,7},{4,0},{5,4},{6,5},{7,6},{8,9},{9,10},{10,1... | collective-permute-start | bytes 1032200 | tf_op jit(solution)/shard_map/ppermute | solution.py:61
  15.1 0.0 collective-permute-done.4
  15.1 1.6 %collective-permute-start.5 = (bf16[42,32,128]{2,1,0:T(8,128)(2,1)S(1)}, bf16[42,32,128]{2,1,0:T(8,128)(2,1)S(1)}, u32[]{:S(2)}, u32[]{:S(2)}) collective-permute-start(bf16[42,32,128]{2,1,0:T(8,128)(2,1)S(1)} %collective-permute-done.4), channel_id=1, source_target_pairs={{0,1},{1,2},{2,3},{3,7},{4,0},{5,4},{6,5},{7,6},{8,9},{9,10},{10,1... | collective-permute-start | bytes 1032200 | tf_op jit(solution)/shard_map/ppermute | solution.py:61
  16.7 3.1 %collective-permute-done.7.received_ref.after_ref = bf16[42,32,128]{2,1,0:T(8,128)(2,1)S(1)} collective-permute-done((bf16[42,32,128]{2,1,0:T(8,128)(2,1)S(1)}, bf16[42,32,128]{2,1,0:T(8,128)(2,1)S(1)}, u32[]{:S(2)}, u32[]{:S(2)}) %collective-permute-start.7) | collective-permute-done | bytes 344096 | tf_op jit(solution)/shard_map/ppermute | solution.py:61
  19.9 2.5 %collective-permute-start.10 = (bf16[42,32,128]{2,1,0:T(8,128)(2,1)S(1)}, bf16[42,32,128]{2,1,0:T(8,128)(2,1)S(1)}, u32[]{:S(2)}, u32[]{:S(2)}) collective-permute-start(bf16[42,32,128]{2,1,0:T(8,128)(2,1)S(1)} %passed.8), channel_id=1, source_target_pairs={{0,1},{1,2},{2,3},{3,7},{4,0},{5,4},{6,5},{7,6},{8,9},{9,10},{10,1... | collective-permute-start | bytes 1032200 | tf_op jit(solution)/shard_map/ppermute | solution.py:61
  22.4 1.1 %collective-permute-done.5.received_ref.refs_0_ = bf16[42,32,128]{2,1,0:T(8,128)(2,1)S(1)} collective-permute-done((bf16[42,32,128]{2,1,0:T(8,128)(2,1)S(1)}, bf16[42,32,128]{2,1,0:T(8,128)(2,1)S(1)}, u32[]{:S(2)}, u32[]{:S(2)}) %collective-permute-start.5) | collective-permute-done | bytes 344096 | tf_op jit(solution)/shard_map/ppermute | solution.py:61
  23.6 2.5 %collective-permute-start.6 = (bf16[42,32,128]{2,1,0:T(8,128)(2,1)S(1)}, bf16[42,32,128]{2,1,0:T(8,128)(2,1)S(1)}, u32[]{:S(2)}, u32[]{:S(2)}) collective-permute-start(bf16[42,32,128]{2,1,0:T(8,128)(2,1)S(1)} %passed.6), channel_id=1, source_target_pairs={{0,1},{1,2},{2,3},{3,7},{4,0},{5,4},{6,5},{7,6},{8,9},{9,10},{10,1... | collective-permute-start | bytes 1032200 | tf_op jit(solution)/shard_map/ppermute | solution.py:61
  26.1 0.1 collective-permute-start.8
  26.2 1.0 %collective-permute-done.10.received_ref = bf16[42,32,128]{2,1,0:T(8,128)(2,1)S(1)} collective-permute-done((bf16[42,32,128]{2,1,0:T(8,128)(2,1)S(1)}, bf16[42,32,128]{2,1,0:T(8,128)(2,1)S(1)}, u32[]{:S(2)}, u32[]{:S(2)}) %collective-permute-start.10) | collective-permute-done | bytes 344096 | tf_op jit(solution)/shard_map/ppermute | solution.py:61
  27.3 2.5 %collective-permute-start.17 = (bf16[42,32,128]{2,1,0:T(8,128)(2,1)S(1)}, bf16[42,32,128]{2,1,0:T(8,128)(2,1)S(1)}, u32[]{:S(2)}, u32[]{:S(2)}) collective-permute-start(bf16[42,32,128]{2,1,0:T(8,128)(2,1)S(1)} %passed.10), channel_id=1, source_target_pairs={{0,1},{1,2},{2,3},{3,7},{4,0},{5,4},{6,5},{7,6},{8,9},{9,10},{10,1... | collective-permute-start | bytes 1032200 | tf_op jit(solution)/shard_map/ppermute | solution.py:61
  29.9 1.6 %collective-permute-start.13 = (bf16[128,512]{1,0:T(8,128)(2,1)S(1)}, bf16[128,512]{1,0:T(8,128)(2,1)S(1)}, u32[]{:S(2)}, u32[]{:S(2)}) collective-permute-start(bf16[128,512]{1,0:T(8,128)(2,1)S(1)} %hold.1.refs_0_), channel_id=1, source_target_pairs={{0,8},{4,12},{8,0},{12,4},{16,24},{20,28},{24,16},{28,20},{1,9},{5... | collective-permute-start | bytes 393224 | tf_op jit(solution)/shard_map/ppermute | solution.py:53
  31.4 0.0 collective-permute-done.6.received_ref.refs_0_
  31.4 0.0 collective-permute-done.8.refs_0_.refs_10_
  31.5 2.1 %collective-permute-start.9 = (bf16[42,32,128]{2,1,0:T(8,128)(2,1)S(1)}, bf16[42,32,128]{2,1,0:T(8,128)(2,1)S(1)}, u32[]{:S(2)}, u32[]{:S(2)}) collective-permute-start(bf16[42,32,128]{2,1,0:T(8,128)(2,1)S(1)} %passed.7), channel_id=1, source_target_pairs={{0,1},{1,2},{2,3},{3,7},{4,0},{5,4},{6,5},{7,6},{8,9},{9,10},{10,1... | collective-permute-start | bytes 1032200 | tf_op jit(solution)/shard_map/ppermute | solution.py:61
  33.5 1.5 %collective-permute-start.14 = (bf16[128,512]{1,0:T(8,128)(2,1)S(1)}, bf16[128,512]{1,0:T(8,128)(2,1)S(1)}, u32[]{:S(2)}, u32[]{:S(2)}) collective-permute-start(bf16[128,512]{1,0:T(8,128)(2,1)S(1)} %hold.1.refs_0_), channel_id=1, source_target_pairs={{0,16},{4,20},{8,24},{12,28},{16,0},{20,4},{24,8},{28,12},{1,17},{... | collective-permute-start | bytes 393224 | tf_op jit(solution)/shard_map/ppermute | solution.py:53
  35.1 1.5 %collective-permute-start.15 = (bf16[128,512]{1,0:T(8,128)(2,1)S(1)}, bf16[128,512]{1,0:T(8,128)(2,1)S(1)}, u32[]{:S(2)}, u32[]{:S(2)}) collective-permute-start(bf16[128,512]{1,0:T(8,128)(2,1)S(1)} %hold.1.refs_0_), channel_id=1, source_target_pairs={{0,24},{4,28},{8,16},{12,20},{16,8},{20,12},{24,0},{28,4},{1,25},{... | collective-permute-start | bytes 393224 | tf_op jit(solution)/shard_map/ppermute | solution.py:53
  36.5 0.0 collective-permute-done.17.received_ref
  36.6 0.1 collective-permute-start.11
  36.6 0.1 passed.11
  36.7 1.6 %collective-permute-start.19 = (bf16[42,32,128]{2,1,0:T(8,128)(2,1)S(1)}, bf16[42,32,128]{2,1,0:T(8,128)(2,1)S(1)}, u32[]{:S(2)}, u32[]{:S(2)}) collective-permute-start(bf16[42,32,128]{2,1,0:T(8,128)(2,1)S(1)} %passed.11), channel_id=1, source_target_pairs={{0,1},{1,2},{2,3},{3,7},{4,0},{5,4},{6,5},{7,6},{8,9},{9,10},{10,1... | collective-permute-start | bytes 1032200 | tf_op jit(solution)/shard_map/ppermute | solution.py:61
  38.3 1.2 %collective-permute-done.14.refs_2_ = bf16[128,512]{1,0:T(8,128)(2,1)S(1)} collective-permute-done((bf16[128,512]{1,0:T(8,128)(2,1)S(1)}, bf16[128,512]{1,0:T(8,128)(2,1)S(1)}, u32[]{:S(2)}, u32[]{:S(2)}) %collective-permute-start.14) | collective-permute-done | bytes 131104 | tf_op jit(solution)/shard_map/ppermute | solution.py:53
  39.5 1.5 %collective-permute-done.15.refs_3_ = bf16[128,512]{1,0:T(8,128)(2,1)S(1)} collective-permute-done((bf16[128,512]{1,0:T(8,128)(2,1)S(1)}, bf16[128,512]{1,0:T(8,128)(2,1)S(1)}, u32[]{:S(2)}, u32[]{:S(2)}) %collective-permute-start.15) | collective-permute-done | bytes 131104 | tf_op jit(solution)/shard_map/ppermute | solution.py:53
  41.0 0.1 collective-permute-start.16
  41.1 0.5 %collective-permute-start.18 = (bf16[2,21,32,128]{3,2,1,0:T(8,128)(2,1)S(1)}, bf16[2,21,32,128]{3,2,1,0:T(8,128)(2,1)S(1)}, u32[]{:S(2)}, u32[]{:S(2)}) collective-permute-start(bf16[2,21,32,128]{3,2,1,0:T(8,128)(2,1)S(1)} %pick.5), channel_id=1, source_target_pairs={{0,4},{4,0},{8,12},{12,8},{16,20},{20,16},{24,28},{28,24},{1,5},{5... | collective-permute-start | bytes 1032200 | tf_op jit(solution)/shard_map/ppermute | solution.py:50
  41.6 0.0 collective-permute-done.11.refs_0_.refs_11_
  41.7 1.6 %collective-permute-start.12 = (bf16[42,32,128]{2,1,0:T(8,128)(2,1)S(1)}, bf16[42,32,128]{2,1,0:T(8,128)(2,1)S(1)}, u32[]{:S(2)}, u32[]{:S(2)}) collective-permute-start(bf16[42,32,128]{2,1,0:T(8,128)(2,1)S(1)} %passed.9), channel_id=1, source_target_pairs={{0,1},{1,2},{2,3},{3,7},{4,0},{5,4},{6,5},{7,6},{8,9},{9,10},{10,1... | collective-permute-start | bytes 1032200 | tf_op jit(solution)/shard_map/ppermute | solution.py:61
  43.3 0.0 collective-permute-done.19
  43.3 0.0 collective-permute-start.20
  43.3 0.1 collective-permute-done.18.refs_12_
  43.4 2.4 %weights.1 = (f32[672,512]{1,0:T(8,128)}, f32[8,128]{1,0:T(8,128)S(1)}) custom-call(bf16[4,128,512]{2,1,0:T(8,128)(2,1)S(1)} %stack.1.refs_0_, bf16[4,128,512]{2,1,0:T(8,128)(2,1)S(1)} %collective-permute-done.16.refs_1_, bf16[2,21,32,128]{3,2,1,0:T(8,128)(2,1)S(1)} %bitcast.25, bf16[2,21,32,128]{3,2,1,0:T(8,128)(2,1)S(1)} %bitcast.22, ...), custom_call_target="tpu_custom_call" | custom-call | flops 704643072 | bytes 1376256 | tf_op jit(solution)/shard_map/weights/pallas_call | solution.py:252
  45.9 2.2 %collective-permute-done.12.mine_ref = bf16[42,32,128]{2,1,0:T(8,128)(2,1)S(1)} collective-permute-done((bf16[42,32,128]{2,1,0:T(8,128)(2,1)S(1)}, bf16[42,32,128]{2,1,0:T(8,128)(2,1)S(1)}, u32[]{:S(2)}, u32[]{:S(2)}) %collective-permute-start.12) | collective-permute-done | bytes 344096 | tf_op jit(solution)/shard_map/ppermute | solution.py:61
  48.0 0.1 half.1.half_ref
  48.2 0.0 collective-permute-done.20.theirs_ref
  48.2 0.8 %inputs.1 = bf16[32,5376]{1,0:T(8,128)(2,1)} custom-call(f32[42,32,128]{2,1,0:T(8,128)S(1)} %half.1.half_ref, bf16[42,32,128]{2,1,0:T(8,128)(2,1)S(1)} %collective-permute-done.20.theirs_ref), custom_call_target="tpu_custom_call" | custom-call | tf_op jit(solution)/shard_map/inputs/pallas_call | solution.py:268
  (17 shorter events, 0.3 us)
Async XLA Ops:
  0.6 5.7 %collective-permute-start = (bf16[128,512]{1,0:T(8,128)(2,1)}, bf16[128,512]{1,0:T(8,128)(2,1)S(1)}, u32[]{:S(2)}, u32[]{:S(2)}) collective-permute-start(bf16[128,512]{1,0:T(8,128)(2,1)} %x_ref.1), channel_id=1, source_target_pairs={{0,4},{4,0},{8,12},{12,8},{16,20},{20,16},{24,28},{28,24},{1,5},{5... | collective-permute-start | bytes 393224 | tf_op jit(solution)/shard_map/ppermute | solution.py:50
  1.1 1.0 %copy-start.2 = (bf16[32,5376]{1,0:T(8,128)(2,1)S(1)}, bf16[32,5376]{1,0:T(8,128)(2,1)}, u32[]{:S(2)}) copy-start(bf16[32,5376]{1,0:T(8,128)(2,1)} %normed_ref.1) | copy-start | bytes 1032196
  2.2 10.6 %collective-permute-start.1 = (bf16[2,32,768]{2,1,0:T(8,128)(2,1)S(1)}, bf16[2,32,768]{2,1,0:T(8,128)(2,1)S(1)}, u32[]{:S(2)}, u32[]{:S(2)}) collective-permute-start(bf16[2,32,768]{2,1,0:T(8,128)(2,1)S(1)} %get-tuple-element.12), channel_id=1, source_target_pairs={{0,8},{4,12},{8,0},{12,4},{16,24},{20,28},{24,16},{28,20},{1,9},{5... | collective-permute-start | bytes 294920 | tf_op jit(solution)/shard_map/ppermute | solution.py:53
  4.7 8.1 %collective-permute-start.2 = (bf16[2,32,768]{2,1,0:T(8,128)(2,1)S(1)}, bf16[2,32,768]{2,1,0:T(8,128)(2,1)S(1)}, u32[]{:S(2)}, u32[]{:S(2)}) collective-permute-start(bf16[2,32,768]{2,1,0:T(8,128)(2,1)S(1)} %get-tuple-element.13), channel_id=1, source_target_pairs={{0,16},{4,20},{8,24},{12,28},{16,0},{20,4},{24,8},{28,12},{1,17},{... | collective-permute-start | bytes 294920 | tf_op jit(solution)/shard_map/ppermute | solution.py:53
  6.3 6.5 %collective-permute-start.3 = (bf16[2,32,768]{2,1,0:T(8,128)(2,1)S(1)}, bf16[2,32,768]{2,1,0:T(8,128)(2,1)S(1)}, u32[]{:S(2)}, u32[]{:S(2)}) collective-permute-start(bf16[2,32,768]{2,1,0:T(8,128)(2,1)S(1)} %get-tuple-element.14), channel_id=1, source_target_pairs={{0,24},{4,28},{8,16},{12,20},{16,8},{20,12},{24,0},{28,4},{1,25},{... | collective-permute-start | bytes 294920 | tf_op jit(solution)/shard_map/ppermute | solution.py:53
  6.3 2.6 %copy-start = (bf16[5376,512]{1,0:T(8,128)(2,1)S(1)}, bf16[5376,512]{1,0:T(8,128)(2,1)}, u32[]{:S(2)}) copy-start(bf16[5376,512]{1,0:T(8,128)(2,1)} %refs_0_.1) | copy-start | bytes 16515076
  8.8 0.9 %copy-start.1 = (bf16[128,512]{1,0:T(8,128)(2,1)S(1)}, bf16[128,512]{1,0:T(8,128)(2,1)}, u32[]{:S(2)}) copy-start(bf16[128,512]{1,0:T(8,128)(2,1)} %x_ref.1) | copy-start | bytes 393220
  13.0 2.1 %collective-permute-start.4 = (bf16[42,32,128]{2,1,0:T(8,128)(2,1)S(1)}, bf16[42,32,128]{2,1,0:T(8,128)(2,1)S(1)}, u32[]{:S(2)}, u32[]{:S(2)}) collective-permute-start(bf16[42,32,128]{2,1,0:T(8,128)(2,1)S(1)} %bitcast.23), channel_id=1, source_target_pairs={{0,4},{4,0},{8,12},{12,8},{16,20},{20,16},{24,28},{28,24},{1,5},{5... | collective-permute-start | bytes 1032200 | tf_op jit(solution)/shard_map/ppermute | solution.py:50
  13.1 6.8 %collective-permute-start.7 = (bf16[42,32,128]{2,1,0:T(8,128)(2,1)S(1)}, bf16[42,32,128]{2,1,0:T(8,128)(2,1)S(1)}, u32[]{:S(2)}, u32[]{:S(2)}) collective-permute-start(bf16[42,32,128]{2,1,0:T(8,128)(2,1)S(1)} %bitcast.24), channel_id=1, source_target_pairs={{0,1},{1,2},{2,3},{3,7},{4,0},{5,4},{6,5},{7,6},{8,9},{9,10},{10,1... | collective-permute-start | bytes 1032200 | tf_op jit(solution)/shard_map/ppermute | solution.py:61
  15.1 8.5 %collective-permute-start.5 = (bf16[42,32,128]{2,1,0:T(8,128)(2,1)S(1)}, bf16[42,32,128]{2,1,0:T(8,128)(2,1)S(1)}, u32[]{:S(2)}, u32[]{:S(2)}) collective-permute-start(bf16[42,32,128]{2,1,0:T(8,128)(2,1)S(1)} %collective-permute-done.4), channel_id=1, source_target_pairs={{0,1},{1,2},{2,3},{3,7},{4,0},{5,4},{6,5},{7,6},{8,9},{9,10},{10,1... | collective-permute-start | bytes 1032200 | tf_op jit(solution)/shard_map/ppermute | solution.py:61
  19.9 7.3 %collective-permute-start.10 = (bf16[42,32,128]{2,1,0:T(8,128)(2,1)S(1)}, bf16[42,32,128]{2,1,0:T(8,128)(2,1)S(1)}, u32[]{:S(2)}, u32[]{:S(2)}) collective-permute-start(bf16[42,32,128]{2,1,0:T(8,128)(2,1)S(1)} %passed.8), channel_id=1, source_target_pairs={{0,1},{1,2},{2,3},{3,7},{4,0},{5,4},{6,5},{7,6},{8,9},{9,10},{10,1... | collective-permute-start | bytes 1032200 | tf_op jit(solution)/shard_map/ppermute | solution.py:61
  23.6 7.8 %collective-permute-start.6 = (bf16[42,32,128]{2,1,0:T(8,128)(2,1)S(1)}, bf16[42,32,128]{2,1,0:T(8,128)(2,1)S(1)}, u32[]{:S(2)}, u32[]{:S(2)}) collective-permute-start(bf16[42,32,128]{2,1,0:T(8,128)(2,1)S(1)} %passed.6), channel_id=1, source_target_pairs={{0,1},{1,2},{2,3},{3,7},{4,0},{5,4},{6,5},{7,6},{8,9},{9,10},{10,1... | collective-permute-start | bytes 1032200 | tf_op jit(solution)/shard_map/ppermute | solution.py:61
  26.1 5.3 %collective-permute-start.8 = (bf16[2,21,32,128]{3,2,1,0:T(8,128)(2,1)S(1)}, bf16[2,21,32,128]{3,2,1,0:T(8,128)(2,1)S(1)}, u32[]{:S(2)}, u32[]{:S(2)}) collective-permute-start(bf16[2,21,32,128]{3,2,1,0:T(8,128)(2,1)S(1)} %pick.3), channel_id=1, source_target_pairs={{0,4},{4,0},{8,12},{12,8},{16,20},{20,16},{24,28},{28,24},{1,5},{5... | collective-permute-start | bytes 1032200 | tf_op jit(solution)/shard_map/ppermute | solution.py:50
  27.3 9.2 %collective-permute-start.17 = (bf16[42,32,128]{2,1,0:T(8,128)(2,1)S(1)}, bf16[42,32,128]{2,1,0:T(8,128)(2,1)S(1)}, u32[]{:S(2)}, u32[]{:S(2)}) collective-permute-start(bf16[42,32,128]{2,1,0:T(8,128)(2,1)S(1)} %passed.10), channel_id=1, source_target_pairs={{0,1},{1,2},{2,3},{3,7},{4,0},{5,4},{6,5},{7,6},{8,9},{9,10},{10,1... | collective-permute-start | bytes 1032200 | tf_op jit(solution)/shard_map/ppermute | solution.py:61
  29.9 6.8 %collective-permute-start.13 = (bf16[128,512]{1,0:T(8,128)(2,1)S(1)}, bf16[128,512]{1,0:T(8,128)(2,1)S(1)}, u32[]{:S(2)}, u32[]{:S(2)}) collective-permute-start(bf16[128,512]{1,0:T(8,128)(2,1)S(1)} %hold.1.refs_0_), channel_id=1, source_target_pairs={{0,8},{4,12},{8,0},{12,4},{16,24},{20,28},{24,16},{28,20},{1,9},{5... | collective-permute-start | bytes 393224 | tf_op jit(solution)/shard_map/ppermute | solution.py:53
  31.5 9.6 %collective-permute-start.9 = (bf16[42,32,128]{2,1,0:T(8,128)(2,1)S(1)}, bf16[42,32,128]{2,1,0:T(8,128)(2,1)S(1)}, u32[]{:S(2)}, u32[]{:S(2)}) collective-permute-start(bf16[42,32,128]{2,1,0:T(8,128)(2,1)S(1)} %passed.7), channel_id=1, source_target_pairs={{0,1},{1,2},{2,3},{3,7},{4,0},{5,4},{6,5},{7,6},{8,9},{9,10},{10,1... | collective-permute-start | bytes 1032200 | tf_op jit(solution)/shard_map/ppermute | solution.py:61
  33.5 5.9 %collective-permute-start.14 = (bf16[128,512]{1,0:T(8,128)(2,1)S(1)}, bf16[128,512]{1,0:T(8,128)(2,1)S(1)}, u32[]{:S(2)}, u32[]{:S(2)}) collective-permute-start(bf16[128,512]{1,0:T(8,128)(2,1)S(1)} %hold.1.refs_0_), channel_id=1, source_target_pairs={{0,16},{4,20},{8,24},{12,28},{16,0},{20,4},{24,8},{28,12},{1,17},{... | collective-permute-start | bytes 393224 | tf_op jit(solution)/shard_map/ppermute | solution.py:53
  35.1 5.9 %collective-permute-start.15 = (bf16[128,512]{1,0:T(8,128)(2,1)S(1)}, bf16[128,512]{1,0:T(8,128)(2,1)S(1)}, u32[]{:S(2)}, u32[]{:S(2)}) collective-permute-start(bf16[128,512]{1,0:T(8,128)(2,1)S(1)} %hold.1.refs_0_), channel_id=1, source_target_pairs={{0,24},{4,28},{8,16},{12,20},{16,8},{20,12},{24,0},{28,4},{1,25},{... | collective-permute-start | bytes 393224 | tf_op jit(solution)/shard_map/ppermute | solution.py:53
  36.6 5.1 %collective-permute-start.11 = (bf16[2,21,32,128]{3,2,1,0:T(8,128)(2,1)S(1)}, bf16[2,21,32,128]{3,2,1,0:T(8,128)(2,1)S(1)}, u32[]{:S(2)}, u32[]{:S(2)}) collective-permute-start(bf16[2,21,32,128]{3,2,1,0:T(8,128)(2,1)S(1)} %pick.4), channel_id=1, source_target_pairs={{0,4},{4,0},{8,12},{12,8},{16,20},{20,16},{24,28},{28,24},{1,5},{5... | collective-permute-start | bytes 1032200 | tf_op jit(solution)/shard_map/ppermute | solution.py:50
  36.7 6.6 %collective-permute-start.19 = (bf16[42,32,128]{2,1,0:T(8,128)(2,1)S(1)}, bf16[42,32,128]{2,1,0:T(8,128)(2,1)S(1)}, u32[]{:S(2)}, u32[]{:S(2)}) collective-permute-start(bf16[42,32,128]{2,1,0:T(8,128)(2,1)S(1)} %passed.11), channel_id=1, source_target_pairs={{0,1},{1,2},{2,3},{3,7},{4,0},{5,4},{6,5},{7,6},{8,9},{9,10},{10,1... | collective-permute-start | bytes 1032200 | tf_op jit(solution)/shard_map/ppermute | solution.py:61
  41.0 2.3 %collective-permute-start.16 = (bf16[4,128,512]{2,1,0:T(8,128)(2,1)S(1)}, bf16[4,128,512]{2,1,0:T(8,128)(2,1)S(1)}, u32[]{:S(2)}, u32[]{:S(2)}) collective-permute-start(bf16[4,128,512]{2,1,0:T(8,128)(2,1)S(1)} %stack.1.refs_0_), channel_id=1, source_target_pairs={{0,4},{4,0},{8,12},{12,8},{16,20},{20,16},{24,28},{28,24},{1,5},{5... | collective-permute-start | bytes 1572872 | tf_op jit(solution)/shard_map/ppermute | solution.py:50
  41.1 2.3 %collective-permute-start.18 = (bf16[2,21,32,128]{3,2,1,0:T(8,128)(2,1)S(1)}, bf16[2,21,32,128]{3,2,1,0:T(8,128)(2,1)S(1)}, u32[]{:S(2)}, u32[]{:S(2)}) collective-permute-start(bf16[2,21,32,128]{3,2,1,0:T(8,128)(2,1)S(1)} %pick.5), channel_id=1, source_target_pairs={{0,4},{4,0},{8,12},{12,8},{16,20},{20,16},{24,28},{28,24},{1,5},{5... | collective-permute-start | bytes 1032200 | tf_op jit(solution)/shard_map/ppermute | solution.py:50
  41.7 6.4 %collective-permute-start.12 = (bf16[42,32,128]{2,1,0:T(8,128)(2,1)S(1)}, bf16[42,32,128]{2,1,0:T(8,128)(2,1)S(1)}, u32[]{:S(2)}, u32[]{:S(2)}) collective-permute-start(bf16[42,32,128]{2,1,0:T(8,128)(2,1)S(1)} %passed.9), channel_id=1, source_target_pairs={{0,1},{1,2},{2,3},{3,7},{4,0},{5,4},{6,5},{7,6},{8,9},{9,10},{10,1... | collective-permute-start | bytes 1032200 | tf_op jit(solution)/shard_map/ppermute | solution.py:61
  43.3 4.9 %collective-permute-start.20 = (bf16[42,32,128]{2,1,0:T(8,128)(2,1)S(1)}, bf16[42,32,128]{2,1,0:T(8,128)(2,1)S(1)}, u32[]{:S(2)}, u32[]{:S(2)}) collective-permute-start(bf16[42,32,128]{2,1,0:T(8,128)(2,1)S(1)} %collective-permute-done.19), channel_id=1, source_target_pairs={{0,4},{4,0},{8,12},{12,8},{16,20},{20,16},{24,28},{28,24},{1,5},{5... | collective-permute-start | bytes 1032200 | tf_op jit(solution)/shard_map/ppermute | solution.py:50

commit v3 on v2

--- a/solution.py
+++ b/solution.py
@@ -11,7 +11,7 @@
 LIMIT = 8
 TWICE = 0
 SPLIT = 1
-COST = 1 * 10**8
+COST = 10**6
 BF16 = jnp.bfloat16
 F32 = jnp.float32
 LANES = 128
@@ -187,6 +187,7 @@
         functools.partial(split_kernel, plan),
         out_shape=[jax.ShapeDtypeStruct((2, plan.rows, plan.window), BF16)] * plan.chips,
         in_specs=[VMEM], out_specs=[VMEM] * plan.chips, compiler_params=PARAMS, name="split",
+        cost_estimate=pl.CostEstimate(flops=6 * 10**9, bytes_accessed=0, transcendentals=0),
     )(normed)
     order = range(plan.chips - 1, 0, -1)
     moved = {q: plan.to_chip(pieces[q], q) for q in order}
@@ -230,7 +231,7 @@
     held_kv = pl.pallas_call(
         hold_kernel, out_shape=jax.ShapeDtypeStruct(grad_kv.shape, BF16),
         in_specs=[VMEM, ANY], out_specs=VMEM, compiler_params=PARAMS, name="hold",
-    )(near_kv, first)
+    )(near_kv, part_own)
     kv = pl.pallas_call(
         stack_kernel, out_shape=jax.ShapeDtypeStruct((plan.chips,) + grad_kv.shape, BF16),
         in_specs=[VMEM] * plan.chips, out_specs=VMEM, compiler_params=PARAMS, name="stack",
@@ -240,7 +241,7 @@
     for slot in range(2, n + 1):
         got = [first.reshape(halves), second.reshape(halves)]
         own += got
-        sent = [passed(first, part_other, slot, [trail[slot - 2]]), passed(second, part_own, slot, theirs[-1:])]
+        sent = [passed(first, part_other, slot, [trail[slot - 2]]), passed(second, part_own, slot, theirs[-1:] + ([kvs[1]] if slot == 3 else []))]
         first, second = plan.along(sent[0]), plan.along(sent[1])
         trail.append(second)
         theirs.append(plan.swap_cores(pl.pallas_call(

time: 49.2 us -> 46.5 us (0.945)
  local copies, waits for them, and re-layouts: 4.44 us -> 1.25 us
  waiting for transfers between devices: 10.3 us -> 11.6 us
  starting transfers between devices: 26.5 us -> 25.7 us
    unnamed x6, local copies, waits for them, and re-layouts: 4.44 us -> 1.25 us
    ppermute x6, waiting for transfers between devices: 2.65 us -> 5.45 us  [to_chip(): lax.ppermute(x, 'dp', [(d, 2 * self.chip_to(d // 2, q) + d % 2) for d in...]
    ppermute x8, waiting for transfers between devices: 7.55 us -> 6.13 us  [along(): return lax.ppermute(x, ('dp', 'tensor'), pairs)]
    ppermute x6, starting transfers between devices: 8.66 us -> 7.54 us  [to_chip(): lax.ppermute(x, 'dp', [(d, 2 * self.chip_to(d // 2, q) + d % 2) for d in...]
  transfers between devices with their start and end apart: 21 -> 21, of which waited for: 7 -> 11; matrix products, arithmetic and copies ran while one was open for 0% -> 0% of each run, Pallas kernels for 12% -> 13%
where the time goes in v3:
time: 46.5 us; the launch traced here: 46.4 us
  starting transfers between devices  25.7 us (55%)
  waiting for transfers between devices  11.6 us (25%)
  Pallas kernels  6.91 us (15%)
  local copies, waits for them, and re-layouts  1.25 us (3%)
  between operations  0.82 us (2%)
    ppermute x8, starting transfers between devices, along(): return lax.ppermute(x, ('dp', 'tensor'), pairs)  16.6 us
    ppermute x6, starting transfers between devices, to_chip(): lax.ppermute(x, 'dp', [(d, 2 * self.chip_to(d // 2, q) + d % 2) for d in...  7.54 us
    ppermute x8, waiting for transfers between devices, along(): return lax.ppermute(x, ('dp', 'tensor'), pairs)  6.13 us
    ppermute x6, waiting for transfers between devices, to_chip(): lax.ppermute(x, 'dp', [(d, 2 * self.chip_to(d // 2, q) + d % 2) for d in...  5.45 us
    pallas_call x1, Pallas kernels, body(): pl.pallas_call(functools.partial(partial_kernel, plan), out_shape=[jax.Sh...  3.03 us
    pallas_call x1, Pallas kernels, body(): pl.pallas_call(functools.partial(weight_kernel, plan), out_shape=(jax.Sha...  2.42 us
    ppermute x7, starting transfers between devices, swap_cores(): return lax.ppermute(x, 'dp', [(d, d ^ 1) for d in range(self.n_dp)])  1.63 us
    unnamed x6, local copies, waits for them, and re-layouts  1.25 us
  transfers between devices with their start and end apart: 21, of which 11 were waited for; matrix products, arithmetic and copies ran while one was open for 0% of the time, Pallas kernels for 13%

profile of v3, /device:TPU:0, one launch (start us, length us, event | category | flops | bytes accessed | tf_op | source)
XLA Modules:
  0.0 46.4 jit_solution(12995574950889868329)
XLA Ops:
  0.6 0.5 %collective-permute-start = (bf16[128,512]{1,0:T(8,128)(2,1)}, bf16[128,512]{1,0:T(8,128)(2,1)S(1)}, u32[]{:S(2)}, u32[]{:S(2)}) collective-permute-start(bf16[128,512]{1,0:T(8,128)(2,1)} %x_ref.1), channel_id=1, source_target_pairs={{0,4},{4,0},{8,12},{12,8},{16,20},{20,16},{24,28},{28,24},{1,5},{5... | collective-permute-start | bytes 393224 | tf_op jit(solution)/shard_map/ppermute | solution.py:50
  1.2 1.2 %copy-done.2 = bf16[32,5376]{1,0:T(8,128)(2,1)S(1)} copy-done((bf16[32,5376]{1,0:T(8,128)(2,1)S(1)}, bf16[32,5376]{1,0:T(8,128)(2,1)}, u32[]{:S(2)}) %copy-start.2) | copy-done | bytes 344088
  2.5 2.4 %collective-permute-start.1 = (bf16[2,32,768]{2,1,0:T(8,128)(2,1)S(1)}, bf16[2,32,768]{2,1,0:T(8,128)(2,1)S(1)}, u32[]{:S(2)}, u32[]{:S(2)}) collective-permute-start(bf16[2,32,768]{2,1,0:T(8,128)(2,1)S(1)} %get-tuple-element.12), channel_id=1, source_target_pairs={{0,8},{4,12},{8,0},{12,4},{16,24},{20,28},{24,16},{28,20},{1,9},{5... | collective-permute-start | bytes 294920 | tf_op jit(solution)/shard_map/ppermute | solution.py:53
  4.9 1.5 %collective-permute-start.2 = (bf16[2,32,768]{2,1,0:T(8,128)(2,1)S(1)}, bf16[2,32,768]{2,1,0:T(8,128)(2,1)S(1)}, u32[]{:S(2)}, u32[]{:S(2)}) collective-permute-start(bf16[2,32,768]{2,1,0:T(8,128)(2,1)S(1)} %get-tuple-element.13), channel_id=1, source_target_pairs={{0,16},{4,20},{8,24},{12,28},{16,0},{20,4},{24,8},{28,12},{1,17},{... | collective-permute-start | bytes 294920 | tf_op jit(solution)/shard_map/ppermute | solution.py:53
  6.4 0.0 collective-permute-start.3
  6.5 0.0 collective-permute-done.other_ref
  6.5 3.0 %partials.1 = (bf16[4,42,32,128]{3,2,1,0:T(8,128)(2,1)S(1)}, bf16[4,42,32,128]{3,2,1,0:T(8,128)(2,1)S(1)}) custom-call(bf16[128,512]{1,0:T(8,128)(2,1)S(1)} %copy-done.1, bf16[128,512]{1,0:T(8,128)(2,1)S(1)} %collective-permute-done.other_ref, bf16[5376,512]{1,0:T(8,128)(2,1)S(1)} %copy-done), custom_call_target="tpu_custom_call" | custom-call | flops 1409286144 | bytes 8257536 | tf_op jit(solution)/shard_map/partials/pallas_call | solution.py:197
  9.5 0.0 collective-permute-done.1.refs_1_
  9.5 1.7 %collective-permute-done.2.refs_2_ = bf16[2,32,768]{2,1,0:T(8,128)(2,1)S(1)} collective-permute-done((bf16[2,32,768]{2,1,0:T(8,128)(2,1)S(1)}, bf16[2,32,768]{2,1,0:T(8,128)(2,1)S(1)}, u32[]{:S(2)}, u32[]{:S(2)}) %collective-permute-start.2) | collective-permute-done | bytes 98336 | tf_op jit(solution)/shard_map/ppermute | solution.py:53
  11.2 1.0 %collective-permute-done.3.refs_3_ = bf16[2,32,768]{2,1,0:T(8,128)(2,1)S(1)} collective-permute-done((bf16[2,32,768]{2,1,0:T(8,128)(2,1)S(1)}, bf16[2,32,768]{2,1,0:T(8,128)(2,1)S(1)}, u32[]{:S(2)}, u32[]{:S(2)}) %collective-permute-start.3) | collective-permute-done | bytes 98336 | tf_op jit(solution)/shard_map/ppermute | solution.py:53
  12.2 0.2 turn.1
  12.4 0.1 collective-permute-start.4
  12.5 1.6 %collective-permute-start.7 = (bf16[42,32,128]{2,1,0:T(8,128)(2,1)S(1)}, bf16[42,32,128]{2,1,0:T(8,128)(2,1)S(1)}, u32[]{:S(2)}, u32[]{:S(2)}) collective-permute-start(bf16[42,32,128]{2,1,0:T(8,128)(2,1)S(1)} %bitcast.24), channel_id=1, source_target_pairs={{0,1},{1,2},{2,3},{3,7},{4,0},{5,4},{6,5},{7,6},{8,9},{9,10},{10,1... | collective-permute-start | bytes 1032200 | tf_op jit(solution)/shard_map/ppermute | solution.py:61
  14.1 0.0 collective-permute-done.4
  14.1 1.6 %collective-permute-start.5 = (bf16[42,32,128]{2,1,0:T(8,128)(2,1)S(1)}, bf16[42,32,128]{2,1,0:T(8,128)(2,1)S(1)}, u32[]{:S(2)}, u32[]{:S(2)}) collective-permute-start(bf16[42,32,128]{2,1,0:T(8,128)(2,1)S(1)} %collective-permute-done.4), channel_id=1, source_target_pairs={{0,1},{1,2},{2,3},{3,7},{4,0},{5,4},{6,5},{7,6},{8,9},{9,10},{10,1... | collective-permute-start | bytes 1032200 | tf_op jit(solution)/shard_map/ppermute | solution.py:61
  15.7 1.6 %collective-permute-start.10 = (bf16[128,512]{1,0:T(8,128)(2,1)S(1)}, bf16[128,512]{1,0:T(8,128)(2,1)S(1)}, u32[]{:S(2)}, u32[]{:S(2)}) collective-permute-start(bf16[128,512]{1,0:T(8,128)(2,1)S(1)} %hold.1.refs_0_), channel_id=1, source_target_pairs={{0,16},{4,20},{8,24},{12,28},{16,0},{20,4},{24,8},{28,12},{1,17},{... | collective-permute-start | bytes 393224 | tf_op jit(solution)/shard_map/ppermute | solution.py:53
  17.2 1.2 %collective-permute-start.11 = (bf16[128,512]{1,0:T(8,128)(2,1)S(1)}, bf16[128,512]{1,0:T(8,128)(2,1)S(1)}, u32[]{:S(2)}, u32[]{:S(2)}) collective-permute-start(bf16[128,512]{1,0:T(8,128)(2,1)S(1)} %hold.1.refs_0_), channel_id=1, source_target_pairs={{0,24},{4,28},{8,16},{12,20},{16,8},{20,12},{24,0},{28,4},{1,25},{... | collective-permute-start | bytes 393224 | tf_op jit(solution)/shard_map/ppermute | solution.py:53
  18.4 0.8 %collective-permute-start.9 = (bf16[128,512]{1,0:T(8,128)(2,1)S(1)}, bf16[128,512]{1,0:T(8,128)(2,1)S(1)}, u32[]{:S(2)}, u32[]{:S(2)}) collective-permute-start(bf16[128,512]{1,0:T(8,128)(2,1)S(1)} %hold.1.refs_0_), channel_id=1, source_target_pairs={{0,8},{4,12},{8,0},{12,4},{16,24},{20,28},{24,16},{28,20},{1,9},{5... | collective-permute-start | bytes 393224 | tf_op jit(solution)/shard_map/ppermute | solution.py:53
  19.2 0.0 collective-permute-done.7.received_ref
  19.3 2.1 %collective-permute-start.14 = (bf16[42,32,128]{2,1,0:T(8,128)(2,1)S(1)}, bf16[42,32,128]{2,1,0:T(8,128)(2,1)S(1)}, u32[]{:S(2)}, u32[]{:S(2)}) collective-permute-start(bf16[42,32,128]{2,1,0:T(8,128)(2,1)S(1)} %passed.8), channel_id=1, source_target_pairs={{0,1},{1,2},{2,3},{3,7},{4,0},{5,4},{6,5},{7,6},{8,9},{9,10},{10,1... | collective-permute-start | bytes 1032200 | tf_op jit(solution)/shard_map/ppermute | solution.py:61
  21.4 1.1 %collective-permute-done.10.refs_2_ = bf16[128,512]{1,0:T(8,128)(2,1)S(1)} collective-permute-done((bf16[128,512]{1,0:T(8,128)(2,1)S(1)}, bf16[128,512]{1,0:T(8,128)(2,1)S(1)}, u32[]{:S(2)}, u32[]{:S(2)}) %collective-permute-start.10) | collective-permute-done | bytes 131104 | tf_op jit(solution)/shard_map/ppermute | solution.py:53
  22.5 1.2 %collective-permute-done.11.refs_3_ = bf16[128,512]{1,0:T(8,128)(2,1)S(1)} collective-permute-done((bf16[128,512]{1,0:T(8,128)(2,1)S(1)}, bf16[128,512]{1,0:T(8,128)(2,1)S(1)}, u32[]{:S(2)}, u32[]{:S(2)}) %collective-permute-start.11) | collective-permute-done | bytes 131104 | tf_op jit(solution)/shard_map/ppermute | solution.py:53
  23.7 0.5 %collective-permute-done.9.refs_1_ = bf16[128,512]{1,0:T(8,128)(2,1)S(1)} collective-permute-done((bf16[128,512]{1,0:T(8,128)(2,1)S(1)}, bf16[128,512]{1,0:T(8,128)(2,1)S(1)}, u32[]{:S(2)}, u32[]{:S(2)}) %collective-permute-start.9) | collective-permute-done | bytes 131104 | tf_op jit(solution)/shard_map/ppermute | solution.py:53
  24.2 0.1 collective-permute-start.12
  24.3 0.1 passed.6
  24.3 1.4 %collective-permute-start.6 = (bf16[42,32,128]{2,1,0:T(8,128)(2,1)S(1)}, bf16[42,32,128]{2,1,0:T(8,128)(2,1)S(1)}, u32[]{:S(2)}, u32[]{:S(2)}) collective-permute-start(bf16[42,32,128]{2,1,0:T(8,128)(2,1)S(1)} %passed.6), channel_id=1, source_target_pairs={{0,1},{1,2},{2,3},{3,7},{4,0},{5,4},{6,5},{7,6},{8,9},{9,10},{10,1... | collective-permute-start | bytes 1032200 | tf_op jit(solution)/shard_map/ppermute | solution.py:61
  25.8 0.1 collective-permute-start.8
  25.9 0.3 collective-permute-done.14.received_ref
  26.2 2.5 %collective-permute-start.17 = (bf16[42,32,128]{2,1,0:T(8,128)(2,1)S(1)}, bf16[42,32,128]{2,1,0:T(8,128)(2,1)S(1)}, u32[]{:S(2)}, u32[]{:S(2)}) collective-permute-start(bf16[42,32,128]{2,1,0:T(8,128)(2,1)S(1)} %passed.10), channel_id=1, source_target_pairs={{0,1},{1,2},{2,3},{3,7},{4,0},{5,4},{6,5},{7,6},{8,9},{9,10},{10,1... | collective-permute-start | bytes 1032200 | tf_op jit(solution)/shard_map/ppermute | solution.py:61
  28.8 0.0 collective-permute-done.12.refs_1_
  28.8 1.7 %collective-permute-done.6.received_ref.refs_0_ = bf16[42,32,128]{2,1,0:T(8,128)(2,1)S(1)} collective-permute-done((bf16[42,32,128]{2,1,0:T(8,128)(2,1)S(1)}, bf16[42,32,128]{2,1,0:T(8,128)(2,1)S(1)}, u32[]{:S(2)}, u32[]{:S(2)}) %collective-permute-start.6) | collective-permute-done | bytes 344096 | tf_op jit(solution)/shard_map/ppermute | solution.py:61
  30.5 0.0 collective-permute-done.8.refs_0_.refs_10_
  30.6 2.6 %collective-permute-start.13 = (bf16[42,32,128]{2,1,0:T(8,128)(2,1)S(1)}, bf16[42,32,128]{2,1,0:T(8,128)(2,1)S(1)}, u32[]{:S(2)}, u32[]{:S(2)}) collective-permute-start(bf16[42,32,128]{2,1,0:T(8,128)(2,1)S(1)} %passed.7), channel_id=1, source_target_pairs={{0,1},{1,2},{2,3},{3,7},{4,0},{5,4},{6,5},{7,6},{8,9},{9,10},{10,1... | collective-permute-start | bytes 1032200 | tf_op jit(solution)/shard_map/ppermute | solution.py:61
  33.1 0.1 collective-permute-start.15
  33.2 1.0 %collective-permute-done.17.received_ref = bf16[42,32,128]{2,1,0:T(8,128)(2,1)S(1)} collective-permute-done((bf16[42,32,128]{2,1,0:T(8,128)(2,1)S(1)}, bf16[42,32,128]{2,1,0:T(8,128)(2,1)S(1)}, u32[]{:S(2)}, u32[]{:S(2)}) %collective-permute-start.17) | collective-permute-done | bytes 344096 | tf_op jit(solution)/shard_map/ppermute | solution.py:61
  34.2 2.5 %collective-permute-start.19 = (bf16[42,32,128]{2,1,0:T(8,128)(2,1)S(1)}, bf16[42,32,128]{2,1,0:T(8,128)(2,1)S(1)}, u32[]{:S(2)}, u32[]{:S(2)}) collective-permute-start(bf16[42,32,128]{2,1,0:T(8,128)(2,1)S(1)} %passed.11), channel_id=1, source_target_pairs={{0,1},{1,2},{2,3},{3,7},{4,0},{5,4},{6,5},{7,6},{8,9},{9,10},{10,1... | collective-permute-start | bytes 1032200 | tf_op jit(solution)/shard_map/ppermute | solution.py:61
  36.8 1.1 %collective-permute-done.13.received_ref = bf16[42,32,128]{2,1,0:T(8,128)(2,1)S(1)} collective-permute-done((bf16[42,32,128]{2,1,0:T(8,128)(2,1)S(1)}, bf16[42,32,128]{2,1,0:T(8,128)(2,1)S(1)}, u32[]{:S(2)}, u32[]{:S(2)}) %collective-permute-start.13) | collective-permute-done | bytes 344096 | tf_op jit(solution)/shard_map/ppermute | solution.py:61
  37.9 0.4 collective-permute-start.18
  38.4 0.0 collective-permute-done.15.refs_0_.refs_11_
  38.4 2.2 %collective-permute-start.16 = (bf16[42,32,128]{2,1,0:T(8,128)(2,1)S(1)}, bf16[42,32,128]{2,1,0:T(8,128)(2,1)S(1)}, u32[]{:S(2)}, u32[]{:S(2)}) collective-permute-start(bf16[42,32,128]{2,1,0:T(8,128)(2,1)S(1)} %passed.9), channel_id=1, source_target_pairs={{0,1},{1,2},{2,3},{3,7},{4,0},{5,4},{6,5},{7,6},{8,9},{9,10},{10,1... | collective-permute-start | bytes 1032200 | tf_op jit(solution)/shard_map/ppermute | solution.py:61
  40.6 0.9 %collective-permute-done.19 = bf16[42,32,128]{2,1,0:T(8,128)(2,1)S(1)} collective-permute-done((bf16[42,32,128]{2,1,0:T(8,128)(2,1)S(1)}, bf16[42,32,128]{2,1,0:T(8,128)(2,1)S(1)}, u32[]{:S(2)}, u32[]{:S(2)}) %collective-permute-start.19) | collective-permute-done | bytes 344096 | tf_op jit(solution)/shard_map/ppermute | solution.py:61
  41.6 0.4 collective-permute-start.20
  42.0 0.0 collective-permute-done.18.refs_12_
  42.0 2.4 %weights.1 = (f32[672,512]{1,0:T(8,128)}, f32[8,128]{1,0:T(8,128)S(1)}) custom-call(bf16[4,128,512]{2,1,0:T(8,128)(2,1)S(1)} %stack.1.refs_0_, bf16[4,128,512]{2,1,0:T(8,128)(2,1)S(1)} %collective-permute-done.12.refs_1_, bf16[2,21,32,128]{3,2,1,0:T(8,128)(2,1)S(1)} %bitcast.25, bf16[2,21,32,128]{3,2,1,0:T(8,128)(2,1)S(1)} %bitcast.22, ...), custom_call_target="tpu_custom_call" | custom-call | flops 704643072 | bytes 1376256 | tf_op jit(solution)/shard_map/weights/pallas_call | solution.py:253
  44.4 1.0 %collective-permute-done.16.mine_ref = bf16[42,32,128]{2,1,0:T(8,128)(2,1)S(1)} collective-permute-done((bf16[42,32,128]{2,1,0:T(8,128)(2,1)S(1)}, bf16[42,32,128]{2,1,0:T(8,128)(2,1)S(1)}, u32[]{:S(2)}, u32[]{:S(2)}) %collective-permute-start.16) | collective-permute-done | bytes 344096 | tf_op jit(solution)/shard_map/ppermute | solution.py:61
  45.4 0.1 half.1.half_ref
  45.5 0.0 collective-permute-done.20.theirs_ref
  45.5 0.8 %inputs.1 = bf16[32,5376]{1,0:T(8,128)(2,1)} custom-call(f32[42,32,128]{2,1,0:T(8,128)S(1)} %half.1.half_ref, bf16[42,32,128]{2,1,0:T(8,128)(2,1)S(1)} %collective-permute-done.20.theirs_ref), custom_call_target="tpu_custom_call" | custom-call | tf_op jit(solution)/shard_map/inputs/pallas_call | solution.py:269
  (17 shorter events, 0.3 us)
Async XLA Ops:
  0.6 5.8 %copy-start.1 = (bf16[128,512]{1,0:T(8,128)(2,1)S(1)}, bf16[128,512]{1,0:T(8,128)(2,1)}, u32[]{:S(2)}) copy-start(bf16[128,512]{1,0:T(8,128)(2,1)} %x_ref.1) | copy-start | bytes 393220
  0.6 5.8 %copy-start = (bf16[5376,512]{1,0:T(8,128)(2,1)S(1)}, bf16[5376,512]{1,0:T(8,128)(2,1)}, u32[]{:S(2)}) copy-start(bf16[5376,512]{1,0:T(8,128)(2,1)} %refs_0_.1) | copy-start | bytes 16515076
  0.6 5.8 %collective-permute-start = (bf16[128,512]{1,0:T(8,128)(2,1)}, bf16[128,512]{1,0:T(8,128)(2,1)S(1)}, u32[]{:S(2)}, u32[]{:S(2)}) collective-permute-start(bf16[128,512]{1,0:T(8,128)(2,1)} %x_ref.1), channel_id=1, source_target_pairs={{0,4},{4,0},{8,12},{12,8},{16,20},{20,16},{24,28},{28,24},{1,5},{5... | collective-permute-start | bytes 393224 | tf_op jit(solution)/shard_map/ppermute | solution.py:50
  1.2 1.2 %copy-start.2 = (bf16[32,5376]{1,0:T(8,128)(2,1)S(1)}, bf16[32,5376]{1,0:T(8,128)(2,1)}, u32[]{:S(2)}) copy-start(bf16[32,5376]{1,0:T(8,128)(2,1)} %normed_ref.1) | copy-start | bytes 1032196
  2.5 7.0 %collective-permute-start.1 = (bf16[2,32,768]{2,1,0:T(8,128)(2,1)S(1)}, bf16[2,32,768]{2,1,0:T(8,128)(2,1)S(1)}, u32[]{:S(2)}, u32[]{:S(2)}) collective-permute-start(bf16[2,32,768]{2,1,0:T(8,128)(2,1)S(1)} %get-tuple-element.12), channel_id=1, source_target_pairs={{0,8},{4,12},{8,0},{12,4},{16,24},{20,28},{24,16},{28,20},{1,9},{5... | collective-permute-start | bytes 294920 | tf_op jit(solution)/shard_map/ppermute | solution.py:53
  4.9 6.3 %collective-permute-start.2 = (bf16[2,32,768]{2,1,0:T(8,128)(2,1)S(1)}, bf16[2,32,768]{2,1,0:T(8,128)(2,1)S(1)}, u32[]{:S(2)}, u32[]{:S(2)}) collective-permute-start(bf16[2,32,768]{2,1,0:T(8,128)(2,1)S(1)} %get-tuple-element.13), channel_id=1, source_target_pairs={{0,16},{4,20},{8,24},{12,28},{16,0},{20,4},{24,8},{28,12},{1,17},{... | collective-permute-start | bytes 294920 | tf_op jit(solution)/shard_map/ppermute | solution.py:53
  6.4 5.8 %collective-permute-start.3 = (bf16[2,32,768]{2,1,0:T(8,128)(2,1)S(1)}, bf16[2,32,768]{2,1,0:T(8,128)(2,1)S(1)}, u32[]{:S(2)}, u32[]{:S(2)}) collective-permute-start(bf16[2,32,768]{2,1,0:T(8,128)(2,1)S(1)} %get-tuple-element.14), channel_id=1, source_target_pairs={{0,24},{4,28},{8,16},{12,20},{16,8},{20,12},{24,0},{28,4},{1,25},{... | collective-permute-start | bytes 294920 | tf_op jit(solution)/shard_map/ppermute | solution.py:53
  12.4 1.7 %collective-permute-start.4 = (bf16[42,32,128]{2,1,0:T(8,128)(2,1)S(1)}, bf16[42,32,128]{2,1,0:T(8,128)(2,1)S(1)}, u32[]{:S(2)}, u32[]{:S(2)}) collective-permute-start(bf16[42,32,128]{2,1,0:T(8,128)(2,1)S(1)} %bitcast.23), channel_id=1, source_target_pairs={{0,4},{4,0},{8,12},{12,8},{16,20},{20,16},{24,28},{28,24},{1,5},{5... | collective-permute-start | bytes 1032200 | tf_op jit(solution)/shard_map/ppermute | solution.py:50
  12.5 6.8 %collective-permute-start.7 = (bf16[42,32,128]{2,1,0:T(8,128)(2,1)S(1)}, bf16[42,32,128]{2,1,0:T(8,128)(2,1)S(1)}, u32[]{:S(2)}, u32[]{:S(2)}) collective-permute-start(bf16[42,32,128]{2,1,0:T(8,128)(2,1)S(1)} %bitcast.24), channel_id=1, source_target_pairs={{0,1},{1,2},{2,3},{3,7},{4,0},{5,4},{6,5},{7,6},{8,9},{9,10},{10,1... | collective-permute-start | bytes 1032200 | tf_op jit(solution)/shard_map/ppermute | solution.py:61
  14.1 10.2 %collective-permute-start.5 = (bf16[42,32,128]{2,1,0:T(8,128)(2,1)S(1)}, bf16[42,32,128]{2,1,0:T(8,128)(2,1)S(1)}, u32[]{:S(2)}, u32[]{:S(2)}) collective-permute-start(bf16[42,32,128]{2,1,0:T(8,128)(2,1)S(1)} %collective-permute-done.4), channel_id=1, source_target_pairs={{0,1},{1,2},{2,3},{3,7},{4,0},{5,4},{6,5},{7,6},{8,9},{9,10},{10,1... | collective-permute-start | bytes 1032200 | tf_op jit(solution)/shard_map/ppermute | solution.py:61
  15.7 6.8 %collective-permute-start.10 = (bf16[128,512]{1,0:T(8,128)(2,1)S(1)}, bf16[128,512]{1,0:T(8,128)(2,1)S(1)}, u32[]{:S(2)}, u32[]{:S(2)}) collective-permute-start(bf16[128,512]{1,0:T(8,128)(2,1)S(1)} %hold.1.refs_0_), channel_id=1, source_target_pairs={{0,16},{4,20},{8,24},{12,28},{16,0},{20,4},{24,8},{28,12},{1,17},{... | collective-permute-start | bytes 393224 | tf_op jit(solution)/shard_map/ppermute | solution.py:53
  17.2 6.4 %collective-permute-start.11 = (bf16[128,512]{1,0:T(8,128)(2,1)S(1)}, bf16[128,512]{1,0:T(8,128)(2,1)S(1)}, u32[]{:S(2)}, u32[]{:S(2)}) collective-permute-start(bf16[128,512]{1,0:T(8,128)(2,1)S(1)} %hold.1.refs_0_), channel_id=1, source_target_pairs={{0,24},{4,28},{8,16},{12,20},{16,8},{20,12},{24,0},{28,4},{1,25},{... | collective-permute-start | bytes 393224 | tf_op jit(solution)/shard_map/ppermute | solution.py:53
  18.4 5.7 %collective-permute-start.9 = (bf16[128,512]{1,0:T(8,128)(2,1)S(1)}, bf16[128,512]{1,0:T(8,128)(2,1)S(1)}, u32[]{:S(2)}, u32[]{:S(2)}) collective-permute-start(bf16[128,512]{1,0:T(8,128)(2,1)S(1)} %hold.1.refs_0_), channel_id=1, source_target_pairs={{0,8},{4,12},{8,0},{12,4},{16,24},{20,28},{24,16},{28,20},{1,9},{5... | collective-permute-start | bytes 393224 | tf_op jit(solution)/shard_map/ppermute | solution.py:53
  19.3 6.9 %collective-permute-start.14 = (bf16[42,32,128]{2,1,0:T(8,128)(2,1)S(1)}, bf16[42,32,128]{2,1,0:T(8,128)(2,1)S(1)}, u32[]{:S(2)}, u32[]{:S(2)}) collective-permute-start(bf16[42,32,128]{2,1,0:T(8,128)(2,1)S(1)} %passed.8), channel_id=1, source_target_pairs={{0,1},{1,2},{2,3},{3,7},{4,0},{5,4},{6,5},{7,6},{8,9},{9,10},{10,1... | collective-permute-start | bytes 1032200 | tf_op jit(solution)/shard_map/ppermute | solution.py:61
  24.2 4.6 %collective-permute-start.12 = (bf16[4,128,512]{2,1,0:T(8,128)(2,1)S(1)}, bf16[4,128,512]{2,1,0:T(8,128)(2,1)S(1)}, u32[]{:S(2)}, u32[]{:S(2)}) collective-permute-start(bf16[4,128,512]{2,1,0:T(8,128)(2,1)S(1)} %stack.1.refs_0_), channel_id=1, source_target_pairs={{0,4},{4,0},{8,12},{12,8},{16,20},{20,16},{24,28},{28,24},{1,5},{5... | collective-permute-start | bytes 1572872 | tf_op jit(solution)/shard_map/ppermute | solution.py:50
  24.3 6.2 %collective-permute-start.6 = (bf16[42,32,128]{2,1,0:T(8,128)(2,1)S(1)}, bf16[42,32,128]{2,1,0:T(8,128)(2,1)S(1)}, u32[]{:S(2)}, u32[]{:S(2)}) collective-permute-start(bf16[42,32,128]{2,1,0:T(8,128)(2,1)S(1)} %passed.6), channel_id=1, source_target_pairs={{0,1},{1,2},{2,3},{3,7},{4,0},{5,4},{6,5},{7,6},{8,9},{9,10},{10,1... | collective-permute-start | bytes 1032200 | tf_op jit(solution)/shard_map/ppermute | solution.py:61
  25.8 4.7 %collective-permute-start.8 = (bf16[2,21,32,128]{3,2,1,0:T(8,128)(2,1)S(1)}, bf16[2,21,32,128]{3,2,1,0:T(8,128)(2,1)S(1)}, u32[]{:S(2)}, u32[]{:S(2)}) collective-permute-start(bf16[2,21,32,128]{3,2,1,0:T(8,128)(2,1)S(1)} %pick.3), channel_id=1, source_target_pairs={{0,4},{4,0},{8,12},{12,8},{16,20},{20,16},{24,28},{28,24},{1,5},{5... | collective-permute-start | bytes 1032200 | tf_op jit(solution)/shard_map/ppermute | solution.py:50
  26.2 8.0 %collective-permute-start.17 = (bf16[42,32,128]{2,1,0:T(8,128)(2,1)S(1)}, bf16[42,32,128]{2,1,0:T(8,128)(2,1)S(1)}, u32[]{:S(2)}, u32[]{:S(2)}) collective-permute-start(bf16[42,32,128]{2,1,0:T(8,128)(2,1)S(1)} %passed.10), channel_id=1, source_target_pairs={{0,1},{1,2},{2,3},{3,7},{4,0},{5,4},{6,5},{7,6},{8,9},{9,10},{10,1... | collective-permute-start | bytes 1032200 | tf_op jit(solution)/shard_map/ppermute | solution.py:61
  30.6 7.3 %collective-permute-start.13 = (bf16[42,32,128]{2,1,0:T(8,128)(2,1)S(1)}, bf16[42,32,128]{2,1,0:T(8,128)(2,1)S(1)}, u32[]{:S(2)}, u32[]{:S(2)}) collective-permute-start(bf16[42,32,128]{2,1,0:T(8,128)(2,1)S(1)} %passed.7), channel_id=1, source_target_pairs={{0,1},{1,2},{2,3},{3,7},{4,0},{5,4},{6,5},{7,6},{8,9},{9,10},{10,1... | collective-permute-start | bytes 1032200 | tf_op jit(solution)/shard_map/ppermute | solution.py:61
  33.1 5.2 %collective-permute-start.15 = (bf16[2,21,32,128]{3,2,1,0:T(8,128)(2,1)S(1)}, bf16[2,21,32,128]{3,2,1,0:T(8,128)(2,1)S(1)}, u32[]{:S(2)}, u32[]{:S(2)}) collective-permute-start(bf16[2,21,32,128]{3,2,1,0:T(8,128)(2,1)S(1)} %pick.4), channel_id=1, source_target_pairs={{0,4},{4,0},{8,12},{12,8},{16,20},{20,16},{24,28},{28,24},{1,5},{5... | collective-permute-start | bytes 1032200 | tf_op jit(solution)/shard_map/ppermute | solution.py:50
  34.2 7.3 %collective-permute-start.19 = (bf16[42,32,128]{2,1,0:T(8,128)(2,1)S(1)}, bf16[42,32,128]{2,1,0:T(8,128)(2,1)S(1)}, u32[]{:S(2)}, u32[]{:S(2)}) collective-permute-start(bf16[42,32,128]{2,1,0:T(8,128)(2,1)S(1)} %passed.11), channel_id=1, source_target_pairs={{0,1},{1,2},{2,3},{3,7},{4,0},{5,4},{6,5},{7,6},{8,9},{9,10},{10,1... | collective-permute-start | bytes 1032200 | tf_op jit(solution)/shard_map/ppermute | solution.py:61
  37.9 4.0 %collective-permute-start.18 = (bf16[2,21,32,128]{3,2,1,0:T(8,128)(2,1)S(1)}, bf16[2,21,32,128]{3,2,1,0:T(8,128)(2,1)S(1)}, u32[]{:S(2)}, u32[]{:S(2)}) collective-permute-start(bf16[2,21,32,128]{3,2,1,0:T(8,128)(2,1)S(1)} %pick.5), channel_id=1, source_target_pairs={{0,4},{4,0},{8,12},{12,8},{16,20},{20,16},{24,28},{28,24},{1,5},{5... | collective-permute-start | bytes 1032200 | tf_op jit(solution)/shard_map/ppermute | solution.py:50
  38.4 7.0 %collective-permute-start.16 = (bf16[42,32,128]{2,1,0:T(8,128)(2,1)S(1)}, bf16[42,32,128]{2,1,0:T(8,128)(2,1)S(1)}, u32[]{:S(2)}, u32[]{:S(2)}) collective-permute-start(bf16[42,32,128]{2,1,0:T(8,128)(2,1)S(1)} %passed.9), channel_id=1, source_target_pairs={{0,1},{1,2},{2,3},{3,7},{4,0},{5,4},{6,5},{7,6},{8,9},{9,10},{10,1... | collective-permute-start | bytes 1032200 | tf_op jit(solution)/shard_map/ppermute | solution.py:61
  41.6 3.9 %collective-permute-start.20 = (bf16[42,32,128]{2,1,0:T(8,128)(2,1)S(1)}, bf16[42,32,128]{2,1,0:T(8,128)(2,1)S(1)}, u32[]{:S(2)}, u32[]{:S(2)}) collective-permute-start(bf16[42,32,128]{2,1,0:T(8,128)(2,1)S(1)} %collective-permute-done.19), channel_id=1, source_target_pairs={{0,4},{4,0},{8,12},{12,8},{16,20},{20,16},{24,28},{28,24},{1,5},{5... | collective-permute-start | bytes 1032200 | tf_op jit(solution)/shard_map/ppermute | solution.py:50

commit v4 on v3

--- a/solution.py
+++ b/solution.py
@@ -11,7 +11,8 @@
 LIMIT = 8
 TWICE = 0
 SPLIT = 1
-COST = 10**6
+ORD = (0, 3, 1, 2)
+COST = 4 * 10**8
 BF16 = jnp.bfloat16
 F32 = jnp.float32
 LANES = 128
@@ -70,7 +71,7 @@
 
 
 def turn_kernel(plan, *refs):
-    pieces, out_ref, scratch = refs[: plan.chips], refs[-2], refs[-1]
+    pieces, out_ref, scratch = [refs[ORD.index(q)] for q in range(plan.chips)] if plan.chips == 4 else refs[: plan.chips], refs[-2], refs[-1]
     chip = lax.axis_index("dp") // 2
     per_tile = LANES // plan.rows
     for group in range(2):
@@ -148,8 +149,8 @@
     out_ref[1] = second_ref[1 - core]
 
 
-def stack_kernel(*refs):
-    for i, ref in enumerate(refs[:-1]):
+def stack_kernel(count, *refs):
+    for i, ref in enumerate(refs[:count]):
         refs[-1][i] = ref[...]
 
 
@@ -214,7 +215,7 @@
         in_specs=[VMEM] * plan.chips + [ANY], out_specs=VMEM,
         scratch_shapes=[pltpu.VMEM((plan.window, LANES), BF16)],
         compiler_params=PARAMS, name="turn",
-    )(*pieces, part_own).reshape(flat)
+    )(*([pieces[q] for q in ORD] if plan.chips == 4 else pieces), part_own).reshape(flat)
     second = plan.swap_cores(first)
 
     def passed(received, partial, slot, after):
@@ -232,17 +233,18 @@
         hold_kernel, out_shape=jax.ShapeDtypeStruct(grad_kv.shape, BF16),
         in_specs=[VMEM, ANY], out_specs=VMEM, compiler_params=PARAMS, name="hold",
     )(near_kv, part_own)
-    kv = pl.pallas_call(
-        stack_kernel, out_shape=jax.ShapeDtypeStruct((plan.chips,) + grad_kv.shape, BF16),
-        in_specs=[VMEM] * plan.chips, out_specs=VMEM, compiler_params=PARAMS, name="stack",
-    )(*[plan.to_chip(held_kv, q) if q else held_kv for q in range(plan.chips)])
-    kvs = [kv, plan.swap_cores(kv)]
     trail = [own[1], second]
     for slot in range(2, n + 1):
         got = [first.reshape(halves), second.reshape(halves)]
         own += got
         sent = [passed(first, part_other, slot, [trail[slot - 2]]), passed(second, part_own, slot, theirs[-1:] + ([kvs[1]] if slot == 3 else []))]
         first, second = plan.along(sent[0]), plan.along(sent[1])
+        if slot == 2:
+            kv = pl.pallas_call(
+                functools.partial(stack_kernel, plan.chips), out_shape=jax.ShapeDtypeStruct((plan.chips,) + grad_kv.shape, BF16),
+                in_specs=[VMEM] * plan.chips + [ANY], out_specs=VMEM, compiler_params=PARAMS, name="stack",
+            )(*[plan.to_chip(held_kv, q) if q else held_kv for q in range(plan.chips)], sent[1])
+            kvs = [kv, plan.swap_cores(kv)]
         trail.append(second)
         theirs.append(plan.swap_cores(pl.pallas_call(
             pick_kernel, out_shape=jax.ShapeDtypeStruct(halves, BF16), in_specs=[VMEM] * 2, out_specs=VMEM,

time: 46.5 us -> 46.1 us (level)
    ppermute x6, waiting for transfers between devices: 5.45 us -> 3.9 us  [to_chip(): lax.ppermute(x, 'dp', [(d, 2 * self.chip_to(d // 2, q) + d % 2) for d in...]
    ppermute x8, waiting for transfers between devices: 6.13 us -> 7.26 us  [along(): return lax.ppermute(x, ('dp', 'tensor'), pairs)]
  transfers between devices with their start and end apart: 21 -> 21, of which waited for: 11 -> 10; matrix products, arithmetic and copies ran while one was open for 0% -> 0% of each run, Pallas kernels for 13% -> 13%
where the time goes in v4:
time: 46.1 us; the launch traced here: 46 us
  starting transfers between devices  25.8 us (56%)
  waiting for transfers between devices  11.2 us (24%)
  Pallas kernels  6.89 us (15%)
  local copies, waits for them, and re-layouts  1.25 us (3%)
  between operations  0.82 us (2%)
    ppermute x8, starting transfers between devices, along(): return lax.ppermute(x, ('dp', 'tensor'), pairs)  16.5 us
    ppermute x6, starting transfers between devices, to_chip(): lax.ppermute(x, 'dp', [(d, 2 * self.chip_to(d // 2, q) + d % 2) for d in...  7.6 us
    ppermute x8, waiting for transfers between devices, along(): return lax.ppermute(x, ('dp', 'tensor'), pairs)  7.26 us
    ppermute x6, waiting for transfers between devices, to_chip(): lax.ppermute(x, 'dp', [(d, 2 * self.chip_to(d // 2, q) + d % 2) for d in...  3.9 us
    pallas_call x1, Pallas kernels, body(): pl.pallas_call(functools.partial(partial_kernel, plan), out_shape=[jax.Sh...  3.04 us
    pallas_call x1, Pallas kernels, body(): pl.pallas_call(functools.partial(weight_kernel, plan), out_shape=(jax.Sha...  2.42 us
    ppermute x7, starting transfers between devices, swap_cores(): return lax.ppermute(x, 'dp', [(d, d ^ 1) for d in range(self.n_dp)])  1.66 us
    unnamed x6, local copies, waits for them, and re-layouts  1.25 us
  transfers between devices with their start and end apart: 21, of which 10 were waited for; matrix products, arithmetic and copies ran while one was open for 0% of the time, Pallas kernels for 13%

profile of v4, /device:TPU:0, one launch (start us, length us, event | category | flops | bytes accessed | tf_op | source)
XLA Modules:
  0.0 46.0 jit_solution(2925128379235113132)
XLA Ops:
  0.6 0.5 %collective-permute-start = (bf16[128,512]{1,0:T(8,128)(2,1)}, bf16[128,512]{1,0:T(8,128)(2,1)S(1)}, u32[]{:S(2)}, u32[]{:S(2)}) collective-permute-start(bf16[128,512]{1,0:T(8,128)(2,1)} %x_ref.1), channel_id=1, source_target_pairs={{0,4},{4,0},{8,12},{12,8},{16,20},{20,16},{24,28},{28,24},{1,5},{5... | collective-permute-start | bytes 393224 | tf_op jit(solution)/shard_map/ppermute | solution.py:51
  1.2 1.2 %copy-done.2 = bf16[32,5376]{1,0:T(8,128)(2,1)S(1)} copy-done((bf16[32,5376]{1,0:T(8,128)(2,1)S(1)}, bf16[32,5376]{1,0:T(8,128)(2,1)}, u32[]{:S(2)}) %copy-start.2) | copy-done | bytes 344088
  2.5 3.4 %collective-permute-start.1 = (bf16[2,32,768]{2,1,0:T(8,128)(2,1)S(1)}, bf16[2,32,768]{2,1,0:T(8,128)(2,1)S(1)}, u32[]{:S(2)}, u32[]{:S(2)}) collective-permute-start(bf16[2,32,768]{2,1,0:T(8,128)(2,1)S(1)} %get-tuple-element.12), channel_id=1, source_target_pairs={{0,24},{4,28},{8,16},{12,20},{16,8},{20,12},{24,0},{28,4},{1,25},{... | collective-permute-start | bytes 294920 | tf_op jit(solution)/shard_map/ppermute | solution.py:54
  5.9 0.5 %collective-permute-start.2 = (bf16[2,32,768]{2,1,0:T(8,128)(2,1)S(1)}, bf16[2,32,768]{2,1,0:T(8,128)(2,1)S(1)}, u32[]{:S(2)}, u32[]{:S(2)}) collective-permute-start(bf16[2,32,768]{2,1,0:T(8,128)(2,1)S(1)} %get-tuple-element.13), channel_id=1, source_target_pairs={{0,8},{4,12},{8,0},{12,4},{16,24},{20,28},{24,16},{28,20},{1,9},{5... | collective-permute-start | bytes 294920 | tf_op jit(solution)/shard_map/ppermute | solution.py:54
  6.4 0.1 collective-permute-start.3
  6.5 0.0 collective-permute-done.other_ref
  6.5 3.0 %partials.1 = (bf16[4,42,32,128]{3,2,1,0:T(8,128)(2,1)S(1)}, bf16[4,42,32,128]{3,2,1,0:T(8,128)(2,1)S(1)}) custom-call(bf16[128,512]{1,0:T(8,128)(2,1)S(1)} %copy-done.1, bf16[128,512]{1,0:T(8,128)(2,1)S(1)} %collective-permute-done.other_ref, bf16[5376,512]{1,0:T(8,128)(2,1)S(1)} %copy-done), custom_call_target="tpu_custom_call" | custom-call | flops 1409286144 | bytes 8257536 | tf_op jit(solution)/shard_map/partials/pallas_call | solution.py:198
  9.6 0.0 collective-permute-done.1.refs_1_
  9.6 2.3 %collective-permute-done.2.refs_2_ = bf16[2,32,768]{2,1,0:T(8,128)(2,1)S(1)} collective-permute-done((bf16[2,32,768]{2,1,0:T(8,128)(2,1)S(1)}, bf16[2,32,768]{2,1,0:T(8,128)(2,1)S(1)}, u32[]{:S(2)}, u32[]{:S(2)}) %collective-permute-start.2) | collective-permute-done | bytes 98336 | tf_op jit(solution)/shard_map/ppermute | solution.py:54
  11.9 0.0 collective-permute-done.3.refs_3_
  11.9 0.2 turn.1
  12.1 0.1 collective-permute-start.4
  12.2 1.6 %collective-permute-start.7 = (bf16[42,32,128]{2,1,0:T(8,128)(2,1)S(1)}, bf16[42,32,128]{2,1,0:T(8,128)(2,1)S(1)}, u32[]{:S(2)}, u32[]{:S(2)}) collective-permute-start(bf16[42,32,128]{2,1,0:T(8,128)(2,1)S(1)} %bitcast.24), channel_id=1, source_target_pairs={{0,1},{1,2},{2,3},{3,7},{4,0},{5,4},{6,5},{7,6},{8,9},{9,10},{10,1... | collective-permute-start | bytes 1032200 | tf_op jit(solution)/shard_map/ppermute | solution.py:62
  13.8 0.0 collective-permute-done.4
  13.8 1.6 %collective-permute-start.5 = (bf16[42,32,128]{2,1,0:T(8,128)(2,1)S(1)}, bf16[42,32,128]{2,1,0:T(8,128)(2,1)S(1)}, u32[]{:S(2)}, u32[]{:S(2)}) collective-permute-start(bf16[42,32,128]{2,1,0:T(8,128)(2,1)S(1)} %collective-permute-done.4), channel_id=1, source_target_pairs={{0,1},{1,2},{2,3},{3,7},{4,0},{5,4},{6,5},{7,6},{8,9},{9,10},{10,1... | collective-permute-start | bytes 1032200 | tf_op jit(solution)/shard_map/ppermute | solution.py:62
  15.4 1.5 %collective-permute-start.10 = (bf16[128,512]{1,0:T(8,128)(2,1)S(1)}, bf16[128,512]{1,0:T(8,128)(2,1)S(1)}, u32[]{:S(2)}, u32[]{:S(2)}) collective-permute-start(bf16[128,512]{1,0:T(8,128)(2,1)S(1)} %hold.1.refs_0_), channel_id=1, source_target_pairs={{0,16},{4,20},{8,24},{12,28},{16,0},{20,4},{24,8},{28,12},{1,17},{... | collective-permute-start | bytes 393224 | tf_op jit(solution)/shard_map/ppermute | solution.py:54
  16.9 1.5 %collective-permute-start.11 = (bf16[128,512]{1,0:T(8,128)(2,1)S(1)}, bf16[128,512]{1,0:T(8,128)(2,1)S(1)}, u32[]{:S(2)}, u32[]{:S(2)}) collective-permute-start(bf16[128,512]{1,0:T(8,128)(2,1)S(1)} %hold.1.refs_0_), channel_id=1, source_target_pairs={{0,24},{4,28},{8,16},{12,20},{16,8},{20,12},{24,0},{28,4},{1,25},{... | collective-permute-start | bytes 393224 | tf_op jit(solution)/shard_map/ppermute | solution.py:54
  18.4 0.5 %collective-permute-start.9 = (bf16[128,512]{1,0:T(8,128)(2,1)S(1)}, bf16[128,512]{1,0:T(8,128)(2,1)S(1)}, u32[]{:S(2)}, u32[]{:S(2)}) collective-permute-start(bf16[128,512]{1,0:T(8,128)(2,1)S(1)} %hold.1.refs_0_), channel_id=1, source_target_pairs={{0,8},{4,12},{8,0},{12,4},{16,24},{20,28},{24,16},{28,20},{1,9},{5... | collective-permute-start | bytes 393224 | tf_op jit(solution)/shard_map/ppermute | solution.py:54
  18.9 0.0 collective-permute-done.7.received_ref
  19.0 2.1 %collective-permute-start.14 = (bf16[42,32,128]{2,1,0:T(8,128)(2,1)S(1)}, bf16[42,32,128]{2,1,0:T(8,128)(2,1)S(1)}, u32[]{:S(2)}, u32[]{:S(2)}) collective-permute-start(bf16[42,32,128]{2,1,0:T(8,128)(2,1)S(1)} %passed.8), channel_id=1, source_target_pairs={{0,1},{1,2},{2,3},{3,7},{4,0},{5,4},{6,5},{7,6},{8,9},{9,10},{10,1... | collective-permute-start | bytes 1032200 | tf_op jit(solution)/shard_map/ppermute | solution.py:62
  21.1 1.1 %collective-permute-done.5.received_ref.refs_0_ = bf16[42,32,128]{2,1,0:T(8,128)(2,1)S(1)} collective-permute-done((bf16[42,32,128]{2,1,0:T(8,128)(2,1)S(1)}, bf16[42,32,128]{2,1,0:T(8,128)(2,1)S(1)}, u32[]{:S(2)}, u32[]{:S(2)}) %collective-permute-start.5) | collective-permute-done | bytes 344096 | tf_op jit(solution)/shard_map/ppermute | solution.py:62
  22.2 0.0 collective-permute-done.10.refs_2_
  22.3 1.1 %collective-permute-done.11.refs_3_ = bf16[128,512]{1,0:T(8,128)(2,1)S(1)} collective-permute-done((bf16[128,512]{1,0:T(8,128)(2,1)S(1)}, bf16[128,512]{1,0:T(8,128)(2,1)S(1)}, u32[]{:S(2)}, u32[]{:S(2)}) %collective-permute-start.11) | collective-permute-done | bytes 131104 | tf_op jit(solution)/shard_map/ppermute | solution.py:54
  23.3 0.5 %collective-permute-done.9.refs_1_ = bf16[128,512]{1,0:T(8,128)(2,1)S(1)} collective-permute-done((bf16[128,512]{1,0:T(8,128)(2,1)S(1)}, bf16[128,512]{1,0:T(8,128)(2,1)S(1)}, u32[]{:S(2)}, u32[]{:S(2)}) %collective-permute-start.9) | collective-permute-done | bytes 131104 | tf_op jit(solution)/shard_map/ppermute | solution.py:54
  23.9 0.1 collective-permute-start.12
  23.9 1.4 %collective-permute-start.6 = (bf16[42,32,128]{2,1,0:T(8,128)(2,1)S(1)}, bf16[42,32,128]{2,1,0:T(8,128)(2,1)S(1)}, u32[]{:S(2)}, u32[]{:S(2)}) collective-permute-start(bf16[42,32,128]{2,1,0:T(8,128)(2,1)S(1)} %passed.6.refs_4_), channel_id=1, source_target_pairs={{0,1},{1,2},{2,3},{3,7},{4,0},{5,4},{6,5},{7,6},{8,9},{9,10},{10,1... | collective-permute-start | bytes 1032200 | tf_op jit(solution)/shard_map/ppermute | solution.py:62
  25.4 0.1 collective-permute-start.8
  25.5 0.4 collective-permute-done.14.received_ref
  25.9 2.5 %collective-permute-start.17 = (bf16[42,32,128]{2,1,0:T(8,128)(2,1)S(1)}, bf16[42,32,128]{2,1,0:T(8,128)(2,1)S(1)}, u32[]{:S(2)}, u32[]{:S(2)}) collective-permute-start(bf16[42,32,128]{2,1,0:T(8,128)(2,1)S(1)} %passed.10), channel_id=1, source_target_pairs={{0,1},{1,2},{2,3},{3,7},{4,0},{5,4},{6,5},{7,6},{8,9},{9,10},{10,1... | collective-permute-start | bytes 1032200 | tf_op jit(solution)/shard_map/ppermute | solution.py:62
  28.5 1.7 %collective-permute-done.6.received_ref.refs_0_ = bf16[42,32,128]{2,1,0:T(8,128)(2,1)S(1)} collective-permute-done((bf16[42,32,128]{2,1,0:T(8,128)(2,1)S(1)}, bf16[42,32,128]{2,1,0:T(8,128)(2,1)S(1)}, u32[]{:S(2)}, u32[]{:S(2)}) %collective-permute-start.6) | collective-permute-done | bytes 344096 | tf_op jit(solution)/shard_map/ppermute | solution.py:62
  30.2 0.0 collective-permute-done.8.refs_0_.refs_10_
  30.2 0.0 collective-permute-done.12.refs_1_
  30.2 2.6 %collective-permute-start.13 = (bf16[42,32,128]{2,1,0:T(8,128)(2,1)S(1)}, bf16[42,32,128]{2,1,0:T(8,128)(2,1)S(1)}, u32[]{:S(2)}, u32[]{:S(2)}) collective-permute-start(bf16[42,32,128]{2,1,0:T(8,128)(2,1)S(1)} %passed.7), channel_id=1, source_target_pairs={{0,1},{1,2},{2,3},{3,7},{4,0},{5,4},{6,5},{7,6},{8,9},{9,10},{10,1... | collective-permute-start | bytes 1032200 | tf_op jit(solution)/shard_map/ppermute | solution.py:62
  32.8 0.1 collective-permute-start.15
  32.9 1.0 %collective-permute-done.17.received_ref = bf16[42,32,128]{2,1,0:T(8,128)(2,1)S(1)} collective-permute-done((bf16[42,32,128]{2,1,0:T(8,128)(2,1)S(1)}, bf16[42,32,128]{2,1,0:T(8,128)(2,1)S(1)}, u32[]{:S(2)}, u32[]{:S(2)}) %collective-permute-start.17) | collective-permute-done | bytes 344096 | tf_op jit(solution)/shard_map/ppermute | solution.py:62
  33.9 2.5 %collective-permute-start.19 = (bf16[42,32,128]{2,1,0:T(8,128)(2,1)S(1)}, bf16[42,32,128]{2,1,0:T(8,128)(2,1)S(1)}, u32[]{:S(2)}, u32[]{:S(2)}) collective-permute-start(bf16[42,32,128]{2,1,0:T(8,128)(2,1)S(1)} %passed.11), channel_id=1, source_target_pairs={{0,1},{1,2},{2,3},{3,7},{4,0},{5,4},{6,5},{7,6},{8,9},{9,10},{10,1... | collective-permute-start | bytes 1032200 | tf_op jit(solution)/shard_map/ppermute | solution.py:62
  36.4 1.1 %collective-permute-done.13.received_ref = bf16[42,32,128]{2,1,0:T(8,128)(2,1)S(1)} collective-permute-done((bf16[42,32,128]{2,1,0:T(8,128)(2,1)S(1)}, bf16[42,32,128]{2,1,0:T(8,128)(2,1)S(1)}, u32[]{:S(2)}, u32[]{:S(2)}) %collective-permute-start.13) | collective-permute-done | bytes 344096 | tf_op jit(solution)/shard_map/ppermute | solution.py:62
  37.6 0.5 %collective-permute-start.18 = (bf16[2,21,32,128]{3,2,1,0:T(8,128)(2,1)S(1)}, bf16[2,21,32,128]{3,2,1,0:T(8,128)(2,1)S(1)}, u32[]{:S(2)}, u32[]{:S(2)}) collective-permute-start(bf16[2,21,32,128]{3,2,1,0:T(8,128)(2,1)S(1)} %pick.5), channel_id=1, source_target_pairs={{0,4},{4,0},{8,12},{12,8},{16,20},{20,16},{24,28},{28,24},{1,5},{5... | collective-permute-start | bytes 1032200 | tf_op jit(solution)/shard_map/ppermute | solution.py:51
  38.0 0.0 collective-permute-done.15.refs_0_.refs_11_
  38.0 2.2 %collective-permute-start.16 = (bf16[42,32,128]{2,1,0:T(8,128)(2,1)S(1)}, bf16[42,32,128]{2,1,0:T(8,128)(2,1)S(1)}, u32[]{:S(2)}, u32[]{:S(2)}) collective-permute-start(bf16[42,32,128]{2,1,0:T(8,128)(2,1)S(1)} %passed.9), channel_id=1, source_target_pairs={{0,1},{1,2},{2,3},{3,7},{4,0},{5,4},{6,5},{7,6},{8,9},{9,10},{10,1... | collective-permute-start | bytes 1032200 | tf_op jit(solution)/shard_map/ppermute | solution.py:62
  40.3 0.9 %collective-permute-done.19 = bf16[42,32,128]{2,1,0:T(8,128)(2,1)S(1)} collective-permute-done((bf16[42,32,128]{2,1,0:T(8,128)(2,1)S(1)}, bf16[42,32,128]{2,1,0:T(8,128)(2,1)S(1)}, u32[]{:S(2)}, u32[]{:S(2)}) %collective-permute-start.19) | collective-permute-done | bytes 344096 | tf_op jit(solution)/shard_map/ppermute | solution.py:62
  41.2 0.4 collective-permute-start.20
  41.6 0.0 collective-permute-done.18.refs_12_
  41.6 2.4 %weights.1 = (f32[672,512]{1,0:T(8,128)}, f32[8,128]{1,0:T(8,128)S(1)}) custom-call(bf16[4,128,512]{2,1,0:T(8,128)(2,1)S(1)} %stack.1.refs_0_, bf16[4,128,512]{2,1,0:T(8,128)(2,1)S(1)} %collective-permute-done.12.refs_1_, bf16[2,21,32,128]{3,2,1,0:T(8,128)(2,1)S(1)} %bitcast.25, bf16[2,21,32,128]{3,2,1,0:T(8,128)(2,1)S(1)} %bitcast.22, ...), custom_call_target="tpu_custom_call" | custom-call | flops 704643072 | bytes 1376256 | tf_op jit(solution)/shard_map/weights/pallas_call | solution.py:255
  44.0 1.0 %collective-permute-done.16.mine_ref = bf16[42,32,128]{2,1,0:T(8,128)(2,1)S(1)} collective-permute-done((bf16[42,32,128]{2,1,0:T(8,128)(2,1)S(1)}, bf16[42,32,128]{2,1,0:T(8,128)(2,1)S(1)}, u32[]{:S(2)}, u32[]{:S(2)}) %collective-permute-start.16) | collective-permute-done | bytes 344096 | tf_op jit(solution)/shard_map/ppermute | solution.py:62
  45.0 0.1 half.1.half_ref
  45.1 0.0 collective-permute-done.20.theirs_ref
  45.2 0.8 %inputs.1 = bf16[32,5376]{1,0:T(8,128)(2,1)} custom-call(f32[42,32,128]{2,1,0:T(8,128)S(1)} %half.1.half_ref, bf16[42,32,128]{2,1,0:T(8,128)(2,1)S(1)} %collective-permute-done.20.theirs_ref), custom_call_target="tpu_custom_call" | custom-call | tf_op jit(solution)/shard_map/inputs/pallas_call | solution.py:271
  (17 shorter events, 0.3 us)
Async XLA Ops:
  0.6 5.9 %copy-start.1 = (bf16[128,512]{1,0:T(8,128)(2,1)S(1)}, bf16[128,512]{1,0:T(8,128)(2,1)}, u32[]{:S(2)}) copy-start(bf16[128,512]{1,0:T(8,128)(2,1)} %x_ref.1) | copy-start | bytes 393220
  0.6 5.9 %copy-start = (bf16[5376,512]{1,0:T(8,128)(2,1)S(1)}, bf16[5376,512]{1,0:T(8,128)(2,1)}, u32[]{:S(2)}) copy-start(bf16[5376,512]{1,0:T(8,128)(2,1)} %refs_0_.1) | copy-start | bytes 16515076
  0.6 5.9 %collective-permute-start = (bf16[128,512]{1,0:T(8,128)(2,1)}, bf16[128,512]{1,0:T(8,128)(2,1)S(1)}, u32[]{:S(2)}, u32[]{:S(2)}) collective-permute-start(bf16[128,512]{1,0:T(8,128)(2,1)} %x_ref.1), channel_id=1, source_target_pairs={{0,4},{4,0},{8,12},{12,8},{16,20},{20,16},{24,28},{28,24},{1,5},{5... | collective-permute-start | bytes 393224 | tf_op jit(solution)/shard_map/ppermute | solution.py:51
  1.2 1.2 %copy-start.2 = (bf16[32,5376]{1,0:T(8,128)(2,1)S(1)}, bf16[32,5376]{1,0:T(8,128)(2,1)}, u32[]{:S(2)}) copy-start(bf16[32,5376]{1,0:T(8,128)(2,1)} %normed_ref.1) | copy-start | bytes 1032196
  2.5 7.1 %collective-permute-start.1 = (bf16[2,32,768]{2,1,0:T(8,128)(2,1)S(1)}, bf16[2,32,768]{2,1,0:T(8,128)(2,1)S(1)}, u32[]{:S(2)}, u32[]{:S(2)}) collective-permute-start(bf16[2,32,768]{2,1,0:T(8,128)(2,1)S(1)} %get-tuple-element.12), channel_id=1, source_target_pairs={{0,24},{4,28},{8,16},{12,20},{16,8},{20,12},{24,0},{28,4},{1,25},{... | collective-permute-start | bytes 294920 | tf_op jit(solution)/shard_map/ppermute | solution.py:54
  5.9 6.0 %collective-permute-start.2 = (bf16[2,32,768]{2,1,0:T(8,128)(2,1)S(1)}, bf16[2,32,768]{2,1,0:T(8,128)(2,1)S(1)}, u32[]{:S(2)}, u32[]{:S(2)}) collective-permute-start(bf16[2,32,768]{2,1,0:T(8,128)(2,1)S(1)} %get-tuple-element.13), channel_id=1, source_target_pairs={{0,8},{4,12},{8,0},{12,4},{16,24},{20,28},{24,16},{28,20},{1,9},{5... | collective-permute-start | bytes 294920 | tf_op jit(solution)/shard_map/ppermute | solution.py:54
  6.4 5.5 %collective-permute-start.3 = (bf16[2,32,768]{2,1,0:T(8,128)(2,1)S(1)}, bf16[2,32,768]{2,1,0:T(8,128)(2,1)S(1)}, u32[]{:S(2)}, u32[]{:S(2)}) collective-permute-start(bf16[2,32,768]{2,1,0:T(8,128)(2,1)S(1)} %get-tuple-element.14), channel_id=1, source_target_pairs={{0,16},{4,20},{8,24},{12,28},{16,0},{20,4},{24,8},{28,12},{1,17},{... | collective-permute-start | bytes 294920 | tf_op jit(solution)/shard_map/ppermute | solution.py:54
  12.1 1.7 %collective-permute-start.4 = (bf16[42,32,128]{2,1,0:T(8,128)(2,1)S(1)}, bf16[42,32,128]{2,1,0:T(8,128)(2,1)S(1)}, u32[]{:S(2)}, u32[]{:S(2)}) collective-permute-start(bf16[42,32,128]{2,1,0:T(8,128)(2,1)S(1)} %bitcast.23), channel_id=1, source_target_pairs={{0,4},{4,0},{8,12},{12,8},{16,20},{20,16},{24,28},{28,24},{1,5},{5... | collective-permute-start | bytes 1032200 | tf_op jit(solution)/shard_map/ppermute | solution.py:51
  12.2 6.8 %collective-permute-start.7 = (bf16[42,32,128]{2,1,0:T(8,128)(2,1)S(1)}, bf16[42,32,128]{2,1,0:T(8,128)(2,1)S(1)}, u32[]{:S(2)}, u32[]{:S(2)}) collective-permute-start(bf16[42,32,128]{2,1,0:T(8,128)(2,1)S(1)} %bitcast.24), channel_id=1, source_target_pairs={{0,1},{1,2},{2,3},{3,7},{4,0},{5,4},{6,5},{7,6},{8,9},{9,10},{10,1... | collective-permute-start | bytes 1032200 | tf_op jit(solution)/shard_map/ppermute | solution.py:62
  13.8 8.4 %collective-permute-start.5 = (bf16[42,32,128]{2,1,0:T(8,128)(2,1)S(1)}, bf16[42,32,128]{2,1,0:T(8,128)(2,1)S(1)}, u32[]{:S(2)}, u32[]{:S(2)}) collective-permute-start(bf16[42,32,128]{2,1,0:T(8,128)(2,1)S(1)} %collective-permute-done.4), channel_id=1, source_target_pairs={{0,1},{1,2},{2,3},{3,7},{4,0},{5,4},{6,5},{7,6},{8,9},{9,10},{10,1... | collective-permute-start | bytes 1032200 | tf_op jit(solution)/shard_map/ppermute | solution.py:62
  15.4 6.9 %collective-permute-start.10 = (bf16[128,512]{1,0:T(8,128)(2,1)S(1)}, bf16[128,512]{1,0:T(8,128)(2,1)S(1)}, u32[]{:S(2)}, u32[]{:S(2)}) collective-permute-start(bf16[128,512]{1,0:T(8,128)(2,1)S(1)} %hold.1.refs_0_), channel_id=1, source_target_pairs={{0,16},{4,20},{8,24},{12,28},{16,0},{20,4},{24,8},{28,12},{1,17},{... | collective-permute-start | bytes 393224 | tf_op jit(solution)/shard_map/ppermute | solution.py:54
  16.9 6.4 %collective-permute-start.11 = (bf16[128,512]{1,0:T(8,128)(2,1)S(1)}, bf16[128,512]{1,0:T(8,128)(2,1)S(1)}, u32[]{:S(2)}, u32[]{:S(2)}) collective-permute-start(bf16[128,512]{1,0:T(8,128)(2,1)S(1)} %hold.1.refs_0_), channel_id=1, source_target_pairs={{0,24},{4,28},{8,16},{12,20},{16,8},{20,12},{24,0},{28,4},{1,25},{... | collective-permute-start | bytes 393224 | tf_op jit(solution)/shard_map/ppermute | solution.py:54
  18.4 5.4 %collective-permute-start.9 = (bf16[128,512]{1,0:T(8,128)(2,1)S(1)}, bf16[128,512]{1,0:T(8,128)(2,1)S(1)}, u32[]{:S(2)}, u32[]{:S(2)}) collective-permute-start(bf16[128,512]{1,0:T(8,128)(2,1)S(1)} %hold.1.refs_0_), channel_id=1, source_target_pairs={{0,8},{4,12},{8,0},{12,4},{16,24},{20,28},{24,16},{28,20},{1,9},{5... | collective-permute-start | bytes 393224 | tf_op jit(solution)/shard_map/ppermute | solution.py:54
  19.0 6.9 %collective-permute-start.14 = (bf16[42,32,128]{2,1,0:T(8,128)(2,1)S(1)}, bf16[42,32,128]{2,1,0:T(8,128)(2,1)S(1)}, u32[]{:S(2)}, u32[]{:S(2)}) collective-permute-start(bf16[42,32,128]{2,1,0:T(8,128)(2,1)S(1)} %passed.8), channel_id=1, source_target_pairs={{0,1},{1,2},{2,3},{3,7},{4,0},{5,4},{6,5},{7,6},{8,9},{9,10},{10,1... | collective-permute-start | bytes 1032200 | tf_op jit(solution)/shard_map/ppermute | solution.py:62
  23.9 6.3 %collective-permute-start.12 = (bf16[4,128,512]{2,1,0:T(8,128)(2,1)S(1)}, bf16[4,128,512]{2,1,0:T(8,128)(2,1)S(1)}, u32[]{:S(2)}, u32[]{:S(2)}) collective-permute-start(bf16[4,128,512]{2,1,0:T(8,128)(2,1)S(1)} %stack.1.refs_0_), channel_id=1, source_target_pairs={{0,4},{4,0},{8,12},{12,8},{16,20},{20,16},{24,28},{28,24},{1,5},{5... | collective-permute-start | bytes 1572872 | tf_op jit(solution)/shard_map/ppermute | solution.py:51
  23.9 6.2 %collective-permute-start.6 = (bf16[42,32,128]{2,1,0:T(8,128)(2,1)S(1)}, bf16[42,32,128]{2,1,0:T(8,128)(2,1)S(1)}, u32[]{:S(2)}, u32[]{:S(2)}) collective-permute-start(bf16[42,32,128]{2,1,0:T(8,128)(2,1)S(1)} %passed.6.refs_4_), channel_id=1, source_target_pairs={{0,1},{1,2},{2,3},{3,7},{4,0},{5,4},{6,5},{7,6},{8,9},{9,10},{10,1... | collective-permute-start | bytes 1032200 | tf_op jit(solution)/shard_map/ppermute | solution.py:62
  25.4 4.7 %collective-permute-start.8 = (bf16[2,21,32,128]{3,2,1,0:T(8,128)(2,1)S(1)}, bf16[2,21,32,128]{3,2,1,0:T(8,128)(2,1)S(1)}, u32[]{:S(2)}, u32[]{:S(2)}) collective-permute-start(bf16[2,21,32,128]{3,2,1,0:T(8,128)(2,1)S(1)} %pick.3), channel_id=1, source_target_pairs={{0,4},{4,0},{8,12},{12,8},{16,20},{20,16},{24,28},{28,24},{1,5},{5... | collective-permute-start | bytes 1032200 | tf_op jit(solution)/shard_map/ppermute | solution.py:51
  25.9 7.9 %collective-permute-start.17 = (bf16[42,32,128]{2,1,0:T(8,128)(2,1)S(1)}, bf16[42,32,128]{2,1,0:T(8,128)(2,1)S(1)}, u32[]{:S(2)}, u32[]{:S(2)}) collective-permute-start(bf16[42,32,128]{2,1,0:T(8,128)(2,1)S(1)} %passed.10), channel_id=1, source_target_pairs={{0,1},{1,2},{2,3},{3,7},{4,0},{5,4},{6,5},{7,6},{8,9},{9,10},{10,1... | collective-permute-start | bytes 1032200 | tf_op jit(solution)/shard_map/ppermute | solution.py:62
  30.2 7.3 %collective-permute-start.13 = (bf16[42,32,128]{2,1,0:T(8,128)(2,1)S(1)}, bf16[42,32,128]{2,1,0:T(8,128)(2,1)S(1)}, u32[]{:S(2)}, u32[]{:S(2)}) collective-permute-start(bf16[42,32,128]{2,1,0:T(8,128)(2,1)S(1)} %passed.7), channel_id=1, source_target_pairs={{0,1},{1,2},{2,3},{3,7},{4,0},{5,4},{6,5},{7,6},{8,9},{9,10},{10,1... | collective-permute-start | bytes 1032200 | tf_op jit(solution)/shard_map/ppermute | solution.py:62
  32.8 5.2 %collective-permute-start.15 = (bf16[2,21,32,128]{3,2,1,0:T(8,128)(2,1)S(1)}, bf16[2,21,32,128]{3,2,1,0:T(8,128)(2,1)S(1)}, u32[]{:S(2)}, u32[]{:S(2)}) collective-permute-start(bf16[2,21,32,128]{3,2,1,0:T(8,128)(2,1)S(1)} %pick.4), channel_id=1, source_target_pairs={{0,4},{4,0},{8,12},{12,8},{16,20},{20,16},{24,28},{28,24},{1,5},{5... | collective-permute-start | bytes 1032200 | tf_op jit(solution)/shard_map/ppermute | solution.py:51
  33.9 7.3 %collective-permute-start.19 = (bf16[42,32,128]{2,1,0:T(8,128)(2,1)S(1)}, bf16[42,32,128]{2,1,0:T(8,128)(2,1)S(1)}, u32[]{:S(2)}, u32[]{:S(2)}) collective-permute-start(bf16[42,32,128]{2,1,0:T(8,128)(2,1)S(1)} %passed.11), channel_id=1, source_target_pairs={{0,1},{1,2},{2,3},{3,7},{4,0},{5,4},{6,5},{7,6},{8,9},{9,10},{10,1... | collective-permute-start | bytes 1032200 | tf_op jit(solution)/shard_map/ppermute | solution.py:62
  37.6 4.1 %collective-permute-start.18 = (bf16[2,21,32,128]{3,2,1,0:T(8,128)(2,1)S(1)}, bf16[2,21,32,128]{3,2,1,0:T(8,128)(2,1)S(1)}, u32[]{:S(2)}, u32[]{:S(2)}) collective-permute-start(bf16[2,21,32,128]{3,2,1,0:T(8,128)(2,1)S(1)} %pick.5), channel_id=1, source_target_pairs={{0,4},{4,0},{8,12},{12,8},{16,20},{20,16},{24,28},{28,24},{1,5},{5... | collective-permute-start | bytes 1032200 | tf_op jit(solution)/shard_map/ppermute | solution.py:51
  38.0 7.0 %collective-permute-start.16 = (bf16[42,32,128]{2,1,0:T(8,128)(2,1)S(1)}, bf16[42,32,128]{2,1,0:T(8,128)(2,1)S(1)}, u32[]{:S(2)}, u32[]{:S(2)}) collective-permute-start(bf16[42,32,128]{2,1,0:T(8,128)(2,1)S(1)} %passed.9), channel_id=1, source_target_pairs={{0,1},{1,2},{2,3},{3,7},{4,0},{5,4},{6,5},{7,6},{8,9},{9,10},{10,1... | collective-permute-start | bytes 1032200 | tf_op jit(solution)/shard_map/ppermute | solution.py:62
  41.2 3.9 %collective-permute-start.20 = (bf16[42,32,128]{2,1,0:T(8,128)(2,1)S(1)}, bf16[42,32,128]{2,1,0:T(8,128)(2,1)S(1)}, u32[]{:S(2)}, u32[]{:S(2)}) collective-permute-start(bf16[42,32,128]{2,1,0:T(8,128)(2,1)S(1)} %collective-permute-done.19), channel_id=1, source_target_pairs={{0,4},{4,0},{8,12},{12,8},{16,20},{20,16},{24,28},{28,24},{1,5},{5... | collective-permute-start | bytes 1032200 | tf_op jit(solution)/shard_map/ppermute | solution.py:51

commit v5 on v4

--- a/solution.py
+++ b/solution.py
@@ -31,8 +31,8 @@
         self.tokens = self.rows * self.n_dp
         self.tiles = self.feats // LANES
         self.half_tiles = self.tokens // 2 // LANES
-        starts = [self.width * d // LANES * LANES for d in range(self.n_dp)]
-        ends = [self.width * d - s + self.width for d, s in enumerate(starts)]
+        pair = 2 * self.width
+        ends = [pair * m % LANES + pair for m in range(self.chips)]
         self.window = -(-max(ends) // LANES) * LANES
         self.step = math.gcd(self.width, LANES)
         self.power = self.chips & (self.chips - 1) == 0
@@ -43,8 +43,8 @@
     def chip_from(self, chip, q):
         return chip ^ q if self.power else lax.rem(chip + self.chips - q, self.chips)
 
-    def start_of(self, d):
-        exact = d * self.width
+    def start_of(self, chip):
+        exact = 2 * chip * self.width
         return jnp.minimum(exact // LANES * LANES, self.feats - self.window)
 
     def swap_cores(self, x):
@@ -65,21 +65,20 @@
 def split_kernel(plan, normed_ref, *out_refs):
     chip = lax.axis_index("dp") // 2
     for q, out_ref in enumerate(out_refs):
-        for group in range(2):
-            start = pl.multiple_of(plan.start_of(2 * plan.chip_to(chip, q) + group), LANES)
-            out_ref[group] = normed_ref[:, pl.ds(start, plan.window)]
+        start = pl.multiple_of(plan.start_of(plan.chip_to(chip, q)), LANES)
+        out_ref[...] = normed_ref[:, pl.ds(start, plan.window)]
 
 
 def turn_kernel(plan, *refs):
     pieces, out_ref, scratch = [refs[ORD.index(q)] for q in range(plan.chips)] if plan.chips == 4 else refs[: plan.chips], refs[-2], refs[-1]
     chip = lax.axis_index("dp") // 2
     per_tile = LANES // plan.rows
-    for group in range(2):
-        d = 2 * chip + group
-        offset = pl.multiple_of(d * plan.width - plan.start_of(d), plan.step)
-        for j in range(plan.half_tiles):
-            tile = jnp.concatenate([ref[group] for ref in pieces[j * per_tile : (j + 1) * per_tile]], axis=0)
-            scratch[...] = tile.T
+    begin = 2 * chip * plan.width - plan.start_of(chip)
+    for j in range(plan.half_tiles):
+        tile = jnp.concatenate([ref[...] for ref in pieces[j * per_tile : (j + 1) * per_tile]], axis=0)
+        scratch[...] = tile.T
+        for group in range(2):
+            offset = pl.multiple_of(begin + group * plan.width, plan.step)
             out_ref[group, j] = scratch[pl.ds(offset, plan.width), :]
 
 
@@ -186,7 +185,7 @@
     near_kv = plan.swap_cores(other_kv) if TWICE else grad_kv
     pieces = pl.pallas_call(
         functools.partial(split_kernel, plan),
-        out_shape=[jax.ShapeDtypeStruct((2, plan.rows, plan.window), BF16)] * plan.chips,
+        out_shape=[jax.ShapeDtypeStruct((plan.rows, plan.window), BF16)] * plan.chips,
         in_specs=[VMEM], out_specs=[VMEM] * plan.chips, compiler_params=PARAMS, name="split",
         cost_estimate=pl.CostEstimate(flops=6 * 10**9, bytes_accessed=0, transcendentals=0),
     )(normed)

time: 46.1 us -> 45.8 us (level)
  no operation moved by 1% of the time
where the time goes in v5:
time: 45.8 us; the launch traced here: 45.6 us
  starting transfers between devices  25.8 us (56%)
  waiting for transfers between devices  10.9 us (24%)
  Pallas kernels  6.88 us (15%)
  local copies, waits for them, and re-layouts  1.25 us (3%)
  between operations  0.81 us (2%)
    ppermute x8, starting transfers between devices, along(): return lax.ppermute(x, ('dp', 'tensor'), pairs)  16.5 us
    ppermute x6, starting transfers between devices, to_chip(): lax.ppermute(x, 'dp', [(d, 2 * self.chip_to(d // 2, q) + d % 2) for d in...  7.6 us
    ppermute x8, waiting for transfers between devices, along(): return lax.ppermute(x, ('dp', 'tensor'), pairs)  7.26 us
    ppermute x6, waiting for transfers between devices, to_chip(): lax.ppermute(x, 'dp', [(d, 2 * self.chip_to(d // 2, q) + d % 2) for d in...  3.55 us
    pallas_call x1, Pallas kernels, body(): pl.pallas_call(functools.partial(partial_kernel, plan), out_shape=[jax.Sh...  3.04 us
    pallas_call x1, Pallas kernels, body(): pl.pallas_call(functools.partial(weight_kernel, plan), out_shape=(jax.Sha...  2.42 us
    ppermute x7, starting transfers between devices, swap_cores(): return lax.ppermute(x, 'dp', [(d, d ^ 1) for d in range(self.n_dp)])  1.66 us
    unnamed x6, local copies, waits for them, and re-layouts  1.25 us
  transfers between devices with their start and end apart: 21, of which 10 were waited for; matrix products, arithmetic and copies ran while one was open for 0% of the time, Pallas kernels for 13%

profile of v5, /device:TPU:0, one launch (start us, length us, event | category | flops | bytes accessed | tf_op | source)
XLA Modules:
  0.0 45.6 jit_solution(5098970477436335727)
XLA Ops:
  0.6 0.5 %collective-permute-start = (bf16[128,512]{1,0:T(8,128)(2,1)}, bf16[128,512]{1,0:T(8,128)(2,1)S(1)}, u32[]{:S(2)}, u32[]{:S(2)}) collective-permute-start(bf16[128,512]{1,0:T(8,128)(2,1)} %x_ref.1), channel_id=1, source_target_pairs={{0,4},{4,0},{8,12},{12,8},{16,20},{20,16},{24,28},{28,24},{1,5},{5... | collective-permute-start | bytes 393224 | tf_op jit(solution)/shard_map/ppermute | solution.py:51
  1.2 1.2 %copy-done.2 = bf16[32,5376]{1,0:T(8,128)(2,1)S(1)} copy-done((bf16[32,5376]{1,0:T(8,128)(2,1)S(1)}, bf16[32,5376]{1,0:T(8,128)(2,1)}, u32[]{:S(2)}) %copy-start.2) | copy-done | bytes 344088
  2.4 3.4 %collective-permute-start.1 = (bf16[32,1408]{1,0:T(8,128)(2,1)S(1)}, bf16[32,1408]{1,0:T(8,128)(2,1)S(1)}, u32[]{:S(2)}, u32[]{:S(2)}) collective-permute-start(bf16[32,1408]{1,0:T(8,128)(2,1)S(1)} %get-tuple-element.12), channel_id=1, source_target_pairs={{0,24},{4,28},{8,16},{12,20},{16,8},{20,12},{24,0},{28,4},{1,25},{... | collective-permute-start | bytes 270344 | tf_op jit(solution)/shard_map/ppermute | solution.py:54
  5.8 0.5 %collective-permute-start.2 = (bf16[32,1408]{1,0:T(8,128)(2,1)S(1)}, bf16[32,1408]{1,0:T(8,128)(2,1)S(1)}, u32[]{:S(2)}, u32[]{:S(2)}) collective-permute-start(bf16[32,1408]{1,0:T(8,128)(2,1)S(1)} %get-tuple-element.13), channel_id=1, source_target_pairs={{0,8},{4,12},{8,0},{12,4},{16,24},{20,28},{24,16},{28,20},{1,9},{5... | collective-permute-start | bytes 270344 | tf_op jit(solution)/shard_map/ppermute | solution.py:54
  6.4 0.1 collective-permute-start.3
  6.5 0.0 collective-permute-done.other_ref
  6.5 3.0 %partials.1 = (bf16[4,42,32,128]{3,2,1,0:T(8,128)(2,1)S(1)}, bf16[4,42,32,128]{3,2,1,0:T(8,128)(2,1)S(1)}) custom-call(bf16[128,512]{1,0:T(8,128)(2,1)S(1)} %copy-done.1, bf16[128,512]{1,0:T(8,128)(2,1)S(1)} %collective-permute-done.other_ref, bf16[5376,512]{1,0:T(8,128)(2,1)S(1)} %copy-done), custom_call_target="tpu_custom_call" | custom-call | flops 1409286144 | bytes 8257536 | tf_op jit(solution)/shard_map/partials/pallas_call | solution.py:197
  9.5 0.0 collective-permute-done.1.refs_1_
  9.6 2.0 %collective-permute-done.2.refs_2_ = bf16[32,1408]{1,0:T(8,128)(2,1)S(1)} collective-permute-done((bf16[32,1408]{1,0:T(8,128)(2,1)S(1)}, bf16[32,1408]{1,0:T(8,128)(2,1)S(1)}, u32[]{:S(2)}, u32[]{:S(2)}) %collective-permute-start.2) | collective-permute-done | bytes 90144 | tf_op jit(solution)/shard_map/ppermute | solution.py:54
  11.5 0.0 collective-permute-done.3.refs_3_
  11.5 0.2 turn.1
  11.7 0.1 collective-permute-start.4
  11.8 1.6 %collective-permute-start.7 = (bf16[42,32,128]{2,1,0:T(8,128)(2,1)S(1)}, bf16[42,32,128]{2,1,0:T(8,128)(2,1)S(1)}, u32[]{:S(2)}, u32[]{:S(2)}) collective-permute-start(bf16[42,32,128]{2,1,0:T(8,128)(2,1)S(1)} %bitcast.24), channel_id=1, source_target_pairs={{0,1},{1,2},{2,3},{3,7},{4,0},{5,4},{6,5},{7,6},{8,9},{9,10},{10,1... | collective-permute-start | bytes 1032200 | tf_op jit(solution)/shard_map/ppermute | solution.py:62
  13.4 0.0 collective-permute-done.4
  13.4 1.6 %collective-permute-start.5 = (bf16[42,32,128]{2,1,0:T(8,128)(2,1)S(1)}, bf16[42,32,128]{2,1,0:T(8,128)(2,1)S(1)}, u32[]{:S(2)}, u32[]{:S(2)}) collective-permute-start(bf16[42,32,128]{2,1,0:T(8,128)(2,1)S(1)} %collective-permute-done.4), channel_id=1, source_target_pairs={{0,1},{1,2},{2,3},{3,7},{4,0},{5,4},{6,5},{7,6},{8,9},{9,10},{10,1... | collective-permute-start | bytes 1032200 | tf_op jit(solution)/shard_map/ppermute | solution.py:62
  15.0 1.5 %collective-permute-start.10 = (bf16[128,512]{1,0:T(8,128)(2,1)S(1)}, bf16[128,512]{1,0:T(8,128)(2,1)S(1)}, u32[]{:S(2)}, u32[]{:S(2)}) collective-permute-start(bf16[128,512]{1,0:T(8,128)(2,1)S(1)} %hold.1.refs_0_), channel_id=1, source_target_pairs={{0,16},{4,20},{8,24},{12,28},{16,0},{20,4},{24,8},{28,12},{1,17},{... | collective-permute-start | bytes 393224 | tf_op jit(solution)/shard_map/ppermute | solution.py:54
  16.6 1.5 %collective-permute-start.11 = (bf16[128,512]{1,0:T(8,128)(2,1)S(1)}, bf16[128,512]{1,0:T(8,128)(2,1)S(1)}, u32[]{:S(2)}, u32[]{:S(2)}) collective-permute-start(bf16[128,512]{1,0:T(8,128)(2,1)S(1)} %hold.1.refs_0_), channel_id=1, source_target_pairs={{0,24},{4,28},{8,16},{12,20},{16,8},{20,12},{24,0},{28,4},{1,25},{... | collective-permute-start | bytes 393224 | tf_op jit(solution)/shard_map/ppermute | solution.py:54
  18.0 0.5 %collective-permute-start.9 = (bf16[128,512]{1,0:T(8,128)(2,1)S(1)}, bf16[128,512]{1,0:T(8,128)(2,1)S(1)}, u32[]{:S(2)}, u32[]{:S(2)}) collective-permute-start(bf16[128,512]{1,0:T(8,128)(2,1)S(1)} %hold.1.refs_0_), channel_id=1, source_target_pairs={{0,8},{4,12},{8,0},{12,4},{16,24},{20,28},{24,16},{28,20},{1,9},{5... | collective-permute-start | bytes 393224 | tf_op jit(solution)/shard_map/ppermute | solution.py:54
  18.6 0.0 collective-permute-done.7.received_ref
  18.6 2.1 %collective-permute-start.14 = (bf16[42,32,128]{2,1,0:T(8,128)(2,1)S(1)}, bf16[42,32,128]{2,1,0:T(8,128)(2,1)S(1)}, u32[]{:S(2)}, u32[]{:S(2)}) collective-permute-start(bf16[42,32,128]{2,1,0:T(8,128)(2,1)S(1)} %passed.8), channel_id=1, source_target_pairs={{0,1},{1,2},{2,3},{3,7},{4,0},{5,4},{6,5},{7,6},{8,9},{9,10},{10,1... | collective-permute-start | bytes 1032200 | tf_op jit(solution)/shard_map/ppermute | solution.py:62
  20.7 1.1 %collective-permute-done.5.received_ref.refs_0_ = bf16[42,32,128]{2,1,0:T(8,128)(2,1)S(1)} collective-permute-done((bf16[42,32,128]{2,1,0:T(8,128)(2,1)S(1)}, bf16[42,32,128]{2,1,0:T(8,128)(2,1)S(1)}, u32[]{:S(2)}, u32[]{:S(2)}) %collective-permute-start.5) | collective-permute-done | bytes 344096 | tf_op jit(solution)/shard_map/ppermute | solution.py:62
  21.9 0.0 collective-permute-done.10.refs_2_
  21.9 1.1 %collective-permute-done.11.refs_3_ = bf16[128,512]{1,0:T(8,128)(2,1)S(1)} collective-permute-done((bf16[128,512]{1,0:T(8,128)(2,1)S(1)}, bf16[128,512]{1,0:T(8,128)(2,1)S(1)}, u32[]{:S(2)}, u32[]{:S(2)}) %collective-permute-start.11) | collective-permute-done | bytes 131104 | tf_op jit(solution)/shard_map/ppermute | solution.py:54
  23.0 0.5 %collective-permute-done.9.refs_1_ = bf16[128,512]{1,0:T(8,128)(2,1)S(1)} collective-permute-done((bf16[128,512]{1,0:T(8,128)(2,1)S(1)}, bf16[128,512]{1,0:T(8,128)(2,1)S(1)}, u32[]{:S(2)}, u32[]{:S(2)}) %collective-permute-start.9) | collective-permute-done | bytes 131104 | tf_op jit(solution)/shard_map/ppermute | solution.py:54
  23.5 0.1 collective-permute-start.12
  23.6 1.4 %collective-permute-start.6 = (bf16[42,32,128]{2,1,0:T(8,128)(2,1)S(1)}, bf16[42,32,128]{2,1,0:T(8,128)(2,1)S(1)}, u32[]{:S(2)}, u32[]{:S(2)}) collective-permute-start(bf16[42,32,128]{2,1,0:T(8,128)(2,1)S(1)} %passed.6.refs_4_), channel_id=1, source_target_pairs={{0,1},{1,2},{2,3},{3,7},{4,0},{5,4},{6,5},{7,6},{8,9},{9,10},{10,1... | collective-permute-start | bytes 1032200 | tf_op jit(solution)/shard_map/ppermute | solution.py:62
  25.0 0.1 collective-permute-start.8
  25.1 0.4 collective-permute-done.14.received_ref
  25.6 2.5 %collective-permute-start.17 = (bf16[42,32,128]{2,1,0:T(8,128)(2,1)S(1)}, bf16[42,32,128]{2,1,0:T(8,128)(2,1)S(1)}, u32[]{:S(2)}, u32[]{:S(2)}) collective-permute-start(bf16[42,32,128]{2,1,0:T(8,128)(2,1)S(1)} %passed.10), channel_id=1, source_target_pairs={{0,1},{1,2},{2,3},{3,7},{4,0},{5,4},{6,5},{7,6},{8,9},{9,10},{10,1... | collective-permute-start | bytes 1032200 | tf_op jit(solution)/shard_map/ppermute | solution.py:62
  28.1 1.7 %collective-permute-done.6.received_ref.refs_0_ = bf16[42,32,128]{2,1,0:T(8,128)(2,1)S(1)} collective-permute-done((bf16[42,32,128]{2,1,0:T(8,128)(2,1)S(1)}, bf16[42,32,128]{2,1,0:T(8,128)(2,1)S(1)}, u32[]{:S(2)}, u32[]{:S(2)}) %collective-permute-start.6) | collective-permute-done | bytes 344096 | tf_op jit(solution)/shard_map/ppermute | solution.py:62
  29.8 0.0 collective-permute-done.8.refs_0_.refs_10_
  29.8 0.0 collective-permute-done.12.refs_1_
  29.8 2.6 %collective-permute-start.13 = (bf16[42,32,128]{2,1,0:T(8,128)(2,1)S(1)}, bf16[42,32,128]{2,1,0:T(8,128)(2,1)S(1)}, u32[]{:S(2)}, u32[]{:S(2)}) collective-permute-start(bf16[42,32,128]{2,1,0:T(8,128)(2,1)S(1)} %passed.7), channel_id=1, source_target_pairs={{0,1},{1,2},{2,3},{3,7},{4,0},{5,4},{6,5},{7,6},{8,9},{9,10},{10,1... | collective-permute-start | bytes 1032200 | tf_op jit(solution)/shard_map/ppermute | solution.py:62
  32.4 0.1 collective-permute-start.15
  32.5 1.0 %collective-permute-done.17.received_ref = bf16[42,32,128]{2,1,0:T(8,128)(2,1)S(1)} collective-permute-done((bf16[42,32,128]{2,1,0:T(8,128)(2,1)S(1)}, bf16[42,32,128]{2,1,0:T(8,128)(2,1)S(1)}, u32[]{:S(2)}, u32[]{:S(2)}) %collective-permute-start.17) | collective-permute-done | bytes 344096 | tf_op jit(solution)/shard_map/ppermute | solution.py:62
  33.5 2.5 %collective-permute-start.19 = (bf16[42,32,128]{2,1,0:T(8,128)(2,1)S(1)}, bf16[42,32,128]{2,1,0:T(8,128)(2,1)S(1)}, u32[]{:S(2)}, u32[]{:S(2)}) collective-permute-start(bf16[42,32,128]{2,1,0:T(8,128)(2,1)S(1)} %passed.11), channel_id=1, source_target_pairs={{0,1},{1,2},{2,3},{3,7},{4,0},{5,4},{6,5},{7,6},{8,9},{9,10},{10,1... | collective-permute-start | bytes 1032200 | tf_op jit(solution)/shard_map/ppermute | solution.py:62
  36.1 1.1 %collective-permute-done.13.received_ref = bf16[42,32,128]{2,1,0:T(8,128)(2,1)S(1)} collective-permute-done((bf16[42,32,128]{2,1,0:T(8,128)(2,1)S(1)}, bf16[42,32,128]{2,1,0:T(8,128)(2,1)S(1)}, u32[]{:S(2)}, u32[]{:S(2)}) %collective-permute-start.13) | collective-permute-done | bytes 344096 | tf_op jit(solution)/shard_map/ppermute | solution.py:62
  37.2 0.5 %collective-permute-start.18 = (bf16[2,21,32,128]{3,2,1,0:T(8,128)(2,1)S(1)}, bf16[2,21,32,128]{3,2,1,0:T(8,128)(2,1)S(1)}, u32[]{:S(2)}, u32[]{:S(2)}) collective-permute-start(bf16[2,21,32,128]{3,2,1,0:T(8,128)(2,1)S(1)} %pick.5), channel_id=1, source_target_pairs={{0,4},{4,0},{8,12},{12,8},{16,20},{20,16},{24,28},{28,24},{1,5},{5... | collective-permute-start | bytes 1032200 | tf_op jit(solution)/shard_map/ppermute | solution.py:51
  37.6 0.0 collective-permute-done.15.refs_0_.refs_11_
  37.7 2.2 %collective-permute-start.16 = (bf16[42,32,128]{2,1,0:T(8,128)(2,1)S(1)}, bf16[42,32,128]{2,1,0:T(8,128)(2,1)S(1)}, u32[]{:S(2)}, u32[]{:S(2)}) collective-permute-start(bf16[42,32,128]{2,1,0:T(8,128)(2,1)S(1)} %passed.9), channel_id=1, source_target_pairs={{0,1},{1,2},{2,3},{3,7},{4,0},{5,4},{6,5},{7,6},{8,9},{9,10},{10,1... | collective-permute-start | bytes 1032200 | tf_op jit(solution)/shard_map/ppermute | solution.py:62
  39.9 0.9 %collective-permute-done.19 = bf16[42,32,128]{2,1,0:T(8,128)(2,1)S(1)} collective-permute-done((bf16[42,32,128]{2,1,0:T(8,128)(2,1)S(1)}, bf16[42,32,128]{2,1,0:T(8,128)(2,1)S(1)}, u32[]{:S(2)}, u32[]{:S(2)}) %collective-permute-start.19) | collective-permute-done | bytes 344096 | tf_op jit(solution)/shard_map/ppermute | solution.py:62
  40.8 0.4 collective-permute-start.20
  41.2 0.0 collective-permute-done.18.refs_12_
  41.2 2.4 %weights.1 = (f32[672,512]{1,0:T(8,128)}, f32[8,128]{1,0:T(8,128)S(1)}) custom-call(bf16[4,128,512]{2,1,0:T(8,128)(2,1)S(1)} %stack.1.refs_0_, bf16[4,128,512]{2,1,0:T(8,128)(2,1)S(1)} %collective-permute-done.12.refs_1_, bf16[2,21,32,128]{3,2,1,0:T(8,128)(2,1)S(1)} %bitcast.25, bf16[2,21,32,128]{3,2,1,0:T(8,128)(2,1)S(1)} %bitcast.22, ...), custom_call_target="tpu_custom_call" | custom-call | flops 704643072 | bytes 1376256 | tf_op jit(solution)/shard_map/weights/pallas_call | solution.py:254
  43.7 1.0 %collective-permute-done.16.mine_ref = bf16[42,32,128]{2,1,0:T(8,128)(2,1)S(1)} collective-permute-done((bf16[42,32,128]{2,1,0:T(8,128)(2,1)S(1)}, bf16[42,32,128]{2,1,0:T(8,128)(2,1)S(1)}, u32[]{:S(2)}, u32[]{:S(2)}) %collective-permute-start.16) | collective-permute-done | bytes 344096 | tf_op jit(solution)/shard_map/ppermute | solution.py:62
  44.7 0.1 half.1.half_ref
  44.8 0.0 collective-permute-done.20.theirs_ref
  44.8 0.8 %inputs.1 = bf16[32,5376]{1,0:T(8,128)(2,1)} custom-call(f32[42,32,128]{2,1,0:T(8,128)S(1)} %half.1.half_ref, bf16[42,32,128]{2,1,0:T(8,128)(2,1)S(1)} %collective-permute-done.20.theirs_ref), custom_call_target="tpu_custom_call" | custom-call | tf_op jit(solution)/shard_map/inputs/pallas_call | solution.py:270
  (17 shorter events, 0.3 us)
Async XLA Ops:
  0.6 5.9 %copy-start.1 = (bf16[128,512]{1,0:T(8,128)(2,1)S(1)}, bf16[128,512]{1,0:T(8,128)(2,1)}, u32[]{:S(2)}) copy-start(bf16[128,512]{1,0:T(8,128)(2,1)} %x_ref.1) | copy-start | bytes 393220
  0.6 5.9 %copy-start = (bf16[5376,512]{1,0:T(8,128)(2,1)S(1)}, bf16[5376,512]{1,0:T(8,128)(2,1)}, u32[]{:S(2)}) copy-start(bf16[5376,512]{1,0:T(8,128)(2,1)} %refs_0_.1) | copy-start | bytes 16515076
  0.6 5.8 %collective-permute-start = (bf16[128,512]{1,0:T(8,128)(2,1)}, bf16[128,512]{1,0:T(8,128)(2,1)S(1)}, u32[]{:S(2)}, u32[]{:S(2)}) collective-permute-start(bf16[128,512]{1,0:T(8,128)(2,1)} %x_ref.1), channel_id=1, source_target_pairs={{0,4},{4,0},{8,12},{12,8},{16,20},{20,16},{24,28},{28,24},{1,5},{5... | collective-permute-start | bytes 393224 | tf_op jit(solution)/shard_map/ppermute | solution.py:51
  1.2 1.2 %copy-start.2 = (bf16[32,5376]{1,0:T(8,128)(2,1)S(1)}, bf16[32,5376]{1,0:T(8,128)(2,1)}, u32[]{:S(2)}) copy-start(bf16[32,5376]{1,0:T(8,128)(2,1)} %normed_ref.1) | copy-start | bytes 1032196
  2.4 7.1 %collective-permute-start.1 = (bf16[32,1408]{1,0:T(8,128)(2,1)S(1)}, bf16[32,1408]{1,0:T(8,128)(2,1)S(1)}, u32[]{:S(2)}, u32[]{:S(2)}) collective-permute-start(bf16[32,1408]{1,0:T(8,128)(2,1)S(1)} %get-tuple-element.12), channel_id=1, source_target_pairs={{0,24},{4,28},{8,16},{12,20},{16,8},{20,12},{24,0},{28,4},{1,25},{... | collective-permute-start | bytes 270344 | tf_op jit(solution)/shard_map/ppermute | solution.py:54
  5.8 5.7 %collective-permute-start.2 = (bf16[32,1408]{1,0:T(8,128)(2,1)S(1)}, bf16[32,1408]{1,0:T(8,128)(2,1)S(1)}, u32[]{:S(2)}, u32[]{:S(2)}) collective-permute-start(bf16[32,1408]{1,0:T(8,128)(2,1)S(1)} %get-tuple-element.13), channel_id=1, source_target_pairs={{0,8},{4,12},{8,0},{12,4},{16,24},{20,28},{24,16},{28,20},{1,9},{5... | collective-permute-start | bytes 270344 | tf_op jit(solution)/shard_map/ppermute | solution.py:54
  6.4 5.1 %collective-permute-start.3 = (bf16[32,1408]{1,0:T(8,128)(2,1)S(1)}, bf16[32,1408]{1,0:T(8,128)(2,1)S(1)}, u32[]{:S(2)}, u32[]{:S(2)}) collective-permute-start(bf16[32,1408]{1,0:T(8,128)(2,1)S(1)} %get-tuple-element.14), channel_id=1, source_target_pairs={{0,16},{4,20},{8,24},{12,28},{16,0},{20,4},{24,8},{28,12},{1,17},{... | collective-permute-start | bytes 270344 | tf_op jit(solution)/shard_map/ppermute | solution.py:54
  11.7 1.7 %collective-permute-start.4 = (bf16[42,32,128]{2,1,0:T(8,128)(2,1)S(1)}, bf16[42,32,128]{2,1,0:T(8,128)(2,1)S(1)}, u32[]{:S(2)}, u32[]{:S(2)}) collective-permute-start(bf16[42,32,128]{2,1,0:T(8,128)(2,1)S(1)} %bitcast.23), channel_id=1, source_target_pairs={{0,4},{4,0},{8,12},{12,8},{16,20},{20,16},{24,28},{28,24},{1,5},{5... | collective-permute-start | bytes 1032200 | tf_op jit(solution)/shard_map/ppermute | solution.py:51
  11.8 6.8 %collective-permute-start.7 = (bf16[42,32,128]{2,1,0:T(8,128)(2,1)S(1)}, bf16[42,32,128]{2,1,0:T(8,128)(2,1)S(1)}, u32[]{:S(2)}, u32[]{:S(2)}) collective-permute-start(bf16[42,32,128]{2,1,0:T(8,128)(2,1)S(1)} %bitcast.24), channel_id=1, source_target_pairs={{0,1},{1,2},{2,3},{3,7},{4,0},{5,4},{6,5},{7,6},{8,9},{9,10},{10,1... | collective-permute-start | bytes 1032200 | tf_op jit(solution)/shard_map/ppermute | solution.py:62
  13.4 8.4 %collective-permute-start.5 = (bf16[42,32,128]{2,1,0:T(8,128)(2,1)S(1)}, bf16[42,32,128]{2,1,0:T(8,128)(2,1)S(1)}, u32[]{:S(2)}, u32[]{:S(2)}) collective-permute-start(bf16[42,32,128]{2,1,0:T(8,128)(2,1)S(1)} %collective-permute-done.4), channel_id=1, source_target_pairs={{0,1},{1,2},{2,3},{3,7},{4,0},{5,4},{6,5},{7,6},{8,9},{9,10},{10,1... | collective-permute-start | bytes 1032200 | tf_op jit(solution)/shard_map/ppermute | solution.py:62
  15.0 6.9 %collective-permute-start.10 = (bf16[128,512]{1,0:T(8,128)(2,1)S(1)}, bf16[128,512]{1,0:T(8,128)(2,1)S(1)}, u32[]{:S(2)}, u32[]{:S(2)}) collective-permute-start(bf16[128,512]{1,0:T(8,128)(2,1)S(1)} %hold.1.refs_0_), channel_id=1, source_target_pairs={{0,16},{4,20},{8,24},{12,28},{16,0},{20,4},{24,8},{28,12},{1,17},{... | collective-permute-start | bytes 393224 | tf_op jit(solution)/shard_map/ppermute | solution.py:54
  16.6 6.4 %collective-permute-start.11 = (bf16[128,512]{1,0:T(8,128)(2,1)S(1)}, bf16[128,512]{1,0:T(8,128)(2,1)S(1)}, u32[]{:S(2)}, u32[]{:S(2)}) collective-permute-start(bf16[128,512]{1,0:T(8,128)(2,1)S(1)} %hold.1.refs_0_), channel_id=1, source_target_pairs={{0,24},{4,28},{8,16},{12,20},{16,8},{20,12},{24,0},{28,4},{1,25},{... | collective-permute-start | bytes 393224 | tf_op jit(solution)/shard_map/ppermute | solution.py:54
  18.0 5.4 %collective-permute-start.9 = (bf16[128,512]{1,0:T(8,128)(2,1)S(1)}, bf16[128,512]{1,0:T(8,128)(2,1)S(1)}, u32[]{:S(2)}, u32[]{:S(2)}) collective-permute-start(bf16[128,512]{1,0:T(8,128)(2,1)S(1)} %hold.1.refs_0_), channel_id=1, source_target_pairs={{0,8},{4,12},{8,0},{12,4},{16,24},{20,28},{24,16},{28,20},{1,9},{5... | collective-permute-start | bytes 393224 | tf_op jit(solution)/shard_map/ppermute | solution.py:54
  18.6 6.9 %collective-permute-start.14 = (bf16[42,32,128]{2,1,0:T(8,128)(2,1)S(1)}, bf16[42,32,128]{2,1,0:T(8,128)(2,1)S(1)}, u32[]{:S(2)}, u32[]{:S(2)}) collective-permute-start(bf16[42,32,128]{2,1,0:T(8,128)(2,1)S(1)} %passed.8), channel_id=1, source_target_pairs={{0,1},{1,2},{2,3},{3,7},{4,0},{5,4},{6,5},{7,6},{8,9},{9,10},{10,1... | collective-permute-start | bytes 1032200 | tf_op jit(solution)/shard_map/ppermute | solution.py:62
  23.5 6.3 %collective-permute-start.12 = (bf16[4,128,512]{2,1,0:T(8,128)(2,1)S(1)}, bf16[4,128,512]{2,1,0:T(8,128)(2,1)S(1)}, u32[]{:S(2)}, u32[]{:S(2)}) collective-permute-start(bf16[4,128,512]{2,1,0:T(8,128)(2,1)S(1)} %stack.1.refs_0_), channel_id=1, source_target_pairs={{0,4},{4,0},{8,12},{12,8},{16,20},{20,16},{24,28},{28,24},{1,5},{5... | collective-permute-start | bytes 1572872 | tf_op jit(solution)/shard_map/ppermute | solution.py:51
  23.6 6.2 %collective-permute-start.6 = (bf16[42,32,128]{2,1,0:T(8,128)(2,1)S(1)}, bf16[42,32,128]{2,1,0:T(8,128)(2,1)S(1)}, u32[]{:S(2)}, u32[]{:S(2)}) collective-permute-start(bf16[42,32,128]{2,1,0:T(8,128)(2,1)S(1)} %passed.6.refs_4_), channel_id=1, source_target_pairs={{0,1},{1,2},{2,3},{3,7},{4,0},{5,4},{6,5},{7,6},{8,9},{9,10},{10,1... | collective-permute-start | bytes 1032200 | tf_op jit(solution)/shard_map/ppermute | solution.py:62
  25.0 4.7 %collective-permute-start.8 = (bf16[2,21,32,128]{3,2,1,0:T(8,128)(2,1)S(1)}, bf16[2,21,32,128]{3,2,1,0:T(8,128)(2,1)S(1)}, u32[]{:S(2)}, u32[]{:S(2)}) collective-permute-start(bf16[2,21,32,128]{3,2,1,0:T(8,128)(2,1)S(1)} %pick.3), channel_id=1, source_target_pairs={{0,4},{4,0},{8,12},{12,8},{16,20},{20,16},{24,28},{28,24},{1,5},{5... | collective-permute-start | bytes 1032200 | tf_op jit(solution)/shard_map/ppermute | solution.py:51
  25.6 7.9 %collective-permute-start.17 = (bf16[42,32,128]{2,1,0:T(8,128)(2,1)S(1)}, bf16[42,32,128]{2,1,0:T(8,128)(2,1)S(1)}, u32[]{:S(2)}, u32[]{:S(2)}) collective-permute-start(bf16[42,32,128]{2,1,0:T(8,128)(2,1)S(1)} %passed.10), channel_id=1, source_target_pairs={{0,1},{1,2},{2,3},{3,7},{4,0},{5,4},{6,5},{7,6},{8,9},{9,10},{10,1... | collective-permute-start | bytes 1032200 | tf_op jit(solution)/shard_map/ppermute | solution.py:62
  29.8 7.3 %collective-permute-start.13 = (bf16[42,32,128]{2,1,0:T(8,128)(2,1)S(1)}, bf16[42,32,128]{2,1,0:T(8,128)(2,1)S(1)}, u32[]{:S(2)}, u32[]{:S(2)}) collective-permute-start(bf16[42,32,128]{2,1,0:T(8,128)(2,1)S(1)} %passed.7), channel_id=1, source_target_pairs={{0,1},{1,2},{2,3},{3,7},{4,0},{5,4},{6,5},{7,6},{8,9},{9,10},{10,1... | collective-permute-start | bytes 1032200 | tf_op jit(solution)/shard_map/ppermute | solution.py:62
  32.4 5.2 %collective-permute-start.15 = (bf16[2,21,32,128]{3,2,1,0:T(8,128)(2,1)S(1)}, bf16[2,21,32,128]{3,2,1,0:T(8,128)(2,1)S(1)}, u32[]{:S(2)}, u32[]{:S(2)}) collective-permute-start(bf16[2,21,32,128]{3,2,1,0:T(8,128)(2,1)S(1)} %pick.4), channel_id=1, source_target_pairs={{0,4},{4,0},{8,12},{12,8},{16,20},{20,16},{24,28},{28,24},{1,5},{5... | collective-permute-start | bytes 1032200 | tf_op jit(solution)/shard_map/ppermute | solution.py:51
  33.5 7.3 %collective-permute-start.19 = (bf16[42,32,128]{2,1,0:T(8,128)(2,1)S(1)}, bf16[42,32,128]{2,1,0:T(8,128)(2,1)S(1)}, u32[]{:S(2)}, u32[]{:S(2)}) collective-permute-start(bf16[42,32,128]{2,1,0:T(8,128)(2,1)S(1)} %passed.11), channel_id=1, source_target_pairs={{0,1},{1,2},{2,3},{3,7},{4,0},{5,4},{6,5},{7,6},{8,9},{9,10},{10,1... | collective-permute-start | bytes 1032200 | tf_op jit(solution)/shard_map/ppermute | solution.py:62
  37.2 4.1 %collective-permute-start.18 = (bf16[2,21,32,128]{3,2,1,0:T(8,128)(2,1)S(1)}, bf16[2,21,32,128]{3,2,1,0:T(8,128)(2,1)S(1)}, u32[]{:S(2)}, u32[]{:S(2)}) collective-permute-start(bf16[2,21,32,128]{3,2,1,0:T(8,128)(2,1)S(1)} %pick.5), channel_id=1, source_target_pairs={{0,4},{4,0},{8,12},{12,8},{16,20},{20,16},{24,28},{28,24},{1,5},{5... | collective-permute-start | bytes 1032200 | tf_op jit(solution)/shard_map/ppermute | solution.py:51
  37.7 7.0 %collective-permute-start.16 = (bf16[42,32,128]{2,1,0:T(8,128)(2,1)S(1)}, bf16[42,32,128]{2,1,0:T(8,128)(2,1)S(1)}, u32[]{:S(2)}, u32[]{:S(2)}) collective-permute-start(bf16[42,32,128]{2,1,0:T(8,128)(2,1)S(1)} %passed.9), channel_id=1, source_target_pairs={{0,1},{1,2},{2,3},{3,7},{4,0},{5,4},{6,5},{7,6},{8,9},{9,10},{10,1... | collective-permute-start | bytes 1032200 | tf_op jit(solution)/shard_map/ppermute | solution.py:62
  40.8 3.9 %collective-permute-start.20 = (bf16[42,32,128]{2,1,0:T(8,128)(2,1)S(1)}, bf16[42,32,128]{2,1,0:T(8,128)(2,1)S(1)}, u32[]{:S(2)}, u32[]{:S(2)}) collective-permute-start(bf16[42,32,128]{2,1,0:T(8,128)(2,1)S(1)} %collective-permute-done.19), channel_id=1, source_target_pairs={{0,4},{4,0},{8,12},{12,8},{16,20},{20,16},{24,28},{28,24},{1,5},{5... | collective-permute-start | bytes 1032200 | tf_op jit(solution)/shard_map/ppermute | solution.py:51

commit v6 on v5

--- a/solution.py
+++ b/solution.py
@@ -11,7 +11,7 @@
 LIMIT = 8
 TWICE = 0
 SPLIT = 1
-ORD = (0, 3, 1, 2)
+ORD = (0, 3, 2, 1)
 COST = 4 * 10**8
 BF16 = jnp.bfloat16
 F32 = jnp.float32
@@ -213,7 +213,7 @@
         out_shape=jax.ShapeDtypeStruct((2, plan.half_tiles, plan.width, LANES), BF16),
         in_specs=[VMEM] * plan.chips + [ANY], out_specs=VMEM,
         scratch_shapes=[pltpu.VMEM((plan.window, LANES), BF16)],
-        compiler_params=PARAMS, name="turn",
+        compiler_params=PARAMS, name="turn", cost_estimate=pl.CostEstimate(flops=2000000000, bytes_accessed=0, transcendentals=0),
     )(*([pieces[q] for q in ORD] if plan.chips == 4 else pieces), part_own).reshape(flat)
     second = plan.swap_cores(first)
 
@@ -231,23 +231,23 @@
     held_kv = pl.pallas_call(
         hold_kernel, out_shape=jax.ShapeDtypeStruct(grad_kv.shape, BF16),
         in_specs=[VMEM, ANY], out_specs=VMEM, compiler_params=PARAMS, name="hold",
-    )(near_kv, part_own)
+    )(near_kv, own[1])
     trail = [own[1], second]
     for slot in range(2, n + 1):
         got = [first.reshape(halves), second.reshape(halves)]
         own += got
-        sent = [passed(first, part_other, slot, [trail[slot - 2]]), passed(second, part_own, slot, theirs[-1:] + ([kvs[1]] if slot == 3 else []))]
+        sent = [passed(first, part_other, slot, []), passed(second, part_own, slot, theirs[-1:] + ([kvs[1]] if slot == 3 else []))]
         first, second = plan.along(sent[0]), plan.along(sent[1])
         if slot == 2:
             kv = pl.pallas_call(
                 functools.partial(stack_kernel, plan.chips), out_shape=jax.ShapeDtypeStruct((plan.chips,) + grad_kv.shape, BF16),
                 in_specs=[VMEM] * plan.chips + [ANY], out_specs=VMEM, compiler_params=PARAMS, name="stack",
-            )(*[plan.to_chip(held_kv, q) if q else held_kv for q in range(plan.chips)], sent[1])
+            )(*[plan.to_chip(held_kv, q) if q else held_kv for q in range(plan.chips)], sent[0])
             kvs = [kv, plan.swap_cores(kv)]
         trail.append(second)
         theirs.append(plan.swap_cores(pl.pallas_call(
             pick_kernel, out_shape=jax.ShapeDtypeStruct(halves, BF16), in_specs=[VMEM] * 2, out_specs=VMEM,
-            compiler_params=PARAMS, name="pick",
+            compiler_params=PARAMS, name="pick", cost_estimate=pl.CostEstimate(flops=1000000000, bytes_accessed=0, transcendentals=0),
         )(*got)))
     rest = plan.swap_cores(first)
 

time: 45.8 us -> 45.6 us (level)
    ppermute x8, waiting for transfers between devices: 7.26 us -> 6.09 us  [along(): return lax.ppermute(x, ('dp', 'tensor'), pairs)]
    ppermute x6, waiting for transfers between devices: 3.55 us -> 4.55 us  [to_chip(): lax.ppermute(x, 'dp', [(d, 2 * self.chip_to(d // 2, q) + d % 2) for d in...]
  transfers between devices with their start and end apart: 21 -> 21, of which waited for: 10 -> 11; matrix products, arithmetic and copies ran while one was open for 0% -> 0% of each run, Pallas kernels for 13% -> 13%
where the time goes in v6:
time: 45.6 us; the launch traced here: 45.5 us
  starting transfers between devices  25.8 us (57%)
  waiting for transfers between devices  10.7 us (23%)
  Pallas kernels  6.9 us (15%)
  local copies, waits for them, and re-layouts  1.25 us (3%)
  between operations  0.81 us (2%)
    ppermute x8, starting transfers between devices, along(): return lax.ppermute(x, ('dp', 'tensor'), pairs)  16.5 us
    ppermute x6, starting transfers between devices, to_chip(): lax.ppermute(x, 'dp', [(d, 2 * self.chip_to(d // 2, q) + d % 2) for d in...  7.6 us
    ppermute x8, waiting for transfers between devices, along(): return lax.ppermute(x, ('dp', 'tensor'), pairs)  6.09 us
    ppermute x6, waiting for transfers between devices, to_chip(): lax.ppermute(x, 'dp', [(d, 2 * self.chip_to(d // 2, q) + d % 2) for d in...  4.55 us
    pallas_call x1, Pallas kernels, body(): pl.pallas_call(functools.partial(partial_kernel, plan), out_shape=[jax.Sh...  3.04 us
    pallas_call x1, Pallas kernels, body(): pl.pallas_call(functools.partial(weight_kernel, plan), out_shape=(jax.Sha...  2.42 us
    ppermute x7, starting transfers between devices, swap_cores(): return lax.ppermute(x, 'dp', [(d, d ^ 1) for d in range(self.n_dp)])  1.72 us
    unnamed x6, local copies, waits for them, and re-layouts  1.25 us
  transfers between devices with their start and end apart: 21, of which 11 were waited for; matrix products, arithmetic and copies ran while one was open for 0% of the time, Pallas kernels for 13%

profile of v6, /device:TPU:0, one launch (start us, length us, event | category | flops | bytes accessed | tf_op | source)
XLA Modules:
  0.0 45.5 jit_solution(12230486758629194701)
XLA Ops:
  0.6 0.5 %collective-permute-start = (bf16[128,512]{1,0:T(8,128)(2,1)}, bf16[128,512]{1,0:T(8,128)(2,1)S(1)}, u32[]{:S(2)}, u32[]{:S(2)}) collective-permute-start(bf16[128,512]{1,0:T(8,128)(2,1)} %x_ref.1), channel_id=1, source_target_pairs={{0,4},{4,0},{8,12},{12,8},{16,20},{20,16},{24,28},{28,24},{1,5},{5... | collective-permute-start | bytes 393224 | tf_op jit(solution)/shard_map/ppermute | solution.py:51
  1.2 1.2 %copy-done.2 = bf16[32,5376]{1,0:T(8,128)(2,1)S(1)} copy-done((bf16[32,5376]{1,0:T(8,128)(2,1)S(1)}, bf16[32,5376]{1,0:T(8,128)(2,1)}, u32[]{:S(2)}) %copy-start.2) | copy-done | bytes 344088
  2.4 3.4 %collective-permute-start.1 = (bf16[32,1408]{1,0:T(8,128)(2,1)S(1)}, bf16[32,1408]{1,0:T(8,128)(2,1)S(1)}, u32[]{:S(2)}, u32[]{:S(2)}) collective-permute-start(bf16[32,1408]{1,0:T(8,128)(2,1)S(1)} %get-tuple-element.12), channel_id=1, source_target_pairs={{0,24},{4,28},{8,16},{12,20},{16,8},{20,12},{24,0},{28,4},{1,25},{... | collective-permute-start | bytes 270344 | tf_op jit(solution)/shard_map/ppermute | solution.py:54
  5.8 0.5 %collective-permute-start.2 = (bf16[32,1408]{1,0:T(8,128)(2,1)S(1)}, bf16[32,1408]{1,0:T(8,128)(2,1)S(1)}, u32[]{:S(2)}, u32[]{:S(2)}) collective-permute-start(bf16[32,1408]{1,0:T(8,128)(2,1)S(1)} %get-tuple-element.13), channel_id=1, source_target_pairs={{0,16},{4,20},{8,24},{12,28},{16,0},{20,4},{24,8},{28,12},{1,17},{... | collective-permute-start | bytes 270344 | tf_op jit(solution)/shard_map/ppermute | solution.py:54
  6.4 0.1 collective-permute-start.3
  6.5 0.0 collective-permute-done.other_ref
  6.5 3.0 %partials.1 = (bf16[4,42,32,128]{3,2,1,0:T(8,128)(2,1)S(1)}, bf16[4,42,32,128]{3,2,1,0:T(8,128)(2,1)S(1)}) custom-call(bf16[128,512]{1,0:T(8,128)(2,1)S(1)} %copy-done.1, bf16[128,512]{1,0:T(8,128)(2,1)S(1)} %collective-permute-done.other_ref, bf16[5376,512]{1,0:T(8,128)(2,1)S(1)} %copy-done), custom_call_target="tpu_custom_call" | custom-call | flops 1409286144 | bytes 8257536 | tf_op jit(solution)/shard_map/partials/pallas_call | solution.py:197
  9.5 0.0 collective-permute-done.1.refs_1_
  9.6 1.7 %collective-permute-done.2.refs_2_ = bf16[32,1408]{1,0:T(8,128)(2,1)S(1)} collective-permute-done((bf16[32,1408]{1,0:T(8,128)(2,1)S(1)}, bf16[32,1408]{1,0:T(8,128)(2,1)S(1)}, u32[]{:S(2)}, u32[]{:S(2)}) %collective-permute-start.2) | collective-permute-done | bytes 90144 | tf_op jit(solution)/shard_map/ppermute | solution.py:54
  11.3 0.3 collective-permute-done.3.refs_3_
  11.5 0.2 turn.1
  11.7 0.1 collective-permute-start.4
  11.8 1.6 %collective-permute-start.7 = (bf16[42,32,128]{2,1,0:T(8,128)(2,1)S(1)}, bf16[42,32,128]{2,1,0:T(8,128)(2,1)S(1)}, u32[]{:S(2)}, u32[]{:S(2)}) collective-permute-start(bf16[42,32,128]{2,1,0:T(8,128)(2,1)S(1)} %bitcast.24), channel_id=1, source_target_pairs={{0,1},{1,2},{2,3},{3,7},{4,0},{5,4},{6,5},{7,6},{8,9},{9,10},{10,1... | collective-permute-start | bytes 1032200 | tf_op jit(solution)/shard_map/ppermute | solution.py:62
  13.4 0.0 collective-permute-done.4
  13.4 1.6 %collective-permute-start.5 = (bf16[42,32,128]{2,1,0:T(8,128)(2,1)S(1)}, bf16[42,32,128]{2,1,0:T(8,128)(2,1)S(1)}, u32[]{:S(2)}, u32[]{:S(2)}) collective-permute-start(bf16[42,32,128]{2,1,0:T(8,128)(2,1)S(1)} %collective-permute-done.4), channel_id=1, source_target_pairs={{0,1},{1,2},{2,3},{3,7},{4,0},{5,4},{6,5},{7,6},{8,9},{9,10},{10,1... | collective-permute-start | bytes 1032200 | tf_op jit(solution)/shard_map/ppermute | solution.py:62
  15.0 1.8 %collective-permute-start.11 = (bf16[128,512]{1,0:T(8,128)(2,1)S(1)}, bf16[128,512]{1,0:T(8,128)(2,1)S(1)}, u32[]{:S(2)}, u32[]{:S(2)}) collective-permute-start(bf16[128,512]{1,0:T(8,128)(2,1)S(1)} %hold.1.refs_0_), channel_id=1, source_target_pairs={{0,24},{4,28},{8,16},{12,20},{16,8},{20,12},{24,0},{28,4},{1,25},{... | collective-permute-start | bytes 393224 | tf_op jit(solution)/shard_map/ppermute | solution.py:54
  16.8 1.3 %collective-permute-start.10 = (bf16[128,512]{1,0:T(8,128)(2,1)S(1)}, bf16[128,512]{1,0:T(8,128)(2,1)S(1)}, u32[]{:S(2)}, u32[]{:S(2)}) collective-permute-start(bf16[128,512]{1,0:T(8,128)(2,1)S(1)} %hold.1.refs_0_), channel_id=1, source_target_pairs={{0,16},{4,20},{8,24},{12,28},{16,0},{20,4},{24,8},{28,12},{1,17},{... | collective-permute-start | bytes 393224 | tf_op jit(solution)/shard_map/ppermute | solution.py:54
  18.1 0.5 %collective-permute-start.9 = (bf16[128,512]{1,0:T(8,128)(2,1)S(1)}, bf16[128,512]{1,0:T(8,128)(2,1)S(1)}, u32[]{:S(2)}, u32[]{:S(2)}) collective-permute-start(bf16[128,512]{1,0:T(8,128)(2,1)S(1)} %hold.1.refs_0_), channel_id=1, source_target_pairs={{0,8},{4,12},{8,0},{12,4},{16,24},{20,28},{24,16},{28,20},{1,9},{5... | collective-permute-start | bytes 393224 | tf_op jit(solution)/shard_map/ppermute | solution.py:54
  18.6 0.0 collective-permute-done.7.received_ref
  18.6 2.1 %collective-permute-start.14 = (bf16[42,32,128]{2,1,0:T(8,128)(2,1)S(1)}, bf16[42,32,128]{2,1,0:T(8,128)(2,1)S(1)}, u32[]{:S(2)}, u32[]{:S(2)}) collective-permute-start(bf16[42,32,128]{2,1,0:T(8,128)(2,1)S(1)} %passed.7.refs_4_), channel_id=1, source_target_pairs={{0,1},{1,2},{2,3},{3,7},{4,0},{5,4},{6,5},{7,6},{8,9},{9,10},{10,1... | collective-permute-start | bytes 1032200 | tf_op jit(solution)/shard_map/ppermute | solution.py:62
  20.7 1.3 %collective-permute-done.11.refs_3_ = bf16[128,512]{1,0:T(8,128)(2,1)S(1)} collective-permute-done((bf16[128,512]{1,0:T(8,128)(2,1)S(1)}, bf16[128,512]{1,0:T(8,128)(2,1)S(1)}, u32[]{:S(2)}, u32[]{:S(2)}) %collective-permute-start.11) | collective-permute-done | bytes 131104 | tf_op jit(solution)/shard_map/ppermute | solution.py:54
  22.0 1.1 %collective-permute-done.10.refs_2_ = bf16[128,512]{1,0:T(8,128)(2,1)S(1)} collective-permute-done((bf16[128,512]{1,0:T(8,128)(2,1)S(1)}, bf16[128,512]{1,0:T(8,128)(2,1)S(1)}, u32[]{:S(2)}, u32[]{:S(2)}) %collective-permute-start.10) | collective-permute-done | bytes 131104 | tf_op jit(solution)/shard_map/ppermute | solution.py:54
  23.1 0.1 collective-permute-done.9.refs_1_
  23.3 0.1 collective-permute-start.12
  23.4 0.0 collective-permute-done.5.received_ref
  23.4 0.1 passed.6
  23.5 1.4 %collective-permute-start.6 = (bf16[42,32,128]{2,1,0:T(8,128)(2,1)S(1)}, bf16[42,32,128]{2,1,0:T(8,128)(2,1)S(1)}, u32[]{:S(2)}, u32[]{:S(2)}) collective-permute-start(bf16[42,32,128]{2,1,0:T(8,128)(2,1)S(1)} %passed.6), channel_id=1, source_target_pairs={{0,1},{1,2},{2,3},{3,7},{4,0},{5,4},{6,5},{7,6},{8,9},{9,10},{10,1... | collective-permute-start | bytes 1032200 | tf_op jit(solution)/shard_map/ppermute | solution.py:62
  24.9 0.1 collective-permute-start.8
  25.0 0.6 %collective-permute-done.14.received_ref = bf16[42,32,128]{2,1,0:T(8,128)(2,1)S(1)} collective-permute-done((bf16[42,32,128]{2,1,0:T(8,128)(2,1)S(1)}, bf16[42,32,128]{2,1,0:T(8,128)(2,1)S(1)}, u32[]{:S(2)}, u32[]{:S(2)}) %collective-permute-start.14) | collective-permute-done | bytes 344096 | tf_op jit(solution)/shard_map/ppermute | solution.py:62
  25.6 2.5 %collective-permute-start.17 = (bf16[42,32,128]{2,1,0:T(8,128)(2,1)S(1)}, bf16[42,32,128]{2,1,0:T(8,128)(2,1)S(1)}, u32[]{:S(2)}, u32[]{:S(2)}) collective-permute-start(bf16[42,32,128]{2,1,0:T(8,128)(2,1)S(1)} %passed.10), channel_id=1, source_target_pairs={{0,1},{1,2},{2,3},{3,7},{4,0},{5,4},{6,5},{7,6},{8,9},{9,10},{10,1... | collective-permute-start | bytes 1032200 | tf_op jit(solution)/shard_map/ppermute | solution.py:62
  28.1 0.0 collective-permute-done.12.refs_1_
  28.1 1.5 %collective-permute-done.6.received_ref = bf16[42,32,128]{2,1,0:T(8,128)(2,1)S(1)} collective-permute-done((bf16[42,32,128]{2,1,0:T(8,128)(2,1)S(1)}, bf16[42,32,128]{2,1,0:T(8,128)(2,1)S(1)}, u32[]{:S(2)}, u32[]{:S(2)}) %collective-permute-start.6) | collective-permute-done | bytes 344096 | tf_op jit(solution)/shard_map/ppermute | solution.py:62
  29.6 0.0 collective-permute-done.8.refs_0_.refs_10_
  29.7 2.6 %collective-permute-start.13 = (bf16[42,32,128]{2,1,0:T(8,128)(2,1)S(1)}, bf16[42,32,128]{2,1,0:T(8,128)(2,1)S(1)}, u32[]{:S(2)}, u32[]{:S(2)}) collective-permute-start(bf16[42,32,128]{2,1,0:T(8,128)(2,1)S(1)} %passed.8), channel_id=1, source_target_pairs={{0,1},{1,2},{2,3},{3,7},{4,0},{5,4},{6,5},{7,6},{8,9},{9,10},{10,1... | collective-permute-start | bytes 1032200 | tf_op jit(solution)/shard_map/ppermute | solution.py:62
  32.2 0.1 collective-permute-start.15
  32.3 1.0 %collective-permute-done.17.received_ref = bf16[42,32,128]{2,1,0:T(8,128)(2,1)S(1)} collective-permute-done((bf16[42,32,128]{2,1,0:T(8,128)(2,1)S(1)}, bf16[42,32,128]{2,1,0:T(8,128)(2,1)S(1)}, u32[]{:S(2)}, u32[]{:S(2)}) %collective-permute-start.17) | collective-permute-done | bytes 344096 | tf_op jit(solution)/shard_map/ppermute | solution.py:62
  33.3 2.5 %collective-permute-start.19 = (bf16[42,32,128]{2,1,0:T(8,128)(2,1)S(1)}, bf16[42,32,128]{2,1,0:T(8,128)(2,1)S(1)}, u32[]{:S(2)}, u32[]{:S(2)}) collective-permute-start(bf16[42,32,128]{2,1,0:T(8,128)(2,1)S(1)} %passed.11), channel_id=1, source_target_pairs={{0,1},{1,2},{2,3},{3,7},{4,0},{5,4},{6,5},{7,6},{8,9},{9,10},{10,1... | collective-permute-start | bytes 1032200 | tf_op jit(solution)/shard_map/ppermute | solution.py:62
  35.9 1.1 %collective-permute-done.13.received_ref = bf16[42,32,128]{2,1,0:T(8,128)(2,1)S(1)} collective-permute-done((bf16[42,32,128]{2,1,0:T(8,128)(2,1)S(1)}, bf16[42,32,128]{2,1,0:T(8,128)(2,1)S(1)}, u32[]{:S(2)}, u32[]{:S(2)}) %collective-permute-start.13) | collective-permute-done | bytes 344096 | tf_op jit(solution)/shard_map/ppermute | solution.py:62
  37.0 0.5 %collective-permute-start.18 = (bf16[2,21,32,128]{3,2,1,0:T(8,128)(2,1)S(1)}, bf16[2,21,32,128]{3,2,1,0:T(8,128)(2,1)S(1)}, u32[]{:S(2)}, u32[]{:S(2)}) collective-permute-start(bf16[2,21,32,128]{3,2,1,0:T(8,128)(2,1)S(1)} %pick.5), channel_id=1, source_target_pairs={{0,4},{4,0},{8,12},{12,8},{16,20},{20,16},{24,28},{28,24},{1,5},{5... | collective-permute-start | bytes 1032200 | tf_op jit(solution)/shard_map/ppermute | solution.py:51
  37.5 0.0 collective-permute-done.15.refs_0_.refs_11_
  37.5 2.2 %collective-permute-start.16 = (bf16[42,32,128]{2,1,0:T(8,128)(2,1)S(1)}, bf16[42,32,128]{2,1,0:T(8,128)(2,1)S(1)}, u32[]{:S(2)}, u32[]{:S(2)}) collective-permute-start(bf16[42,32,128]{2,1,0:T(8,128)(2,1)S(1)} %passed.9), channel_id=1, source_target_pairs={{0,1},{1,2},{2,3},{3,7},{4,0},{5,4},{6,5},{7,6},{8,9},{9,10},{10,1... | collective-permute-start | bytes 1032200 | tf_op jit(solution)/shard_map/ppermute | solution.py:62
  39.7 0.9 %collective-permute-done.19 = bf16[42,32,128]{2,1,0:T(8,128)(2,1)S(1)} collective-permute-done((bf16[42,32,128]{2,1,0:T(8,128)(2,1)S(1)}, bf16[42,32,128]{2,1,0:T(8,128)(2,1)S(1)}, u32[]{:S(2)}, u32[]{:S(2)}) %collective-permute-start.19) | collective-permute-done | bytes 344096 | tf_op jit(solution)/shard_map/ppermute | solution.py:62
  40.7 0.4 collective-permute-start.20
  41.1 2.4 %weights.1 = (f32[672,512]{1,0:T(8,128)}, f32[8,128]{1,0:T(8,128)S(1)}) custom-call(bf16[4,128,512]{2,1,0:T(8,128)(2,1)S(1)} %stack.1.refs_0_, bf16[4,128,512]{2,1,0:T(8,128)(2,1)S(1)} %collective-permute-done.12.refs_1_, bf16[2,21,32,128]{3,2,1,0:T(8,128)(2,1)S(1)} %bitcast.25, bf16[2,21,32,128]{3,2,1,0:T(8,128)(2,1)S(1)} %bitcast.12, ...), custom_call_target="tpu_custom_call" | custom-call | flops 704643072 | bytes 1376256 | tf_op jit(solution)/shard_map/weights/pallas_call | solution.py:254
  43.5 1.0 %collective-permute-done.16.mine_ref = bf16[42,32,128]{2,1,0:T(8,128)(2,1)S(1)} collective-permute-done((bf16[42,32,128]{2,1,0:T(8,128)(2,1)S(1)}, bf16[42,32,128]{2,1,0:T(8,128)(2,1)S(1)}, u32[]{:S(2)}, u32[]{:S(2)}) %collective-permute-start.16) | collective-permute-done | bytes 344096 | tf_op jit(solution)/shard_map/ppermute | solution.py:62
  44.5 0.1 half.1.half_ref
  44.6 0.0 collective-permute-done.20.theirs_ref
  44.6 0.8 %inputs.1 = bf16[32,5376]{1,0:T(8,128)(2,1)} custom-call(f32[42,32,128]{2,1,0:T(8,128)S(1)} %half.1.half_ref, bf16[42,32,128]{2,1,0:T(8,128)(2,1)S(1)} %collective-permute-done.20.theirs_ref), custom_call_target="tpu_custom_call" | custom-call | tf_op jit(solution)/shard_map/inputs/pallas_call | solution.py:270
  (17 shorter events, 0.3 us)
Async XLA Ops:
  0.6 5.9 %copy-start.1 = (bf16[128,512]{1,0:T(8,128)(2,1)S(1)}, bf16[128,512]{1,0:T(8,128)(2,1)}, u32[]{:S(2)}) copy-start(bf16[128,512]{1,0:T(8,128)(2,1)} %x_ref.1) | copy-start | bytes 393220
  0.6 5.9 %copy-start = (bf16[5376,512]{1,0:T(8,128)(2,1)S(1)}, bf16[5376,512]{1,0:T(8,128)(2,1)}, u32[]{:S(2)}) copy-start(bf16[5376,512]{1,0:T(8,128)(2,1)} %refs_0_.1) | copy-start | bytes 16515076
  0.6 5.8 %collective-permute-start = (bf16[128,512]{1,0:T(8,128)(2,1)}, bf16[128,512]{1,0:T(8,128)(2,1)S(1)}, u32[]{:S(2)}, u32[]{:S(2)}) collective-permute-start(bf16[128,512]{1,0:T(8,128)(2,1)} %x_ref.1), channel_id=1, source_target_pairs={{0,4},{4,0},{8,12},{12,8},{16,20},{20,16},{24,28},{28,24},{1,5},{5... | collective-permute-start | bytes 393224 | tf_op jit(solution)/shard_map/ppermute | solution.py:51
  1.2 1.2 %copy-start.2 = (bf16[32,5376]{1,0:T(8,128)(2,1)S(1)}, bf16[32,5376]{1,0:T(8,128)(2,1)}, u32[]{:S(2)}) copy-start(bf16[32,5376]{1,0:T(8,128)(2,1)} %normed_ref.1) | copy-start | bytes 1032196
  2.4 7.1 %collective-permute-start.1 = (bf16[32,1408]{1,0:T(8,128)(2,1)S(1)}, bf16[32,1408]{1,0:T(8,128)(2,1)S(1)}, u32[]{:S(2)}, u32[]{:S(2)}) collective-permute-start(bf16[32,1408]{1,0:T(8,128)(2,1)S(1)} %get-tuple-element.12), channel_id=1, source_target_pairs={{0,24},{4,28},{8,16},{12,20},{16,8},{20,12},{24,0},{28,4},{1,25},{... | collective-permute-start | bytes 270344 | tf_op jit(solution)/shard_map/ppermute | solution.py:54
  5.8 5.4 %collective-permute-start.2 = (bf16[32,1408]{1,0:T(8,128)(2,1)S(1)}, bf16[32,1408]{1,0:T(8,128)(2,1)S(1)}, u32[]{:S(2)}, u32[]{:S(2)}) collective-permute-start(bf16[32,1408]{1,0:T(8,128)(2,1)S(1)} %get-tuple-element.13), channel_id=1, source_target_pairs={{0,16},{4,20},{8,24},{12,28},{16,0},{20,4},{24,8},{28,12},{1,17},{... | collective-permute-start | bytes 270344 | tf_op jit(solution)/shard_map/ppermute | solution.py:54
  6.4 5.2 %collective-permute-start.3 = (bf16[32,1408]{1,0:T(8,128)(2,1)S(1)}, bf16[32,1408]{1,0:T(8,128)(2,1)S(1)}, u32[]{:S(2)}, u32[]{:S(2)}) collective-permute-start(bf16[32,1408]{1,0:T(8,128)(2,1)S(1)} %get-tuple-element.14), channel_id=1, source_target_pairs={{0,8},{4,12},{8,0},{12,4},{16,24},{20,28},{24,16},{28,20},{1,9},{5... | collective-permute-start | bytes 270344 | tf_op jit(solution)/shard_map/ppermute | solution.py:54
  11.7 1.7 %collective-permute-start.4 = (bf16[42,32,128]{2,1,0:T(8,128)(2,1)S(1)}, bf16[42,32,128]{2,1,0:T(8,128)(2,1)S(1)}, u32[]{:S(2)}, u32[]{:S(2)}) collective-permute-start(bf16[42,32,128]{2,1,0:T(8,128)(2,1)S(1)} %bitcast.23), channel_id=1, source_target_pairs={{0,4},{4,0},{8,12},{12,8},{16,20},{20,16},{24,28},{28,24},{1,5},{5... | collective-permute-start | bytes 1032200 | tf_op jit(solution)/shard_map/ppermute | solution.py:51
  11.8 6.8 %collective-permute-start.7 = (bf16[42,32,128]{2,1,0:T(8,128)(2,1)S(1)}, bf16[42,32,128]{2,1,0:T(8,128)(2,1)S(1)}, u32[]{:S(2)}, u32[]{:S(2)}) collective-permute-start(bf16[42,32,128]{2,1,0:T(8,128)(2,1)S(1)} %bitcast.24), channel_id=1, source_target_pairs={{0,1},{1,2},{2,3},{3,7},{4,0},{5,4},{6,5},{7,6},{8,9},{9,10},{10,1... | collective-permute-start | bytes 1032200 | tf_op jit(solution)/shard_map/ppermute | solution.py:62
  13.4 10.0 %collective-permute-start.5 = (bf16[42,32,128]{2,1,0:T(8,128)(2,1)S(1)}, bf16[42,32,128]{2,1,0:T(8,128)(2,1)S(1)}, u32[]{:S(2)}, u32[]{:S(2)}) collective-permute-start(bf16[42,32,128]{2,1,0:T(8,128)(2,1)S(1)} %collective-permute-done.4), channel_id=1, source_target_pairs={{0,1},{1,2},{2,3},{3,7},{4,0},{5,4},{6,5},{7,6},{8,9},{9,10},{10,1... | collective-permute-start | bytes 1032200 | tf_op jit(solution)/shard_map/ppermute | solution.py:62
  15.0 7.0 %collective-permute-start.11 = (bf16[128,512]{1,0:T(8,128)(2,1)S(1)}, bf16[128,512]{1,0:T(8,128)(2,1)S(1)}, u32[]{:S(2)}, u32[]{:S(2)}) collective-permute-start(bf16[128,512]{1,0:T(8,128)(2,1)S(1)} %hold.1.refs_0_), channel_id=1, source_target_pairs={{0,24},{4,28},{8,16},{12,20},{16,8},{20,12},{24,0},{28,4},{1,25},{... | collective-permute-start | bytes 393224 | tf_op jit(solution)/shard_map/ppermute | solution.py:54
  16.8 6.3 %collective-permute-start.10 = (bf16[128,512]{1,0:T(8,128)(2,1)S(1)}, bf16[128,512]{1,0:T(8,128)(2,1)S(1)}, u32[]{:S(2)}, u32[]{:S(2)}) collective-permute-start(bf16[128,512]{1,0:T(8,128)(2,1)S(1)} %hold.1.refs_0_), channel_id=1, source_target_pairs={{0,16},{4,20},{8,24},{12,28},{16,0},{20,4},{24,8},{28,12},{1,17},{... | collective-permute-start | bytes 393224 | tf_op jit(solution)/shard_map/ppermute | solution.py:54
  18.1 5.2 %collective-permute-start.9 = (bf16[128,512]{1,0:T(8,128)(2,1)S(1)}, bf16[128,512]{1,0:T(8,128)(2,1)S(1)}, u32[]{:S(2)}, u32[]{:S(2)}) collective-permute-start(bf16[128,512]{1,0:T(8,128)(2,1)S(1)} %hold.1.refs_0_), channel_id=1, source_target_pairs={{0,8},{4,12},{8,0},{12,4},{16,24},{20,28},{24,16},{28,20},{1,9},{5... | collective-permute-start | bytes 393224 | tf_op jit(solution)/shard_map/ppermute | solution.py:54
  18.6 6.9 %collective-permute-start.14 = (bf16[42,32,128]{2,1,0:T(8,128)(2,1)S(1)}, bf16[42,32,128]{2,1,0:T(8,128)(2,1)S(1)}, u32[]{:S(2)}, u32[]{:S(2)}) collective-permute-start(bf16[42,32,128]{2,1,0:T(8,128)(2,1)S(1)} %passed.7.refs_4_), channel_id=1, source_target_pairs={{0,1},{1,2},{2,3},{3,7},{4,0},{5,4},{6,5},{7,6},{8,9},{9,10},{10,1... | collective-permute-start | bytes 1032200 | tf_op jit(solution)/shard_map/ppermute | solution.py:62
  23.3 4.8 %collective-permute-start.12 = (bf16[4,128,512]{2,1,0:T(8,128)(2,1)S(1)}, bf16[4,128,512]{2,1,0:T(8,128)(2,1)S(1)}, u32[]{:S(2)}, u32[]{:S(2)}) collective-permute-start(bf16[4,128,512]{2,1,0:T(8,128)(2,1)S(1)} %stack.1.refs_0_), channel_id=1, source_target_pairs={{0,4},{4,0},{8,12},{12,8},{16,20},{20,16},{24,28},{28,24},{1,5},{5... | collective-permute-start | bytes 1572872 | tf_op jit(solution)/shard_map/ppermute | solution.py:51
  23.5 6.2 %collective-permute-start.6 = (bf16[42,32,128]{2,1,0:T(8,128)(2,1)S(1)}, bf16[42,32,128]{2,1,0:T(8,128)(2,1)S(1)}, u32[]{:S(2)}, u32[]{:S(2)}) collective-permute-start(bf16[42,32,128]{2,1,0:T(8,128)(2,1)S(1)} %passed.6), channel_id=1, source_target_pairs={{0,1},{1,2},{2,3},{3,7},{4,0},{5,4},{6,5},{7,6},{8,9},{9,10},{10,1... | collective-permute-start | bytes 1032200 | tf_op jit(solution)/shard_map/ppermute | solution.py:62
  24.9 4.7 %collective-permute-start.8 = (bf16[2,21,32,128]{3,2,1,0:T(8,128)(2,1)S(1)}, bf16[2,21,32,128]{3,2,1,0:T(8,128)(2,1)S(1)}, u32[]{:S(2)}, u32[]{:S(2)}) collective-permute-start(bf16[2,21,32,128]{3,2,1,0:T(8,128)(2,1)S(1)} %pick.3), channel_id=1, source_target_pairs={{0,4},{4,0},{8,12},{12,8},{16,20},{20,16},{24,28},{28,24},{1,5},{5... | collective-permute-start | bytes 1032200 | tf_op jit(solution)/shard_map/ppermute | solution.py:51
  25.6 7.7 %collective-permute-start.17 = (bf16[42,32,128]{2,1,0:T(8,128)(2,1)S(1)}, bf16[42,32,128]{2,1,0:T(8,128)(2,1)S(1)}, u32[]{:S(2)}, u32[]{:S(2)}) collective-permute-start(bf16[42,32,128]{2,1,0:T(8,128)(2,1)S(1)} %passed.10), channel_id=1, source_target_pairs={{0,1},{1,2},{2,3},{3,7},{4,0},{5,4},{6,5},{7,6},{8,9},{9,10},{10,1... | collective-permute-start | bytes 1032200 | tf_op jit(solution)/shard_map/ppermute | solution.py:62
  29.7 7.3 %collective-permute-start.13 = (bf16[42,32,128]{2,1,0:T(8,128)(2,1)S(1)}, bf16[42,32,128]{2,1,0:T(8,128)(2,1)S(1)}, u32[]{:S(2)}, u32[]{:S(2)}) collective-permute-start(bf16[42,32,128]{2,1,0:T(8,128)(2,1)S(1)} %passed.8), channel_id=1, source_target_pairs={{0,1},{1,2},{2,3},{3,7},{4,0},{5,4},{6,5},{7,6},{8,9},{9,10},{10,1... | collective-permute-start | bytes 1032200 | tf_op jit(solution)/shard_map/ppermute | solution.py:62
  32.2 5.3 %collective-permute-start.15 = (bf16[2,21,32,128]{3,2,1,0:T(8,128)(2,1)S(1)}, bf16[2,21,32,128]{3,2,1,0:T(8,128)(2,1)S(1)}, u32[]{:S(2)}, u32[]{:S(2)}) collective-permute-start(bf16[2,21,32,128]{3,2,1,0:T(8,128)(2,1)S(1)} %pick.4), channel_id=1, source_target_pairs={{0,4},{4,0},{8,12},{12,8},{16,20},{20,16},{24,28},{28,24},{1,5},{5... | collective-permute-start | bytes 1032200 | tf_op jit(solution)/shard_map/ppermute | solution.py:51
  33.3 7.3 %collective-permute-start.19 = (bf16[42,32,128]{2,1,0:T(8,128)(2,1)S(1)}, bf16[42,32,128]{2,1,0:T(8,128)(2,1)S(1)}, u32[]{:S(2)}, u32[]{:S(2)}) collective-permute-start(bf16[42,32,128]{2,1,0:T(8,128)(2,1)S(1)} %passed.11), channel_id=1, source_target_pairs={{0,1},{1,2},{2,3},{3,7},{4,0},{5,4},{6,5},{7,6},{8,9},{9,10},{10,1... | collective-permute-start | bytes 1032200 | tf_op jit(solution)/shard_map/ppermute | solution.py:62
  37.0 4.1 %collective-permute-start.18 = (bf16[2,21,32,128]{3,2,1,0:T(8,128)(2,1)S(1)}, bf16[2,21,32,128]{3,2,1,0:T(8,128)(2,1)S(1)}, u32[]{:S(2)}, u32[]{:S(2)}) collective-permute-start(bf16[2,21,32,128]{3,2,1,0:T(8,128)(2,1)S(1)} %pick.5), channel_id=1, source_target_pairs={{0,4},{4,0},{8,12},{12,8},{16,20},{20,16},{24,28},{28,24},{1,5},{5... | collective-permute-start | bytes 1032200 | tf_op jit(solution)/shard_map/ppermute | solution.py:51
  37.5 6.9 %collective-permute-start.16 = (bf16[42,32,128]{2,1,0:T(8,128)(2,1)S(1)}, bf16[42,32,128]{2,1,0:T(8,128)(2,1)S(1)}, u32[]{:S(2)}, u32[]{:S(2)}) collective-permute-start(bf16[42,32,128]{2,1,0:T(8,128)(2,1)S(1)} %passed.9), channel_id=1, source_target_pairs={{0,1},{1,2},{2,3},{3,7},{4,0},{5,4},{6,5},{7,6},{8,9},{9,10},{10,1... | collective-permute-start | bytes 1032200 | tf_op jit(solution)/shard_map/ppermute | solution.py:62
  40.7 3.9 %collective-permute-start.20 = (bf16[42,32,128]{2,1,0:T(8,128)(2,1)S(1)}, bf16[42,32,128]{2,1,0:T(8,128)(2,1)S(1)}, u32[]{:S(2)}, u32[]{:S(2)}) collective-permute-start(bf16[42,32,128]{2,1,0:T(8,128)(2,1)S(1)} %collective-permute-done.19), channel_id=1, source_target_pairs={{0,4},{4,0},{8,12},{12,8},{16,20},{20,16},{24,28},{28,24},{1,5},{5... | collective-permute-start | bytes 1032200 | tf_op jit(solution)/shard_map/ppermute | solution.py:51
